TPU v7x, 128 devices: a whole 4x4x4 slice. The times are simulated.
128 devices in a mesh: seq: 32 (over x, y_lo, z), mp: 4 (over y_hi, core).
Axes of the slice: x: 4, y: 4 (y_hi: 2, y_lo: 2; y = y_hi * 2 + y_lo), z: 4, core: 2. Of those that a mesh axis runs over, the one named last changes fastest.
Arguments:
- tokens: bfloat16 [16384, 5376], P('seq', 'mp'), may hold values from -6 to 6
- gain_pre: float32 [5376], replicated, may hold values from 0.1 to 1.9
- w_query: bfloat16 [5376, 2048], P(None, 'mp'), may hold values from -1 to 1
- w_key: bfloat16 [5376, 1024], P(None, 'mp'), may hold values from -1 to 1
- w_value: bfloat16 [5376, 1024], P(None, 'mp'), may hold values from -0.078125 to 0.078125
- w_out: bfloat16 [2048, 5376], P('mp'), may hold values from -0.1875 to 0.1875
- gain_post: float32 [5376], P('mp'), may hold values from 0.1 to 1.9
- prefix_cache: bfloat16 [8, 4096, 2, 1024], P(None, 'seq', None, 'mp'), may hold values from -6 to 6
- template_ids: int32 [4], replicated, may hold values from 0 to 7
- prefix_lengths: int32 [8], replicated, may hold values from 1 to 4096, as said below
- doc_lengths: int32 [4], replicated, may hold values from 1024 to 4096, as said below
Outputs:
- mixed: bfloat16 [16384, 5376], P('seq', 'mp')
Inputs may be any that keep to these rules, and one draw needn't show every extreme that they name: `prefix_lengths`: some template has all 4096 positions. `doc_lengths`: the last document fills all 4096 slots.
All inputs are finite; a program needn't handle non-finite values.
Results may differ from a plain program's by a relative error of at most 0.014.
Values may be sent and summed in bfloat16 or wider, within the bound.
No kernel may reach another device: no remote copies, remote signals or barrier semaphores. Data moves between devices by JAX's collectives and lax.ppermute only.
A program may use at most 128 MiB of HBM per device.

v0:
```python
import jax
import jax.numpy as jnp
from jax import lax
from jax.sharding import PartitionSpec as P

HEAD_DIM = 128
WINDOW = 1024
DOCS = 4


epsilon = 1e-06
query_scalar = 168.0
rope_base = 10000.0


def passed_along(array, axis, by):
    peers = lax.axis_size(axis)
    pairs = [(i, i + by) for i in range(peers) if 0 <= i + by < peers]
    return lax.ppermute(array, axis, pairs)


def rotate(values, places):
    half_dim = values.shape[-1] // 2
    frequency = rope_base ** (-(jnp.arange(half_dim).astype(jnp.float32) * 2.0 / values.shape[-1]))
    angles = places.astype(jnp.float32)[:, None] * frequency[None, :]
    cosine = jnp.cos(angles)[:, None, :]
    sine_part = jnp.sin(angles)[:, None, :]
    first_half = values[..., :half_dim]
    second_half = values[..., half_dim:]
    return jnp.concatenate(
        [
            first_half * cosine - second_half * sine_part,
            second_half * cosine + first_half * sine_part,
        ],
        -1,
    )


def window_mask(
    query_index, query_pos, prefix_len, doc_len, prefix_start, prefix_count, key_index, window_size
):
    prefix_pos = prefix_start + jnp.arange(prefix_count)
    prefix_ok = prefix_pos < prefix_len
    doc_ok = (key_index >= 0) & (key_index < doc_len)
    key_pos = jnp.concatenate([prefix_pos, prefix_len + key_index])
    key_ok = jnp.concatenate([prefix_ok, doc_ok])
    distance = query_pos[:, None] - key_pos[None, :]
    inside = key_ok[None, :] & (distance >= 0) & (distance < window_size)
    own_index = jnp.concatenate([jnp.full((prefix_count,), -1, jnp.int32), key_index])
    self_pair = (own_index[None, :] == query_index[:, None]) & (own_index[None, :] >= 0)
    return inside | self_pair


def attend(queries, keys_all, values_all, allowed):
    scores = jnp.einsum("rkgd,nkd->kgrn", queries, keys_all, preferred_element_type=jnp.float32)
    scores = jnp.where(allowed[None, None], scores, -1e30)
    highest = jnp.max(scores, -1, keepdims=True)
    weights = jnp.exp(scores - highest)
    totals = jnp.sum(weights, -1)
    context = jnp.einsum(
        "kgrn,nkd->rkgd",
        weights.astype(jnp.bfloat16),
        values_all,
        preferred_element_type=jnp.float32,
    )
    return context / jnp.transpose(totals, (2, 0, 1))[..., None]


def shards(
    tokens,
    gain_pre,
    w_query,
    w_key,
    w_value,
    w_out,
    gain_post,
    prefix_cache,
    template_ids,
    prefix_lengths,
    doc_lengths,
):
    whole_rows = lax.all_gather(tokens, "mp", axis=1, tiled=True)
    floated = whole_rows.astype(jnp.float32)
    normed = (
        floated * lax.rsqrt(jnp.mean(floated * floated, 1, keepdims=True) + epsilon) * gain_pre
    ).astype(jnp.bfloat16)
    row_count = tokens.shape[0]
    seq_count = lax.axis_size("seq")
    seq_place = lax.axis_index("seq")
    shards_doc = seq_count // DOCS
    document = seq_place // shards_doc
    local_shard = seq_place % shards_doc
    template = template_ids[document]
    prefix_len = prefix_lengths[template]
    doc_len = doc_lengths[document]
    kv_local = w_key.shape[1] // HEAD_DIM
    heads_local = w_query.shape[1] // HEAD_DIM
    group_size = heads_local // kv_local
    row_range = jnp.arange(row_count)
    query_index = local_shard * row_count + row_range
    query_pos = prefix_len + query_index
    queries = rotate(
        jnp.dot(normed, w_query, preferred_element_type=jnp.float32).reshape(
            row_count, heads_local, HEAD_DIM
        ),
        query_pos,
    )
    queries = (
        (queries * query_scalar ** (-0.5))
        .astype(jnp.bfloat16)
        .reshape(row_count, kv_local, group_size, HEAD_DIM)
    )
    own_keys = rotate(
        jnp.dot(normed, w_key, preferred_element_type=jnp.float32).reshape(
            row_count, kv_local, HEAD_DIM
        ),
        query_pos,
    )
    own_keys = own_keys.astype(jnp.bfloat16).reshape(row_count, kv_local * HEAD_DIM)
    own_values = jnp.dot(normed, w_value, preferred_element_type=jnp.float32).astype(jnp.bfloat16)
    own_pair = jnp.stack([own_keys, own_values], 1)
    reach_count = WINDOW // row_count
    pair_list = []
    index_list = []
    for offset in range(reach_count, 0, -1):
        pair_list.append(passed_along(own_pair, "seq", offset))
        index_list.append((local_shard - offset) * row_count + row_range)
    pair_list.append(own_pair)
    index_list.append(query_index)
    doc_pairs = jnp.concatenate(pair_list, 0)
    key_index = jnp.concatenate(index_list, 0)
    held_rows = prefix_cache.shape[1]
    prefix_total = held_rows * seq_count
    span = min(WINDOW, prefix_total)
    all_lengths = prefix_lengths[template_ids]
    all_starts = jnp.clip(all_lengths - span, 0, prefix_total - span)
    prefix_start = all_starts[document]
    chosen = jnp.take(prefix_cache, template_ids, axis=0)
    gathered = lax.all_gather(chosen, "seq", axis=1, tiled=True)
    prefix_pair = lax.dynamic_slice_in_dim(gathered[document], prefix_start, span, 0)
    prefix_count = prefix_pair.shape[0]
    allowed = window_mask(
        query_index, query_pos, prefix_len, doc_len, prefix_start, prefix_count, key_index, WINDOW
    )
    keys_all = jnp.concatenate([prefix_pair[:, 0], doc_pairs[:, 0]], 0).reshape(
        -1, kv_local, HEAD_DIM
    )
    values_all = jnp.concatenate([prefix_pair[:, 1], doc_pairs[:, 1]], 0).reshape(
        -1, kv_local, HEAD_DIM
    )
    context = attend(queries, keys_all, values_all, allowed)
    context = jnp.where((query_index < doc_len)[:, None, None, None], context, 0.0)
    context = context.astype(jnp.bfloat16).reshape(row_count, heads_local * HEAD_DIM)
    partial_value = jnp.dot(context, w_out, preferred_element_type=jnp.float32)
    feature_count = tokens.shape[1]
    summed = lax.psum(partial_value.astype(jnp.bfloat16), "mp").astype(jnp.float32)
    squares = jnp.mean(summed * summed, 1, keepdims=True)
    own_share = lax.dynamic_slice_in_dim(
        summed, lax.axis_index("mp") * feature_count, feature_count, 1
    )
    result_rows = tokens.astype(jnp.float32) + gain_post * own_share * lax.rsqrt(squares + epsilon)
    return result_rows.astype(jnp.bfloat16)


def solution(mesh):
    placed = (
        P("seq", "mp"),
        P(),
        P(None, "mp"),
        P(None, "mp"),
        P(None, "mp"),
        P("mp", None),
        P("mp"),
        P(None, "seq", None, "mp"),
        P(),
        P(),
        P(),
    )
    return jax.shard_map(
        shards, mesh=mesh, in_specs=placed, out_specs=P("seq", "mp"), check_vma=False
    )
```

profile of v0, /device:TPU:1, one launch (start us, length us, event | category | flops | bytes accessed | tf_op | source)
XLA Modules:
  0.0 455.7 jit_solution(772304646021228458)
XLA Ops:
  6.5 0.0 copy-start
  6.5 0.7 all-gather.5.cloned.1.call-update
  7.3 0.0 all-gather.3.cloned.1.call-start
  7.3 0.7 compare_select_fusion
  8.0 2.8 gather_fusion
  10.9 0.7 compare_and_fusion.1
  11.5 1.3 broadcast_select_fusion
  12.9 0.0 all-gather.3.cloned.1.call-update
  12.9 0.0 all-reduce.2.cloned.1.call-start
  13.0 1.2 dynamic_slice.25
  15.5 1.3 gather_fusion.1
  17.5 1.2 dynamic_slice.26
  18.7 1.3 dynamic_slice.21
  20.0 0.6 dynamic_slice.22
  22.5 0.6 fusion.35
  23.1 1.3 broadcast_compare_fusion.1
  24.4 0.7 fusion.36
  25.1 0.7 iota_add_fusion.3
  25.8 0.6 compare_and_fusion
  26.5 0.6 iota_add_fusion
  27.1 0.7 fusion.33
  27.8 0.5 multiply_cosine_fusion
  28.3 4.6 %fusion.11 = pred[512,2560]{0,1:T(8,128)(4,1)} fusion(s32[512]{0:T(512)S(1)} %get-tuple-element.17, s32[2560]{0:T(1024)S(1)} %pad_add_fusion, s32[512]{0:T(512)S(1)} %get-tuple-element.18, s32[2560]{0:T(1024)S(1)} %pad_add_fusion.1, pred[2560]{0:T(1024)(128)(4,1)S(1)} %broadcast_compare_fusion, pred[2560]{0:T(1024)(128)(4,1)S(1)} %pad_add_fusion.2), kind=kLoop, calls=%fused_computation.20 | loop fusion | flops 10485760 | bytes 1340416 | tf_op jit(solution)/shard_map/or | solution.py:51
  32.9 25.7 %all-gather.5.cloned.1.call-done = bf16[512,5376]{0,1:T(8,128)(2,1)} async-done(((bf16[512,1344]{0,1:T(8,128)(2,1)}), bf16[512,5376]{0,1:T(8,128)(2,1)}) %all-gather.5.cloned.1.call-update) | async-done | bytes 5505040 | tf_op jit(solution)/shard_map/all_gather | solution.py:82
  58.7 3.9 fusion.3
  62.6 0.2 copy-done.4
  62.8 2.1 fusion.45
  65.0 0.1 subtract_convert_fusion
  65.1 0.1 copy.58
  65.2 0.0 copy-start.10
  65.3 6.0 %fusion.20 = bf16[512,1,256]{2,0,1:T(8,128)(2,1)S(1)} fusion(bf16[5376,256]{1,0:T(8,128)(2,1)} %param.15, bf16[512,5376]{0,1:T(8,128)(2,1)} %all-gather.5.cloned.1.call-done, f32[5376]{0:T(1024)} %param.12, f32[512]{0:T(512)S(1)} %add_rsqrt_fusion.1), kind=kOutput, calls=%fused_computation.32 | convolution fusion | flops 1420427264 | bytes 8543232 | tf_op jit(solution)/shard_map/dot_general | solution.py:120
  71.2 0.1 pad_maximum_fusion
  71.3 3.9 collective-permute-start.1
  75.2 4.5 collective-permute-start
  79.7 7.7 %fusion.42 = f32[512,512]{0,1:T(8,128)S(1)} fusion(bf16[5376,512]{1,0:T(8,128)(2,1)} %param.13, bf16[512,5376]{0,1:T(8,128)(2,1)} %all-gather.5.cloned.1.call-done, f32[5376]{0:T(1024)S(1)} %copy-done.10, f32[512]{0:T(512)S(1)} %add_rsqrt_fusion.1), kind=kOutput, calls=%fused_computation.77 | convolution fusion | flops 2829582336 | bytes 12082176 | tf_op jit(solution)/shard_map/dot_general | solution.py:103
  87.4 0.2 multiply_subtract_fusion
  87.6 0.3 copy.50
  87.9 1.3 copy.51
  89.2 4.8 %collective-permute-done.1 = bf16[512,2,256]{2,0,1:T(8,128)(2,1)} collective-permute-done((bf16[512,2,256]{2,0,1:T(8,128)(2,1)S(1)}, bf16[512,2,256]{2,0,1:T(8,128)(2,1)}, u32[]{:S(2)}, u32[]{:S(2)}) %collective-permute-start.1) | collective-permute-done | bytes 524320 | tf_op jit(solution)/shard_map/ppermute | solution.py:19
  94.0 22.5 %collective-permute-done = bf16[512,2,256]{2,0,1:T(8,128)(2,1)} collective-permute-done((bf16[512,2,256]{2,0,1:T(8,128)(2,1)S(1)}, bf16[512,2,256]{2,0,1:T(8,128)(2,1)}, u32[]{:S(2)}, u32[]{:S(2)}) %collective-permute-start) | collective-permute-done | bytes 524320 | tf_op jit(solution)/shard_map/ppermute | solution.py:19
  116.5 1.3 maximum_maximum_fusion
  117.8 1.0 fusion.47
  118.8 2.3 copy.59
  121.1 1.1 concatenate.58
  122.2 1.3 copy.49
  123.5 151.8 %all-gather.3.cloned.1.call-done = bf16[4,4096,2,256]{3,2,1,0:T(2,128)(2,1)} async-done(((bf16[4,128,2,256]{3,2,1,0:T(2,128)(2,1)}), bf16[4,4096,2,256]{3,2,1,0:T(2,128)(2,1)}) %all-gather.3.cloned.1.call-update) | async-done | bytes 16777232 | tf_op jit(solution)/shard_map/all_gather | solution.py:139
  275.4 1.9 constant_dynamic-slice_fusion
  277.3 0.1 copy.61
  277.5 1.0 fusion.48
  278.5 2.0 copy.44
  280.5 2.0 copy.47
  282.6 2.1 copy.48
  284.7 11.7 %fusion = (f32[2,2,512]{2,1,0:T(2,128)S(1)}, f32[2,2560,512,2]{2,1,3,0:T(8,128)}) fusion(pred[512,2560]{0,1:T(8,128)(4,1)S(1)} %copy-done.3, f32[512,2,2,64]{3,0,2,1:T(8,128)} %bitcast.72, f32[512,2,2,64]{3,0,2,1:T(8,128)S(1)} %bitcast.71, bf16[1536,2,128]{2,0,1:T(8,128)(2,1)S(1)} %copy.49, bf16[1024,2,128]{2,0,1:T(8,128)(2,1)} %copy.48), kind=kOutput, calls=%fused_computation.4 | convolution fusion | flops 1356068864 | bytes 24649728 | tf_op jit(solution)/shard_map/rkgd,nkd->kgrn/dot_general | solution.py:55
  296.4 10.2 %fusion.1 = f32[2,2,512]{2,1,0:T(2,128)S(1)} fusion(f32[2,2560,512,2]{2,1,3,0:T(8,128)} %get-tuple-element.16, f32[2,2,512]{2,1,0:T(2,128)S(1)} %get-tuple-element.15, pred[512,2560]{0,1:T(8,128)(4,1)S(1)} %copy-done.3), kind=kLoop, calls=%fused_computation.5 | loop fusion | flops 15726592 | bytes 22298624 | tf_op jit(solution)/shard_map/reduce_sum | solution.py:59
  306.6 0.0 copy-done.6
  306.6 0.0 slice-start.1
  306.7 9.9 %fusion.27 = bf16[512,2,2,128]{0,3,2,1:T(8,128)(2,1)S(1)} fusion(f32[2,2560,512,2]{2,1,3,0:T(8,128)} %get-tuple-element.16, f32[2,2,512]{2,1,0:T(2,128)S(1)} %get-tuple-element.15, pred[512,2560]{0,1:T(8,128)(4,1)S(1)} %copy-done.3, bf16[1536,2,128]{0,2,1:T(8,128)(2,1)S(1)} %bitcast.77, bf16[1024,2,128]{0,2,1:T(8,128)(2,1)S(1)} %bitcast.78, ...), kind=kOutput, calls=%fused_computation.35 | convolution fusion | flops 1361313792 | bytes 24134144 | tf_op jit(solution)/shard_map/kgrn,nkd->rkgd/dot_general | solution.py:60
  316.6 4.9 %convolution_convert_fusion = bf16[512,5376]{0,1:T(8,128)(2,1)} fusion(bf16[512,512]{0,1:T(8,128)(2,1)S(1)} %bitcast.83, bf16[512,5376]{1,0:T(8,128)(2,1)S(1)} %bitcast.82), kind=kOutput, calls=%fused_computation.15 | convolution fusion | flops 2821324800 | bytes 11534336 | tf_op jit(solution)/shard_map/dot_general | solution.py:154
  321.6 0.0 all-reduce.2.cloned.1.call-update
  321.6 120.2 %all-reduce.2.cloned.1.call-done = bf16[512,5376]{0,1:T(8,128)(2,1)} async-done(((bf16[512,5376]{0,1:T(8,128)(2,1)}), bf16[512,5376]{0,1:T(8,128)(2,1)}) %all-reduce.2.cloned.1.call-update) | async-done | bytes 5505040 | tf_op jit(solution)/shard_map/psum | solution.py:156
  441.8 3.9 multiply_reduce_fusion
  445.7 0.3 copy-done.2
  446.0 1.6 convert_element_type.69
  447.6 1.6 add_convert_fusion
  (34 shorter events, 0.1 us)
Async XLA Ops:
  6.5 56.1 %copy-start = (bf16[5376,256]{1,0:T(8,128)(2,1)S(1)}, bf16[5376,256]{1,0:T(8,128)(2,1)}, u32[]{:S(2)}) copy-start(bf16[5376,256]{1,0:T(8,128)(2,1)} %param.14) | copy-start | bytes 8257540
  6.5 52.1 %all-gather.5.cloned.1.call-start = ((), (), s32[]{:S(2)}) async-start(), calls=%async_computation.1 | async-start | bytes 6881280 | tf_op jit(solution)/shard_map/all_gather | solution.py:82
  7.3 268.1 %all-gather.3.cloned.1.call-start = ((), (), s32[]{:S(2)}) async-start(), calls=%async_computation | async-start | bytes 17301504 | tf_op jit(solution)/shard_map/all_gather | solution.py:139
  8.0 54.6 %copy-start.9 = (f32[5376]{0:T(1024)S(1)}, f32[5376]{0:T(1024)}, u32[]{:S(2)}) copy-start(f32[5376]{0:T(1024)} %param.12) | copy-start | bytes 64516
  12.9 428.9 %all-reduce.2.cloned.1.call-start = ((), (), s32[]{:S(2)}) async-start(), calls=%async_computation.2 | async-start | bytes 11010048 | tf_op jit(solution)/shard_map/psum | solution.py:156
  58.7 4.2 copy-start.4
  65.2 14.5 %copy-start.10 = (f32[5376]{0:T(1024)S(1)}, f32[5376]{0:T(1024)}, u32[]{:S(2)}) copy-start(f32[5376]{0:T(1024)} %param.12) | copy-start | bytes 64516
  71.3 22.7 %collective-permute-start.1 = (bf16[512,2,256]{2,0,1:T(8,128)(2,1)S(1)}, bf16[512,2,256]{2,0,1:T(8,128)(2,1)}, u32[]{:S(2)}, u32[]{:S(2)}) collective-permute-start(bf16[512,2,256]{2,0,1:T(8,128)(2,1)S(1)} %pad_maximum_fusion), channel_id=1, source_target_pairs={{0,4},{4,8},{8,12},{12,16},{16,20},{20,24},{24,28},{28,32},{32,36}... | collective-permute-start | bytes 1572872 | tf_op jit(solution)/shard_map/ppermute | solution.py:19
  75.2 41.3 %collective-permute-start = (bf16[512,2,256]{2,0,1:T(8,128)(2,1)S(1)}, bf16[512,2,256]{2,0,1:T(8,128)(2,1)}, u32[]{:S(2)}, u32[]{:S(2)}) collective-permute-start(bf16[512,2,256]{2,0,1:T(8,128)(2,1)S(1)} %pad_maximum_fusion), channel_id=1, source_target_pairs={{0,8},{4,12},{8,16},{12,20},{16,24},{20,28},{24,32},{28,36},{32,40... | collective-permute-start | bytes 1572872 | tf_op jit(solution)/shard_map/ppermute | solution.py:19
  122.2 162.5 %copy-start.3 = (pred[512,2560]{0,1:T(8,128)(4,1)S(1)}, pred[512,2560]{0,1:T(8,128)(4,1)}, u32[]{:S(2)}) copy-start(pred[512,2560]{0,1:T(8,128)(4,1)} %fusion.11) | copy-start | bytes 3932164
  296.4 10.2 %copy-start.6 = (bf16[1536,1,256]{0,2,1:T(8,128)(2,1)S(1)}, bf16[1536,1,256]{0,2,1:T(8,128)(2,1)}, u32[]{:S(2)}) copy-start(bf16[1536,1,256]{0,2,1:T(8,128)(2,1)} %copy.59) | copy-start | bytes 2359300
  296.4 10.2 %copy-start.7 = (bf16[1024,1,256]{0,2,1:T(8,128)(2,1)S(1)}, bf16[1024,1,256]{0,2,1:T(8,128)(2,1)}, u32[]{:S(2)}) copy-start(bf16[1024,1,256]{0,2,1:T(8,128)(2,1)} %copy.44) | copy-start | bytes 1572868
  296.4 20.2 %slice-start = ((s8[5505024]{0:T(1024)(128)(4,1)}), s8[4194304]{0:T(1024)(128)(4,1)S(1)}, s32[]{:S(2)}) async-start(s8[5505024]{0:T(1024)(128)(4,1)} %bitcast.81), calls=%async_computation.3 | async-start | bytes 8388608
  306.6 10.0 %slice-start.1 = ((s8[5505024]{0:T(1024)(128)(4,1)}), s8[1310720]{0:T(1024)(128)(4,1)S(1)}, s32[]{:S(2)}) async-start(s8[5505024]{0:T(1024)(128)(4,1)} %bitcast.81), calls=%async_computation.4 | async-start | bytes 2621440
  441.8 4.2 copy-start.2
  446.0 1.6 copy-start.5
  446.0 1.6 copy-start.8
  446.0 3.2 copy-start.1
Sparse Core Ops, SparseCore 0:
  9.0 49.5 all-gather.4
  60.3 215.0 all-gather.2
  321.7 119.9 all-reduce.1
where the time goes:
time: 456 us
  waiting for transfers between devices  326 us (71%)
  matrix products  42.4 us (9%)
  other arithmetic  35.9 us (8%)
  local copies, waits for them, and re-layouts  25.8 us (6%)
  between operations  17.3 us (4%)
  starting transfers between devices  8.49 us (2%)
    all_gather x1, waiting for transfers between devices, shards(): gathered = lax.all_gather(chosen, 'seq', axis=1, tiled=True)  152 us
    psum x1, waiting for transfers between devices, shards(): lax.psum(partial_value.astype(jnp.bfloat16), 'mp').astype(jnp.float32)  120 us
    ppermute x2, waiting for transfers between devices, passed_along(): return lax.ppermute(array, axis, pairs)  27.3 us
    all_gather x1, waiting for transfers between devices, shards(): whole_rows = lax.all_gather(tokens, 'mp', axis=1, tiled=True)  25.7 us
    dot_general x1, matrix products, attend(): jnp.einsum('rkgd,nkd->kgrn', queries, keys_all, preferred_element_type=jn...  11.7 us
    reduce_sum x1, other arithmetic, attend(): totals = jnp.sum(weights, -1)  10.2 us
    dot_general x1, matrix products, attend(): jnp.einsum('kgrn,nkd->rkgd', weights.astype(jnp.bfloat16), values_all, pr...  9.95 us
  transfers between devices with their start and end apart: 5, of which 5 were waited for; matrix products, arithmetic and copies ran while one was open for 11% of the time, Pallas kernels for 0%

commit v1 on v0

v1 whole, which is shorter than its diff:
```python
import functools

import jax
import jax.numpy as jnp
from jax import lax
from jax.experimental import pallas as pl
from jax.experimental.pallas import tpu as pltpu
from jax.sharding import PartitionSpec as P

HEAD_DIM = 128
WINDOW = 1024
DOCS = 4
MP = 4
ROWS = 512
FEATURES = 1344
HEADS_LOCAL = 4
KV_WIDTH = 256
PAIR = 2 * KV_WIDTH
DOC_SHARDS = 8
HELD = 128
VMEM_LIMIT = 56 * 1024 * 1024

epsilon = 1e-06
query_scalar = 168.0
rope_base = 10000.0
F32 = jnp.float32
BF16 = jnp.bfloat16


def cost(flops, moved, exps=0):
    return pl.CostEstimate(flops=flops, bytes_accessed=moved, transcendentals=exps)


def params():
    return pltpu.CompilerParams(vmem_limit_bytes=VMEM_LIMIT)


def across_mp(array, flip):
    return lax.ppermute(array, "mp", [(i, i ^ flip) for i in range(MP)])


def seq_place(x, y_lo, z):
    return x * 8 + y_lo * 4 + z


def along_x(array, by):
    pairs = [
        (seq_place(x, y, z), seq_place((x + by) % 4, y, z))
        for x in range(4)
        for y in range(2)
        for z in range(4)
    ]
    return lax.ppermute(array, "seq", pairs)


def to_lower_twin(array):
    pairs = [(seq_place(x, 1, z), seq_place(x, 0, z)) for x in range(4) for z in range(4)]
    return lax.ppermute(array, "seq", pairs)


def within_doc(array, by):
    pairs = [
        (d * DOC_SHARDS + i, d * DOC_SHARDS + i + by)
        for d in range(DOCS)
        for i in range(DOC_SHARDS - by)
    ]
    return lax.ppermute(array, "seq", pairs)


def project_kernel(first, last, order, *refs):
    step = pl.program_id(0)
    x_refs, refs = refs[:2], refs[2:]
    gain, wq, wk, wv = refs[:4]
    refs = refs[4:]
    if first:
        acc, squares = refs
    else:
        acc_in, squares_in, cosine, sine, q_ref, kv_ref, acc, squares = refs

    @pl.when(step == 0)
    def _():
        if first:
            acc[...] = jnp.zeros_like(acc)
            squares[...] = jnp.zeros_like(squares)
        else:
            acc[...] = acc_in[...]
            squares[...] = squares_in[...]

    for number in range(2):

        @pl.when(step == number)
        def _(x_ref=x_refs[number]):
            x = x_ref[...].astype(F32)
            squares[...] += jnp.broadcast_to(jnp.sum(x * x, 1, keepdims=True), squares.shape)
            scaled = (x * gain[0]).astype(BF16)
            acc[:, :512] += jnp.dot(scaled, wq[...], preferred_element_type=F32)
            acc[:, 512:768] += jnp.dot(scaled, wk[...], preferred_element_type=F32)
            acc[:, 768:] += jnp.dot(scaled, wv[...], preferred_element_type=F32)

    if last:

        @pl.when(step == 1)
        def _():
            scale = lax.rsqrt(squares[...] * (1.0 / (MP * FEATURES)) + epsilon)
            cos_all = cosine[...]
            sin_all = sine[...]
            for head in range(6):
                cols = slice(head * HEAD_DIM, (head + 1) * HEAD_DIM)
                part = acc[:, cols] * scale
                turned = part * cos_all + pltpu.roll(part, 64, 1) * sin_all
                if head < HEADS_LOCAL:
                    q_ref[:, cols] = (turned * query_scalar ** (-0.5)).astype(BF16)
                else:
                    at = (head - HEADS_LOCAL) * HEAD_DIM
                    kv_ref[:, at : at + HEAD_DIM] = turned.astype(BF16)
            kv_ref[:, KV_WIDTH : KV_WIDTH + HEAD_DIM] = (acc[:, 768:896] * scale).astype(BF16)
            kv_ref[:, KV_WIDTH + HEAD_DIM :] = (acc[:, 896:] * scale).astype(BF16)


def project(order, xs, gain, wq, wk, wv, carried=None, tables=None):
    first = carried is None
    full = lambda shape: pl.BlockSpec(shape, lambda i, order: (0,) * len(shape))
    chunk = lambda width: pl.BlockSpec((FEATURES, width), lambda i, order: (order[i], 0))
    in_specs = [full((ROWS, FEATURES))] * 2 + [
        pl.BlockSpec((1, 1, FEATURES), lambda i, order: (order[i], 0, 0)),
        chunk(512),
        chunk(256),
        chunk(256),
    ]
    args = [*xs, gain, wq, wk, wv]
    acc_shape = [(ROWS, 1024), (ROWS, HEAD_DIM)]
    if first:
        out_shape = [jax.ShapeDtypeStruct(s, F32) for s in acc_shape]
        out_specs = [full(s) for s in acc_shape]
        scratch = []
    else:
        in_specs += [full(s) for s in acc_shape] + [full((ROWS, HEAD_DIM))] * 2
        args += [*carried, *tables]
        out_shape = [jax.ShapeDtypeStruct((ROWS, 512), BF16)] * 2
        out_specs = [full((ROWS, 512))] * 2
        scratch = [pltpu.VMEM(s, F32) for s in acc_shape]
    return pl.pallas_call(
        functools.partial(project_kernel, first, not first),
        grid_spec=pltpu.PrefetchScalarGridSpec(
            num_scalar_prefetch=1,
            grid=(2,),
            in_specs=in_specs,
            out_specs=out_specs,
            scratch_shapes=scratch,
        ),
        out_shape=out_shape,
        compiler_params=params(),
        cost_estimate=cost(2 * ROWS * 2 * FEATURES * 1024, 11_000_000),
    )(order, *args)


def attention_kernel(info, q_ref, own, one_back, two_back, prefix, out, held, sems):
    local = info[0]
    length = info[1]
    real = info[2]

    def copies(branch):
        got = []
        if branch == 0:
            got += [(prefix.at[z, 0], held.at[pl.ds(z * HELD, HELD)]) for z in range(4)]
            got += [(prefix.at[z, 1], held.at[pl.ds(ROWS + z * HELD, HELD)]) for z in range(4)]
        elif branch == 1:
            got += [(prefix.at[z, 1], held.at[pl.ds(z * HELD, HELD)]) for z in range(4)]
            got += [(one_back, held.at[pl.ds(ROWS, ROWS)])]
        else:
            got += [(two_back, held.at[pl.ds(0, ROWS)]), (one_back, held.at[pl.ds(ROWS, ROWS)])]
        return [pltpu.make_async_copy(a, b, sems.at[i]) for i, (a, b) in enumerate(got)]

    for branch in range(3):

        @pl.when(local == branch if branch < 2 else local >= 2)
        def _(branch=branch):
            started = copies(branch)
            for one in started:
                one.start()
            for one in started:
                one.wait()

    column = lax.broadcasted_iota(jnp.int32, (1, ROWS), 1)
    shift_two = jnp.where(local < 2, length, 0)
    limit_two = jnp.where(local < 2, WINDOW - ROWS * local - length, 0)
    shift_one = jnp.where(local < 1, length, 0)
    limit_one = jnp.where(local < 1, ROWS - length, 0)
    place_two = (column - shift_two) & (ROWS - 1)
    place_one = (column - shift_one) & (ROWS - 1)
    one_ok = place_one >= limit_one
    dims = (((1,), (1,)), ((), ()))
    block = 128
    for chunk in range(ROWS // block):
        row = chunk * block + lax.broadcasted_iota(jnp.int32, (block, 1), 0)
        two_ok = place_two > jnp.maximum(row, limit_two - 1)
        reach = (chunk + 1) * block
        own_ok = column[:, :reach] <= row
        row_real = row + local * ROWS < real
        for head in range(HEADS_LOCAL):
            k_cols = slice((head // 2) * HEAD_DIM, (head // 2 + 1) * HEAD_DIM)
            v_cols = slice(KV_WIDTH + k_cols.start, KV_WIDTH + k_cols.stop)
            cols = slice(head * HEAD_DIM, (head + 1) * HEAD_DIM)
            q = q_ref[chunk * block : reach, cols]
            s_two = lax.dot_general(q, held[:ROWS, k_cols], dims, preferred_element_type=F32)
            s_one = lax.dot_general(q, held[ROWS:, k_cols], dims, preferred_element_type=F32)
            s_own = lax.dot_general(q, own[:reach, k_cols], dims, preferred_element_type=F32)
            s_two = jnp.where(two_ok, s_two, -1e30)
            s_one = jnp.where(one_ok, s_one, -1e30)
            s_own = jnp.where(own_ok, s_own, -1e30)
            top = jnp.maximum(
                jnp.maximum(
                    jnp.max(s_two, 1, keepdims=True), jnp.max(s_one, 1, keepdims=True)
                ),
                jnp.max(s_own, 1, keepdims=True),
            )
            w_two = jnp.exp(s_two - top)
            w_one = jnp.exp(s_one - top)
            w_own = jnp.exp(s_own - top)
            total = (
                jnp.sum(w_two, 1, keepdims=True)
                + jnp.sum(w_one, 1, keepdims=True)
                + jnp.sum(w_own, 1, keepdims=True)
            )
            got = (
                jnp.dot(w_two.astype(BF16), held[:ROWS, v_cols], preferred_element_type=F32)
                + jnp.dot(w_one.astype(BF16), held[ROWS:, v_cols], preferred_element_type=F32)
                + jnp.dot(w_own.astype(BF16), own[:reach, v_cols], preferred_element_type=F32)
            )
            got = jnp.where(row_real, got / total, 0.0)
            out[chunk * block : reach, cols] = got.astype(BF16)


def attention(info, q, own, one_back, two_back, prefix):
    full = pl.BlockSpec((ROWS, 512), lambda i, info: (0, 0))
    anywhere = pl.BlockSpec(memory_space=pl.ANY)
    return pl.pallas_call(
        attention_kernel,
        grid_spec=pltpu.PrefetchScalarGridSpec(
            num_scalar_prefetch=1,
            grid=(1,),
            in_specs=[full, full, anywhere, anywhere, anywhere],
            out_specs=full,
            scratch_shapes=[
                pltpu.VMEM((2 * ROWS, PAIR), BF16),
                pltpu.SemaphoreType.DMA((8,)),
            ],
        ),
        out_shape=jax.ShapeDtypeStruct((ROWS, 512), BF16),
        compiler_params=params(),
        cost_estimate=cost(4 * HEADS_LOCAL * ROWS * 1536 * 128, 3_000_000, HEADS_LOCAL * ROWS * 1536),
    )(info, q, own, one_back, two_back, prefix)


def output_kernel(c0, c1, c2, c3, w0, w1, w2, w3, attended, squares):
    total = jnp.dot(c0[...], w0[...], preferred_element_type=F32)
    total += jnp.dot(c1[...], w1[...], preferred_element_type=F32)
    total += jnp.dot(c2[...], w2[...], preferred_element_type=F32)
    total += jnp.dot(c3[...], w3[...], preferred_element_type=F32)
    attended[...] = total
    squares[...] = jnp.broadcast_to(jnp.sum(total * total, 1, keepdims=True), squares.shape)


def output(contexts, weights):
    block = 256
    rows = pl.BlockSpec((block, 512), lambda i: (i, 0))
    full = pl.BlockSpec((512, FEATURES), lambda i: (0, 0))
    return pl.pallas_call(
        output_kernel,
        grid=(ROWS // block,),
        in_specs=[rows] * 4 + [full] * 4,
        out_specs=[
            pl.BlockSpec((block, FEATURES), lambda i: (i, 0)),
            pl.BlockSpec((block, HEAD_DIM), lambda i: (i, 0)),
        ],
        out_shape=[
            jax.ShapeDtypeStruct((ROWS, FEATURES), F32),
            jax.ShapeDtypeStruct((ROWS, HEAD_DIM), F32),
        ],
        compiler_params=params(),
        cost_estimate=cost(2 * ROWS * 2048 * FEATURES, 11_000_000),
    )(*contexts, *weights)


def rope_tables(places):
    lane = jnp.arange(HEAD_DIM)
    frequency = rope_base ** (-((lane % 64).astype(F32) * 2.0 / HEAD_DIM))
    angles = places.astype(F32)[:, None] * frequency[None, :]
    return jnp.cos(angles), jnp.where(lane[None, :] < 64, -jnp.sin(angles), jnp.sin(angles))


def shards(
    tokens,
    gain_pre,
    w_query,
    w_key,
    w_value,
    w_out,
    gain_post,
    prefix_cache,
    template_ids,
    prefix_lengths,
    doc_lengths,
):
    member = lax.axis_index("mp")
    place = lax.axis_index("seq")
    doc = place // DOC_SHARDS
    local = place % DOC_SHARDS
    z_place = place % 4
    length = prefix_lengths[template_ids[doc]]

    far = across_mp(tokens, 2)
    near = across_mp(tokens, 1)

    piece = (place // DOC_SHARDS) * 4 + z_place

    def block_for(flip, start, count):
        return lax.dynamic_slice(w_out, (start, (member ^ flip) * FEATURES), (count, FEATURES))

    w_own = block_for(0, 0, 512)
    w_near = across_mp(block_for(1, 0, 512), 1)
    w_pieces = jnp.stack(
        [across_mp(block_for(2, piece * 32, 32), 2), across_mp(block_for(3, piece * 32, 32), 3)]
    )
    groups = [[seq_place(x, y, z) for x in range(4) for z in range(4)] for y in range(2)]
    w_far = lax.all_gather(w_pieces, "seq", axis=1, tiled=True, axis_index_groups=groups)

    held_at = place * HELD + jnp.arange(HELD)

    def masked_rows(document):
        template = template_ids[document]
        reach = prefix_lengths[template]
        rows = lax.dynamic_index_in_dim(prefix_cache, template, 0, False).reshape(HELD, PAIR)
        wanted = (held_at < reach) & (held_at >= reach - WINDOW)
        return jnp.where(wanted[:, None], rows, jnp.zeros((), BF16))

    mine = masked_rows(doc)
    for by in range(1, 4):
        mine = mine + along_x(masked_rows((doc + by) % DOCS), by)
    twin = to_lower_twin(mine)
    mine_late = ((z_place * HELD + jnp.arange(HELD) - length) & (WINDOW - 1)) >= ROWS
    ordered = jnp.stack(
        [
            jnp.where(mine_late[:, None], twin, mine),
            jnp.where(mine_late[:, None], mine, twin),
        ]
    )
    z_groups = [[seq_place(x, y, z) for z in range(4)] for x in range(4) for y in range(2)]
    prefix = lax.all_gather(ordered[None], "seq", axis=0, tiled=True, axis_index_groups=z_groups)

    tables = rope_tables(length + local * ROWS + jnp.arange(ROWS))
    gain = gain_pre.reshape(MP, 1, FEATURES)
    order = jnp.stack([member, member ^ 1, member ^ 2, member ^ 3]).astype(jnp.int32)
    carried = project(order[:2], [tokens, near], gain, w_query, w_key, w_value)
    far_near = across_mp(far, 1)
    queries, own = project(
        order[2:], [far, far_near], gain, w_query, w_key, w_value, carried, tables
    )
    one_back = within_doc(own, 1)
    two_back = within_doc(own, 2)
    info = jnp.stack([local, length, doc_lengths[doc]]).astype(jnp.int32)
    context = attention(info, queries, own, one_back, two_back, prefix)
    c_far = across_mp(context, 2)
    c_near = across_mp(context, 1)
    c_far_near = across_mp(c_far, 1)
    attended, squares = output(
        [context, c_near, c_far, c_far_near], [w_own, w_near, w_far[0], w_far[1]]
    )
    own_squares = squares[:, 0]
    total = own_squares
    for flip in (1, 2, 3):
        total = total + across_mp(own_squares, flip)
    scale = lax.rsqrt(total * (1.0 / (MP * FEATURES)) + epsilon)
    return (tokens.astype(F32) + gain_post * attended * scale[:, None]).astype(BF16)


def solution(mesh):
    placed = (
        P("seq", "mp"),
        P(),
        P(None, "mp"),
        P(None, "mp"),
        P(None, "mp"),
        P("mp", None),
        P("mp"),
        P(None, "seq", None, "mp"),
        P(),
        P(),
        P(),
    )
    return jax.shard_map(
        shards, mesh=mesh, in_specs=placed, out_specs=P("seq", "mp"), check_vma=False
    )
```

time: 456 us -> 217 us (0.48)
  the two profiles are of different devices: /device:TPU:1 before, /device:TPU:43 now
where the time goes in v1:
time: 217 us; the launch traced here: 216 us
  waiting for transfers between devices  79.6 us (37%)
  Pallas kernels  37.1 us (17%)
  starting transfers between devices  31.8 us (15%)
  local copies, waits for them, and re-layouts  30.7 us (14%)
  between operations  24.4 us (11%)
  other arithmetic  12.3 us (6%)
    ppermute x12, waiting for transfers between devices, across_mp(): return lax.ppermute(array, 'mp', [(i, i ^ flip) for i in range(MP)])  44.8 us
    ppermute x2, waiting for transfers between devices, within_doc(): return lax.ppermute(array, 'seq', pairs)  29.6 us
    ppermute x12, starting transfers between devices, across_mp(): return lax.ppermute(array, 'mp', [(i, i ^ flip) for i in range(MP)])  19.3 us
    pallas_call x2, Pallas kernels, project(): pl.pallas_call(functools.partial(project_kernel, first, not first), grid_...  18.5 us
    pallas_call x1, Pallas kernels, attention(): pl.pallas_call(attention_kernel, grid_spec=pltpu.PrefetchScalarGridSpec(n...  10.5 us
    ppermute x4, local copies, waits for them, and re-layouts, across_mp(): return lax.ppermute(array, 'mp', [(i, i ^ flip) for i in range(MP)])  9.15 us
    pallas_call x1, Pallas kernels, output(): pl.pallas_call(output_kernel, grid=(ROWS // block,), in_specs=[rows] * 4...  8.04 us
    ppermute x2, starting transfers between devices, within_doc(): return lax.ppermute(array, 'seq', pairs)  6.15 us
  transfers between devices with their start and end apart: 20, of which 9 were waited for; matrix products, arithmetic and copies ran while one was open for 14% of the time, Pallas kernels for 13%

profile of v1, /device:TPU:43, one launch (start us, length us, event | category | flops | bytes accessed | tf_op | source)
XLA Modules:
  0.0 215.8 jit_solution(14086748658502840984)
XLA Ops:
  6.5 1.5 fusion.6
  15.5 1.5 constant_dynamic-slice_fusion.5
  17.0 0.7 fusion.5
  18.3 0.7 compare_and_fusion.2
  19.0 1.3 collective-permute-start.5
  21.0 0.7 compare_and_fusion.1
  21.7 0.1 broadcast_select_fusion.1
  21.8 0.9 collective-permute-start.6
  23.3 0.6 compare_and_fusion
  24.1 1.9 collective-permute-start.7
  26.6 0.6 compare_and_fusion.3
  27.3 3.8 %collective-permute-done.7 = bf16[128,512]{1,0:T(8,128)(2,1)S(1)} collective-permute-done((bf16[128,512]{1,0:T(8,128)(2,1)S(1)}, bf16[128,512]{1,0:T(8,128)(2,1)S(1)}, u32[]{:S(2)}, u32[]{:S(2)}) %collective-permute-start.7) | collective-permute-done | bytes 131104 | tf_op jit(solution)/shard_map/ppermute | solution.py:53
  31.1 0.1 add_add_fusion
  31.2 2.2 %collective-permute-start.8 = (bf16[128,512]{1,0:T(8,128)(2,1)S(1)}, bf16[128,512]{1,0:T(8,128)(2,1)S(1)}, u32[]{:S(2)}, u32[]{:S(2)}) collective-permute-start(bf16[128,512]{1,0:T(8,128)(2,1)S(1)} %add_add_fusion), channel_id=1, source_target_pairs={{16,0},{20,4},{24,8},{28,12},{48,32},{52,36},{56,40},{60,44},{80,6... | collective-permute-start | bytes 393224 | tf_op jit(solution)/shard_map/ppermute | solution.py:58
  33.4 0.6 and_compare_fusion
  34.1 1.3 collective-permute-done.8
  35.4 0.1 select_bitcast_fusion.1
  35.4 0.7 pad_maximum_fusion
  36.3 1.1 fusion.4
  37.4 2.4 %collective-permute-start.13 = (bf16[32,1344]{1,0:T(8,128)(2,1)S(1)}, bf16[32,1344]{1,0:T(8,128)(2,1)S(1)}, u32[]{:S(2)}, u32[]{:S(2)}) collective-permute-start(bf16[32,1344]{1,0:T(8,128)(2,1)S(1)} %get-tuple-element.17), channel_id=1, source_target_pairs={{0,2},{1,3},{2,0},{3,1},{4,6},{5,7},{6,4},{7,5},{8,10},{9,11},{10,... | collective-permute-start | bytes 258056 | tf_op jit(solution)/shard_map/ppermute | solution.py:39
  39.8 2.7 %collective-permute-start.14 = (bf16[32,1344]{1,0:T(8,128)(2,1)S(1)}, bf16[32,1344]{1,0:T(8,128)(2,1)S(1)}, u32[]{:S(2)}, u32[]{:S(2)}) collective-permute-start(bf16[32,1344]{1,0:T(8,128)(2,1)S(1)} %get-tuple-element.18), channel_id=1, source_target_pairs={{0,3},{1,2},{2,1},{3,0},{4,7},{5,6},{6,5},{7,4},{8,11},{9,10},{10,... | collective-permute-start | bytes 258056 | tf_op jit(solution)/shard_map/ppermute | solution.py:39
  42.5 3.2 %collective-permute-done.14 = bf16[32,1344]{1,0:T(8,128)(2,1)S(1)} collective-permute-done((bf16[32,1344]{1,0:T(8,128)(2,1)S(1)}, bf16[32,1344]{1,0:T(8,128)(2,1)S(1)}, u32[]{:S(2)}, u32[]{:S(2)}) %collective-permute-start.14) | collective-permute-done | bytes 86048 | tf_op jit(solution)/shard_map/ppermute | solution.py:39
  45.6 0.7 pad_maximum_fusion.1
  46.4 3.4 %collective-permute-start = (bf16[512,1344]{0,1:T(8,128)(2,1)S(1)}, bf16[512,1344]{0,1:T(8,128)(2,1)}, u32[]{:S(2)}, u32[]{:S(2)}) collective-permute-start(bf16[512,1344]{0,1:T(8,128)(2,1)S(1)} %copy-done.1), channel_id=1, source_target_pairs={{0,2},{1,3},{2,0},{3,1},{4,6},{5,7},{6,4},{7,5},{8,10},{9,11},{10,... | collective-permute-start | bytes 4128776 | tf_op jit(solution)/shard_map/ppermute | solution.py:39
  49.7 0.3 collective-permute-start.2
  50.0 29.3 %collective-permute-done = bf16[512,1344]{0,1:T(8,128)(2,1)} collective-permute-done((bf16[512,1344]{0,1:T(8,128)(2,1)S(1)}, bf16[512,1344]{0,1:T(8,128)(2,1)}, u32[]{:S(2)}, u32[]{:S(2)}) %collective-permute-start) | collective-permute-done | bytes 1376288 | tf_op jit(solution)/shard_map/ppermute | solution.py:39
  79.3 1.6 collective-permute-start.1
  81.0 4.5 %constant_dynamic-slice_fusion = (bf16[512,1344]{1,0:T(8,128)(2,1)S(1)}, bf16[512,1344]{1,0:T(8,128)(2,1)}) fusion(bf16[512,5376]{1,0:T(8,128)(2,1)} %param.16, s32[]{:T(128)S(6)} %select_n.133, s32[]{:T(128)S(6)} %select_n.132), kind=kLoop, calls=%fused_computation.22 | loop fusion | bytes 5505032 | tf_op jit(solution)/shard_map/dynamic_slice | solution.py:318
  85.4 1.5 copy.30
  86.9 1.5 copy.22.refs_0_
  89.1 0.7 reshape.73.refs_2_
  89.8 0.6 pad_add_fusion.2.order
  90.4 0.7 pad_add_fusion.1.order
  91.0 1.8 negate_select_fusion
  92.9 2.6 %copy.25.refs_0_ = bf16[512,1344]{1,0:T(8,128)(2,1)} copy(bf16[512,1344]{0,1:T(8,128)(2,1)} %collective-permute-done) | data formatting | bytes 2752512 | tf_op jit(solution)/shard_map/ppermute | solution.py:39
  95.4 2.5 %copy.24.refs_1_ = bf16[512,1344]{1,0:T(8,128)(2,1)} copy(bf16[512,1344]{0,1:T(8,128)(2,1)} %collective-permute-done.2) | data formatting | bytes 2752512 | tf_op jit(solution)/shard_map/ppermute | solution.py:39
  98.0 9.0 %shard_map.109 = (f32[512,1024]{1,0:T(8,128)}, f32[512,128]{1,0:T(8,128)}) custom-call(s32[2]{0:T(128)} %pad_add_fusion.2.order, bf16[512,1344]{1,0:T(8,128)(2,1)} %copy.22.refs_0_, bf16[512,1344]{1,0:T(8,128)(2,1)} %copy.24.refs_1_, f32[4,1,1344]{2,1,0:T(1,128)} %reshape.73.refs_2_, bf16[5376,512]{1,0:T(8,128)(2,1)} %refs_3_.3, bf16[5376,256]{1,0:T(8,128)(2,1)} %refs_4_.3, ...), custom_call_target="tpu_custom_call" | custom-call | flops 2818572288 | bytes 11000000 | tf_op jit(solution)/shard_map/pallas_call | solution.py:142
  106.9 2.5 %copy.26.refs_1_ = bf16[512,1344]{1,0:T(8,128)(2,1)} copy(bf16[512,1344]{0,1:T(8,128)(2,1)} %collective-permute-done.1) | data formatting | bytes 2752512 | tf_op jit(solution)/shard_map/ppermute | solution.py:39
  109.5 9.5 %shard_map.110 = (bf16[512,512]{1,0:T(8,128)(2,1)}, bf16[512,512]{1,0:T(8,128)(2,1)}) custom-call(s32[2]{0:T(128)} %pad_add_fusion.1.order, bf16[512,1344]{1,0:T(8,128)(2,1)} %copy.25.refs_0_, bf16[512,1344]{1,0:T(8,128)(2,1)} %copy.26.refs_1_, f32[4,1,1344]{2,1,0:T(1,128)} %reshape.73.refs_2_, bf16[5376,512]{1,0:T(8,128)(2,1)} %refs_3_.3, ...), custom_call_target="tpu_custom_call" | custom-call | flops 2818572288 | bytes 11000000 | tf_op jit(solution)/shard_map/pallas_call | solution.py:142
  119.0 3.5 %collective-permute-start.3 = (bf16[512,512]{1,0:T(8,128)(2,1)}, bf16[512,512]{1,0:T(8,128)(2,1)S(1)}, u32[]{:S(2)}, u32[]{:S(2)}) collective-permute-start(bf16[512,512]{1,0:T(8,128)(2,1)} %get-tuple-element.14.own), channel_id=1, source_target_pairs={{0,4},{4,8},{8,12},{12,16},{16,20},{20,24},{24,28},{32,36},{36,40}... | collective-permute-start | bytes 1572872 | tf_op jit(solution)/shard_map/ppermute | solution.py:67
  122.6 2.6 %collective-permute-start.4 = (bf16[512,512]{1,0:T(8,128)(2,1)}, bf16[512,512]{1,0:T(8,128)(2,1)S(1)}, u32[]{:S(2)}, u32[]{:S(2)}) collective-permute-start(bf16[512,512]{1,0:T(8,128)(2,1)} %get-tuple-element.14.own), channel_id=1, source_target_pairs={{0,8},{4,12},{8,16},{12,20},{16,24},{20,28},{32,40},{36,44},{40,48... | collective-permute-start | bytes 1572872 | tf_op jit(solution)/shard_map/ppermute | solution.py:67
  125.2 0.6 dynamic_slice.56
  125.8 1.8 pad_add_fusion.info
  127.6 6.5 %collective-permute-done.3.one_back = bf16[512,512]{1,0:T(8,128)(2,1)S(1)} collective-permute-done((bf16[512,512]{1,0:T(8,128)(2,1)}, bf16[512,512]{1,0:T(8,128)(2,1)S(1)}, u32[]{:S(2)}, u32[]{:S(2)}) %collective-permute-start.3) | collective-permute-done | bytes 524320 | tf_op jit(solution)/shard_map/ppermute | solution.py:67
  134.1 23.1 %collective-permute-done.4.two_back = bf16[512,512]{1,0:T(8,128)(2,1)S(1)} collective-permute-done((bf16[512,512]{1,0:T(8,128)(2,1)}, bf16[512,512]{1,0:T(8,128)(2,1)S(1)}, u32[]{:S(2)}, u32[]{:S(2)}) %collective-permute-start.4) | collective-permute-done | bytes 524320 | tf_op jit(solution)/shard_map/ppermute | solution.py:67
  157.2 0.8 copy-done.10
  158.0 10.5 %shard_map.111.c0 = bf16[512,512]{1,0:T(8,128)(2,1)} custom-call(s32[3]{0:T(128)} %pad_add_fusion.info, bf16[512,512]{1,0:T(8,128)(2,1)} %get-tuple-element.13.q_ref, bf16[512,512]{1,0:T(8,128)(2,1)} %get-tuple-element.14.own, bf16[512,512]{1,0:T(8,128)(2,1)} %copy-done.8, bf16[512,512]{1,0:T(8,128)(2,1)} %copy-done.10, bf16[4,2,128,512]{3,2,1,0:T(8,128)(2,1)} %bitcast.46), custom_call_target="tpu_custom_call" | custom-call | flops 1610612736 | bytes 3000000 | tf_op jit(solution)/shard_map/pallas_call | solution.py:237
  168.6 1.8 collective-permute-start.10
  170.3 1.5 copy.28.w1
  171.9 1.6 collective-permute-start.9
  173.4 9.3 %collective-permute-done.10.c2 = bf16[512,512]{1,0:T(8,128)(2,1)S(1)} collective-permute-done((bf16[512,512]{1,0:T(8,128)(2,1)}, bf16[512,512]{1,0:T(8,128)(2,1)S(1)}, u32[]{:S(2)}, u32[]{:S(2)}) %collective-permute-start.10) | collective-permute-done | bytes 524320 | tf_op jit(solution)/shard_map/ppermute | solution.py:39
  182.8 1.9 collective-permute-start.11
  184.7 3.7 %slice_bitcast_fusion = (bf16[512,1344]{1,0:T(8,128)(2,1)}, bf16[512,1344]{1,0:T(8,128)(2,1)}) fusion(bf16[2,512,1344]{2,1,0:T(8,128)(2,1)} %all-gather.4.cloned.1.call-done), kind=kLoop, calls=%fused_computation.1 | loop fusion | bytes 5505024 | tf_op jit(solution)/shard_map/squeeze | solution.py:367
  188.4 0.8 copy-done.7
  189.2 0.2 copy-done.9
  189.3 8.0 %shard_map.112 = (f32[512,1344]{1,0:T(8,128)}, f32[512,128]{1,0:T(8,128)}) custom-call(bf16[512,512]{1,0:T(8,128)(2,1)} %shard_map.111.c0, bf16[512,512]{1,0:T(8,128)(2,1)} %copy-done.7, bf16[512,512]{1,0:T(8,128)(2,1)} %copy-done.6, bf16[512,512]{1,0:T(8,128)(2,1)} %copy-done.9, bf16[512,1344]{1,0:T(8,128)(2,1)} %get-tuple-element.20.w0, ...), custom_call_target="tpu_custom_call" | custom-call | flops 2818572288 | bytes 11000000 | tf_op jit(solution)/shard_map/pallas_call | solution.py:268
  197.4 1.1 slice_reduce_fusion
  198.5 0.3 collective-permute-start.15
  198.7 1.7 collective-permute-start.16
  200.5 1.7 collective-permute-start.17
  202.2 0.5 collective-permute-done.16
  202.7 2.5 %collective-permute-done.17 = f32[512]{0:T(512)S(1)} collective-permute-done((f32[512]{0:T(512)S(1)}, f32[512]{0:T(512)S(1)}, u32[]{:S(2)}, u32[]{:S(2)}) %collective-permute-start.17) | collective-permute-done | bytes 2080 | tf_op jit(solution)/shard_map/ppermute | solution.py:39
  205.2 2.3 %add_convert_fusion = bf16[512,1344]{1,0:T(8,128)(2,1)S(1)} fusion(f32[512,1344]{1,0:T(8,128)} %get-tuple-element.15, bf16[512,1344]{1,0:T(8,128)(2,1)S(1)} %copy-done, f32[512]{0:T(512)S(1)} %add_rsqrt_fusion, f32[1344]{0:T(1024)S(1)} %copy-done.3), kind=kLoop, calls=%fused_computation | loop fusion | flops 3440640 | bytes 5512448 | tf_op jit(solution)/shard_map/convert_element_type | solution.py:374
  207.5 1.5 copy.29
  (47 shorter events, 0.4 us)
Async XLA Ops:
  6.5 10.4 %copy-start.4 = (s32[8]{0:T(128)S(1)}, s32[8]{0:T(128)}, u32[]{:S(2)}) copy-start(s32[8]{0:T(128)} %param.20) | copy-start | bytes 100
  6.5 121.1 %all-gather.6.cloned.1.call-start = ((), (), s32[]{:S(2)}) async-start(), calls=%async_computation.1 | async-start | bytes 1310720 | tf_op jit(solution)/shard_map/all_gather | solution.py:349
  19.0 8.3 %collective-permute-start.5 = (bf16[128,512]{1,0:T(8,128)(2,1)S(1)}, bf16[128,512]{1,0:T(8,128)(2,1)S(1)}, u32[]{:S(2)}, u32[]{:S(2)}) collective-permute-start(bf16[128,512]{1,0:T(8,128)(2,1)S(1)} %broadcast_select_fusion.2), channel_id=1, source_target_pairs={{0,32},{4,36},{8,40},{12,44},{16,48},{20,52},{24,56},{28,60},{32,6... | collective-permute-start | bytes 393224 | tf_op jit(solution)/shard_map/ppermute | solution.py:53
  21.8 5.5 %collective-permute-start.6 = (bf16[128,512]{1,0:T(8,128)(2,1)S(1)}, bf16[128,512]{1,0:T(8,128)(2,1)S(1)}, u32[]{:S(2)}, u32[]{:S(2)}) collective-permute-start(bf16[128,512]{1,0:T(8,128)(2,1)S(1)} %broadcast_select_fusion.1), channel_id=1, source_target_pairs={{0,64},{4,68},{8,72},{12,76},{16,80},{20,84},{24,88},{28,92},{32,9... | collective-permute-start | bytes 393224 | tf_op jit(solution)/shard_map/ppermute | solution.py:53
  24.1 7.0 %collective-permute-start.7 = (bf16[128,512]{1,0:T(8,128)(2,1)S(1)}, bf16[128,512]{1,0:T(8,128)(2,1)S(1)}, u32[]{:S(2)}, u32[]{:S(2)}) collective-permute-start(bf16[128,512]{1,0:T(8,128)(2,1)S(1)} %broadcast_select_fusion), channel_id=1, source_target_pairs={{0,96},{4,100},{8,104},{12,108},{16,112},{20,116},{24,120},{28,124... | collective-permute-start | bytes 393224 | tf_op jit(solution)/shard_map/ppermute | solution.py:53
  31.1 15.2 %copy-start.1 = (bf16[512,1344]{0,1:T(8,128)(2,1)S(1)}, bf16[512,1344]{0,1:T(8,128)(2,1)}, u32[]{:S(2)}) copy-start(bf16[512,1344]{0,1:T(8,128)(2,1)} %param.11) | copy-start | bytes 4128772
  31.2 4.1 %collective-permute-start.8 = (bf16[128,512]{1,0:T(8,128)(2,1)S(1)}, bf16[128,512]{1,0:T(8,128)(2,1)S(1)}, u32[]{:S(2)}, u32[]{:S(2)}) collective-permute-start(bf16[128,512]{1,0:T(8,128)(2,1)S(1)} %add_add_fusion), channel_id=1, source_target_pairs={{16,0},{20,4},{24,8},{28,12},{48,32},{52,36},{56,40},{60,44},{80,6... | collective-permute-start | bytes 393224 | tf_op jit(solution)/shard_map/ppermute | solution.py:58
  36.2 148.5 %all-gather.4.cloned.1.call-start = ((), (), s32[]{:S(2)}) async-start(), calls=%async_computation | async-start | bytes 3063808 | tf_op jit(solution)/shard_map/all_gather | solution.py:326
  37.4 5.1 %collective-permute-start.13 = (bf16[32,1344]{1,0:T(8,128)(2,1)S(1)}, bf16[32,1344]{1,0:T(8,128)(2,1)S(1)}, u32[]{:S(2)}, u32[]{:S(2)}) collective-permute-start(bf16[32,1344]{1,0:T(8,128)(2,1)S(1)} %get-tuple-element.17), channel_id=1, source_target_pairs={{0,2},{1,3},{2,0},{3,1},{4,6},{5,7},{6,4},{7,5},{8,10},{9,11},{10,... | collective-permute-start | bytes 258056 | tf_op jit(solution)/shard_map/ppermute | solution.py:39
  39.8 5.8 %collective-permute-start.14 = (bf16[32,1344]{1,0:T(8,128)(2,1)S(1)}, bf16[32,1344]{1,0:T(8,128)(2,1)S(1)}, u32[]{:S(2)}, u32[]{:S(2)}) collective-permute-start(bf16[32,1344]{1,0:T(8,128)(2,1)S(1)} %get-tuple-element.18), channel_id=1, source_target_pairs={{0,3},{1,2},{2,1},{3,0},{4,7},{5,6},{6,5},{7,4},{8,11},{9,10},{10,... | collective-permute-start | bytes 258056 | tf_op jit(solution)/shard_map/ppermute | solution.py:39
  46.4 33.0 %collective-permute-start = (bf16[512,1344]{0,1:T(8,128)(2,1)S(1)}, bf16[512,1344]{0,1:T(8,128)(2,1)}, u32[]{:S(2)}, u32[]{:S(2)}) collective-permute-start(bf16[512,1344]{0,1:T(8,128)(2,1)S(1)} %copy-done.1), channel_id=1, source_target_pairs={{0,2},{1,3},{2,0},{3,1},{4,6},{5,7},{6,4},{7,5},{8,10},{9,11},{10,... | collective-permute-start | bytes 4128776 | tf_op jit(solution)/shard_map/ppermute | solution.py:39
  49.7 45.7 %collective-permute-start.2 = (bf16[512,1344]{0,1:T(8,128)(2,1)S(1)}, bf16[512,1344]{0,1:T(8,128)(2,1)}, u32[]{:S(2)}, u32[]{:S(2)}) collective-permute-start(bf16[512,1344]{0,1:T(8,128)(2,1)S(1)} %copy-done.1), channel_id=1, source_target_pairs={{0,1},{1,0},{2,3},{3,2},{4,5},{5,4},{6,7},{7,6},{8,9},{9,8},{10,11... | collective-permute-start | bytes 4128776 | tf_op jit(solution)/shard_map/ppermute | solution.py:39
  79.3 27.6 %collective-permute-start.1 = (bf16[512,1344]{0,1:T(8,128)(2,1)}, bf16[512,1344]{0,1:T(8,128)(2,1)}, u32[]{:S(2)}, u32[]{:S(2)}) collective-permute-start(bf16[512,1344]{0,1:T(8,128)(2,1)} %collective-permute-done), channel_id=1, source_target_pairs={{0,1},{1,0},{2,3},{3,2},{4,5},{5,4},{6,7},{7,6},{8,9},{9,8},{10,11... | collective-permute-start | bytes 4128776 | tf_op jit(solution)/shard_map/ppermute | solution.py:39
  86.9 2.2 %copy-start.2 = (f32[5376]{0:T(1024)S(1)}, f32[5376]{0:T(1024)}, u32[]{:S(2)}) copy-start(f32[5376]{0:T(1024)} %param.12) | copy-start | bytes 64516
  86.9 83.4 %collective-permute-start.12 = (bf16[512,1344]{0,1:T(8,128)(2,1)}, bf16[512,1344]{0,1:T(8,128)(2,1)S(1)}, u32[]{:S(2)}, u32[]{:S(2)}) collective-permute-start(bf16[512,1344]{0,1:T(8,128)(2,1)} %copy.30), channel_id=1, source_target_pairs={{0,1},{1,0},{2,3},{3,2},{4,5},{5,4},{6,7},{7,6},{8,9},{9,8},{10,11... | collective-permute-start | bytes 4128776 | tf_op jit(solution)/shard_map/ppermute | solution.py:39
  109.5 15.7 %copy-start.11 = (s32[4]{0:T(128)S(1)}, s32[4]{0:T(128)}, u32[]{:S(2)}) copy-start(s32[4]{0:T(128)} %param.21) | copy-start | bytes 52
  119.0 15.1 %collective-permute-start.3 = (bf16[512,512]{1,0:T(8,128)(2,1)}, bf16[512,512]{1,0:T(8,128)(2,1)S(1)}, u32[]{:S(2)}, u32[]{:S(2)}) collective-permute-start(bf16[512,512]{1,0:T(8,128)(2,1)} %get-tuple-element.14.own), channel_id=1, source_target_pairs={{0,4},{4,8},{8,12},{12,16},{16,20},{20,24},{24,28},{32,36},{36,40}... | collective-permute-start | bytes 1572872 | tf_op jit(solution)/shard_map/ppermute | solution.py:67
  122.6 34.7 %collective-permute-start.4 = (bf16[512,512]{1,0:T(8,128)(2,1)}, bf16[512,512]{1,0:T(8,128)(2,1)S(1)}, u32[]{:S(2)}, u32[]{:S(2)}) collective-permute-start(bf16[512,512]{1,0:T(8,128)(2,1)} %get-tuple-element.14.own), channel_id=1, source_target_pairs={{0,8},{4,12},{8,16},{12,20},{16,24},{20,28},{32,40},{36,44},{40,48... | collective-permute-start | bytes 1572872 | tf_op jit(solution)/shard_map/ppermute | solution.py:67
  134.1 23.1 %copy-start.8 = (bf16[512,512]{1,0:T(8,128)(2,1)}, bf16[512,512]{1,0:T(8,128)(2,1)S(1)}, u32[]{:S(2)}) copy-start(bf16[512,512]{1,0:T(8,128)(2,1)S(1)} %collective-permute-done.3.one_back) | copy-start | bytes 1572868
  157.2 0.8 copy-start.10
  168.6 3.3 %copy-start.5 = (bf16[512,512]{1,0:T(8,128)(2,1)S(1)}, bf16[512,512]{1,0:T(8,128)(2,1)}, u32[]{:S(2)}) copy-start(bf16[512,512]{1,0:T(8,128)(2,1)} %shard_map.111.c0) | copy-start | bytes 1572868
  168.6 14.2 %collective-permute-start.10 = (bf16[512,512]{1,0:T(8,128)(2,1)}, bf16[512,512]{1,0:T(8,128)(2,1)S(1)}, u32[]{:S(2)}, u32[]{:S(2)}) collective-permute-start(bf16[512,512]{1,0:T(8,128)(2,1)} %shard_map.111.c0), channel_id=1, source_target_pairs={{0,2},{1,3},{2,0},{3,1},{4,6},{5,7},{6,4},{7,5},{8,10},{9,11},{10,... | collective-permute-start | bytes 1572872 | tf_op jit(solution)/shard_map/ppermute | solution.py:39
  171.9 16.5 %collective-permute-start.9 = (bf16[512,512]{1,0:T(8,128)(2,1)S(1)}, bf16[512,512]{1,0:T(8,128)(2,1)S(1)}, u32[]{:S(2)}, u32[]{:S(2)}) collective-permute-start(bf16[512,512]{1,0:T(8,128)(2,1)S(1)} %copy-done.5), channel_id=1, source_target_pairs={{0,1},{1,0},{2,3},{3,2},{4,5},{5,4},{6,7},{7,6},{8,9},{9,8},{10,11... | collective-permute-start | bytes 1572872 | tf_op jit(solution)/shard_map/ppermute | solution.py:39
  182.8 5.6 %copy-start.6 = (bf16[512,512]{1,0:T(8,128)(2,1)}, bf16[512,512]{1,0:T(8,128)(2,1)S(1)}, u32[]{:S(2)}) copy-start(bf16[512,512]{1,0:T(8,128)(2,1)S(1)} %collective-permute-done.10.c2) | copy-start | bytes 1572868
  182.8 5.6 %collective-permute-start.11 = (bf16[512,512]{1,0:T(8,128)(2,1)S(1)}, bf16[512,512]{1,0:T(8,128)(2,1)S(1)}, u32[]{:S(2)}, u32[]{:S(2)}) collective-permute-start(bf16[512,512]{1,0:T(8,128)(2,1)S(1)} %collective-permute-done.10.c2), channel_id=1, source_target_pairs={{0,1},{1,0},{2,3},{3,2},{4,5},{5,4},{6,7},{7,6},{8,9},{9,8},{10,11... | collective-permute-start | bytes 1572872 | tf_op jit(solution)/shard_map/ppermute | solution.py:39
  188.4 0.8 copy-start.7
  188.4 0.9 copy-start.9
  189.3 15.8 %copy-start = (bf16[512,1344]{1,0:T(8,128)(2,1)S(1)}, bf16[512,1344]{1,0:T(8,128)(2,1)}, u32[]{:S(2)}) copy-start(bf16[512,1344]{1,0:T(8,128)(2,1)} %copy.22.refs_0_) | copy-start | bytes 4128772
  189.3 15.8 %copy-start.3 = (f32[1344]{0:T(1024)S(1)}, f32[1344]{0:T(1024)}, u32[]{:S(2)}) copy-start(f32[1344]{0:T(1024)} %param.17) | copy-start | bytes 16132
  198.5 3.7 %collective-permute-start.15 = (f32[512]{0:T(512)S(1)}, f32[512]{0:T(512)S(1)}, u32[]{:S(2)}, u32[]{:S(2)}) collective-permute-start(f32[512]{0:T(512)S(1)} %slice_reduce_fusion), channel_id=1, source_target_pairs={{0,1},{1,0},{2,3},{3,2},{4,5},{5,4},{6,7},{7,6},{8,9},{9,8},{10,11... | collective-permute-start | bytes 6152 | tf_op jit(solution)/shard_map/ppermute | solution.py:39
  198.7 3.9 %collective-permute-start.16 = (f32[512]{0:T(512)S(1)}, f32[512]{0:T(512)S(1)}, u32[]{:S(2)}, u32[]{:S(2)}) collective-permute-start(f32[512]{0:T(512)S(1)} %slice_reduce_fusion), channel_id=1, source_target_pairs={{0,2},{1,3},{2,0},{3,1},{4,6},{5,7},{6,4},{7,5},{8,10},{9,11},{10,... | collective-permute-start | bytes 6152 | tf_op jit(solution)/shard_map/ppermute | solution.py:39
  200.5 4.7 %collective-permute-start.17 = (f32[512]{0:T(512)S(1)}, f32[512]{0:T(512)S(1)}, u32[]{:S(2)}, u32[]{:S(2)}) collective-permute-start(f32[512]{0:T(512)S(1)} %slice_reduce_fusion), channel_id=1, source_target_pairs={{0,3},{1,2},{2,1},{3,0},{4,7},{5,6},{6,5},{7,4},{8,11},{9,10},{10,... | collective-permute-start | bytes 6152 | tf_op jit(solution)/shard_map/ppermute | solution.py:39
Sparse Core Ops, SparseCore 0:
  36.3 26.4 all-gather.5
  65.0 47.3 all-gather.3

commit v2 on v1

v2 whole, which is shorter than its diff:
```python
import functools

import jax
import jax.numpy as jnp
from jax import lax
from jax.experimental import pallas as pl
from jax.experimental.pallas import tpu as pltpu
from jax.sharding import PartitionSpec as P

HEAD_DIM = 128
WINDOW = 1024
DOCS = 4
MP = 4
ROWS = 512
HALF = 256
FEATURES = 1344
STEP = 672
HEADS_LOCAL = 4
KV_WIDTH = 256
PAIR = 2 * KV_WIDTH
DOC_SHARDS = 8
HELD = 128
STRIP = FEATURES // 4
VMEM_LIMIT = 60 * 1024 * 1024

epsilon = 1e-06
query_scalar = 168.0
rope_base = 10000.0
F32 = jnp.float32
BF16 = jnp.bfloat16


def cost(flops, moved, exps=0):
    return pl.CostEstimate(flops=flops, bytes_accessed=moved, transcendentals=exps)


def params():
    return pltpu.CompilerParams(vmem_limit_bytes=VMEM_LIMIT)


def across_mp(array, flip):
    return lax.ppermute(array, "mp", [(i, i ^ flip) for i in range(MP)])


def seq_place(x, y_lo, z):
    return x * 8 + y_lo * 4 + z


def along_x(array, by):
    pairs = [
        (seq_place(x, y, z), seq_place((x + by) % 4, y, z))
        for x in range(4)
        for y in range(2)
        for z in range(4)
    ]
    return lax.ppermute(array, "seq", pairs)


def along_z(array, by):
    pairs = [
        (seq_place(x, y, z), seq_place(x, y, (z + by) % 4))
        for x in range(4)
        for y in range(2)
        for z in range(4)
    ]
    return lax.ppermute(array, "seq", pairs)


def to_twin(array):
    pairs = [(i, i ^ 4) for i in range(DOCS * DOC_SHARDS)]
    return lax.ppermute(array, "seq", pairs)


def z_flip(array, flip):
    return lax.ppermute(array, "seq", [(i, i ^ flip) for i in range(DOCS * DOC_SHARDS)])


def within_doc(array, by):
    pairs = [
        (d * DOC_SHARDS + i, d * DOC_SHARDS + (i + by) % DOC_SHARDS)
        for d in range(DOCS)
        for i in range(DOC_SHARDS)
    ]
    return lax.ppermute(array, "seq", pairs)


def after(array, *others):
    return lax.optimization_barrier((array, *others))[0]


TN = (((0,), (0,)), ((), ()))
NT = (((1,), (1,)), ((), ()))


IN_HBM = pl.BlockSpec(memory_space=pltpu.HBM)


def add_projection(x_ref, gain, wq, wk, wv, acc, squares):
    x = jnp.transpose(x_ref[...]).astype(F32)
    squares[...] += jnp.broadcast_to(jnp.sum(x * x, 1, keepdims=True), squares.shape)
    scaled = (x * gain[0]).astype(BF16)
    acc[:, :512] += jnp.dot(scaled, wq[...], preferred_element_type=F32)
    acc[:, 512:768] += jnp.dot(scaled, wk[...], preferred_element_type=F32)
    acc[:, 768:] += jnp.dot(scaled, wv[...], preferred_element_type=F32)


def first_kernel(order, x0, x1, gain, wq, wk, wv, acc, squares):
    step = pl.program_id(0)

    @pl.when(step == 0)
    def _():
        acc[...] = jnp.zeros_like(acc)
        squares[...] = jnp.zeros_like(squares)

    for number, x_ref in enumerate((x0, x1)):

        @pl.when(step // 2 == number)
        def _(x_ref=x_ref):
            add_projection(x_ref, gain, wq, wk, wv, acc, squares)


def last_kernel(
    order, x0, x1, gain, wq, wk, wv, gate, acc_in, squares_in, cosine, sine, q_ref, kv_ref, acc, squares
):
    step = pl.program_id(0)

    @pl.when(step == 0)
    def _():
        acc[...] = acc_in[...]
        squares[...] = squares_in[...]

    for number, x_ref in enumerate((x0, x1)):

        @pl.when(step // 2 == number)
        def _(x_ref=x_ref):
            add_projection(x_ref, gain, wq, wk, wv, acc, squares)

    @pl.when(step == 3)
    def _():
        scale = lax.rsqrt(squares[...] * (1.0 / (MP * FEATURES)) + epsilon)
        cos_all = cosine[...]
        sin_all = sine[...]
        for head in range(6):
            cols = slice(head * HEAD_DIM, (head + 1) * HEAD_DIM)
            part = acc[:, cols] * scale
            turned = part * cos_all + pltpu.roll(part, 64, 1) * sin_all
            if head < HEADS_LOCAL:
                q_ref[:, cols] = (turned * query_scalar ** (-0.5)).astype(BF16)
            else:
                at = (head - HEADS_LOCAL) * HEAD_DIM
                kv_ref[:, at : at + HEAD_DIM] = turned.astype(BF16)
        kv_ref[:, KV_WIDTH : KV_WIDTH + HEAD_DIM] = (acc[:, 768:896] * scale).astype(BF16)
        kv_ref[:, KV_WIDTH + HEAD_DIM :] = (acc[:, 896:] * scale).astype(BF16)


def chunk_specs(rows, first):
    chunk = lambda width: pl.BlockSpec(
        (STEP, width), lambda i, order: (order[first + i // 2] * 2 + i % 2, 0)
    )
    return [
        pl.BlockSpec((STEP, rows), lambda i, order: (jnp.minimum(i, 1), 0)),
        pl.BlockSpec((STEP, rows), lambda i, order: (jnp.maximum(i - 2, 0), 0)),
        pl.BlockSpec(
            (1, 1, STEP), lambda i, order: (order[first + i // 2] * 2 + i % 2, 0, 0)
        ),
        chunk(512),
        chunk(256),
        chunk(256),
    ]


def project_first(order, xs, gain, wq, wk, wv):
    full = lambda shape: pl.BlockSpec(shape, lambda i, order: (0,) * len(shape))
    shapes = [(ROWS, 1024), (ROWS, HEAD_DIM)]
    return pl.pallas_call(
        first_kernel,
        grid_spec=pltpu.PrefetchScalarGridSpec(
            num_scalar_prefetch=1,
            grid=(4,),
            in_specs=chunk_specs(ROWS, 0),
            out_specs=[full(s) for s in shapes],
        ),
        out_shape=[jax.ShapeDtypeStruct(s, F32) for s in shapes],
        compiler_params=params(),
        cost_estimate=cost(1, 1),
    )(order, *xs, gain, wq, wk, wv)


def project_last(half, order, xs, gain, wq, wk, wv, gate, carried, tables):
    place = lambda i, order: (half, 0)
    out = lambda i, order: (0, 0)
    return pl.pallas_call(
        last_kernel,
        grid_spec=pltpu.PrefetchScalarGridSpec(
            num_scalar_prefetch=1,
            grid=(4,),
            in_specs=chunk_specs(HALF, 2)
            + [
                IN_HBM,
                pl.BlockSpec((HALF, 1024), place),
                pl.BlockSpec((HALF, HEAD_DIM), place),
                pl.BlockSpec((HALF, HEAD_DIM), place),
                pl.BlockSpec((HALF, HEAD_DIM), place),
            ],
            out_specs=[pl.BlockSpec((HALF, 512), out)] * 2,
            scratch_shapes=[pltpu.VMEM((HALF, 1024), F32), pltpu.VMEM((HALF, HEAD_DIM), F32)],
        ),
        out_shape=[jax.ShapeDtypeStruct((HALF, 512), BF16)] * 2,
        compiler_params=params(),
        cost_estimate=cost(1, 1),
    )(order, *xs, gain, wq, wk, wv, gate, *carried, *tables)


def attention_kernel(half, where, ids, lengths, reals, q_ref, own_a, own_b, one_a, one_b, two_a, two_b, *refs):
    prefix, (out, held, sems) = refs[:4], refs[4:]
    local = where[2]
    length = lengths[ids[where[1]]]
    real = reals[where[1]]

    def copies(branch):
        late = [
            (prefix[r].at[1], pl.multiple_of((where[3] ^ r) * HELD, HELD), HELD) for r in range(4)
        ]
        early = [
            (prefix[r].at[0], pl.multiple_of((where[3] ^ r) * HELD, HELD), HELD) for r in range(4)
        ]
        one = [(one_a, ROWS, HALF), (one_b, ROWS + HALF, HALF)]
        two = [(two_a, 0, HALF), (two_b, HALF, HALF)]
        if branch == 0:
            got = early + [(a, pl.multiple_of(at + ROWS, HELD), n) for a, at, n in late]
        elif branch == 1:
            got = late + one
        else:
            got = two + one
        return [
            pltpu.make_async_copy(a, held.at[pl.ds(at, n)], sems.at[i])
            for i, (a, at, n) in enumerate(got)
        ]

    for branch in range(3):

        @pl.when(local == branch if branch < 2 else local >= 2)
        def _(branch=branch):
            started = copies(branch)
            for one in started:
                one.start()
            for one in started:
                one.wait()

    column = lax.broadcasted_iota(jnp.int32, (1, ROWS), 1)
    shift_two = jnp.where(local < 2, length, 0)
    limit_two = jnp.where(local < 2, WINDOW - ROWS * local - length, 0)
    shift_one = jnp.where(local < 1, length, 0)
    limit_one = jnp.where(local < 1, ROWS - length, 0)
    place_two = (column - shift_two) & (ROWS - 1)
    place_one = (column - shift_one) & (ROWS - 1)
    one_ok = place_one >= limit_one
    block = 128
    for chunk in range(HALF // block):
        start = chunk * block
        reach = start + block
        row = start + lax.broadcasted_iota(jnp.int32, (block, 1), 0)
        two_ok = place_two > jnp.maximum(row + half * HALF, limit_two - 1)
        own_ok = column[:, :reach] <= row
        row_real = row + half * HALF + local * ROWS < real
        for head in range(HEADS_LOCAL):
            k_cols = slice((head // 2) * HEAD_DIM, (head // 2 + 1) * HEAD_DIM)
            v_cols = slice(KV_WIDTH + k_cols.start, KV_WIDTH + k_cols.stop)
            cols = slice(head * HEAD_DIM, (head + 1) * HEAD_DIM)
            q = q_ref[start:reach, cols]
            parts = [
                (two_ok, held[:ROWS, k_cols], held[:ROWS, v_cols]),
                (one_ok, held[ROWS:, k_cols], held[ROWS:, v_cols]),
            ]
            if half:
                parts.append((None, own_a[:, k_cols], own_a[:, v_cols]))
            last = own_b if half else own_a
            parts.append((own_ok, last[:reach, k_cols], last[:reach, v_cols]))
            scores = []
            for ok, keys, _ in parts:
                s = lax.dot_general(q, keys, NT, preferred_element_type=F32)
                scores.append(s if ok is None else jnp.where(ok, s, -1e30))
            top = functools.reduce(
                jnp.maximum, [jnp.max(s, 1, keepdims=True) for s in scores]
            )
            total = 0.0
            got = 0.0
            for s, (_, _, values) in zip(scores, parts):
                weights = jnp.exp(s - top)
                total += jnp.sum(weights, 1, keepdims=True)
                got += jnp.dot(weights.astype(BF16), values, preferred_element_type=F32)
            got = jnp.where(row_real, got / total, 0.0)
            out[start:reach, cols] = got.astype(BF16)


def attention(half, scalars, q, own_a, own_b, one_a, one_b, two_a, two_b, prefix):
    full = pl.BlockSpec((HALF, 512), lambda i, *scalars: (0, 0))
    return pl.pallas_call(
        functools.partial(attention_kernel, half),
        grid_spec=pltpu.PrefetchScalarGridSpec(
            num_scalar_prefetch=4,
            grid=(1,),
            in_specs=[full] * 3 + [IN_HBM] * 8,
            out_specs=full,
            scratch_shapes=[
                pltpu.VMEM((2 * ROWS, PAIR), BF16),
                pltpu.SemaphoreType.DMA((8,)),
            ],
        ),
        out_shape=jax.ShapeDtypeStruct((HALF, 512), BF16),
        compiler_params=params(),
        cost_estimate=cost(
            4 * HEADS_LOCAL * HALF * 1536 * 128, 2_500_000, HEADS_LOCAL * HALF * 1536
        ),
    )(*scalars, q, own_a, own_b, one_a, one_b, two_a, two_b, *prefix)


def turn_kernel(where, w_ref, gate, own, near, piece_a, piece_b, turned):
    step = pl.program_id(0)
    strip = pl.ds(pl.multiple_of(where[3] * STRIP, 16), STRIP)
    for m in range(MP):
        columns = lambda flip: slice((m ^ flip) * FEATURES, ((m ^ flip) + 1) * FEATURES)

        @pl.when(where[0] == m)
        def _(columns=columns):
            own[...] = jnp.transpose(w_ref[:, columns(0)])
            near[...] = jnp.transpose(w_ref[:, columns(1)])

            @pl.when(step == where[1])
            def _():
                turned[...] = jnp.transpose(w_ref[:, columns(2)])
                piece_a[...] = turned[strip, :]
                turned[...] = jnp.transpose(w_ref[:, columns(3)])
                piece_b[...] = turned[strip, :]


def turned_weights(where, w_out, gate):
    whole = pl.BlockSpec((FEATURES, 128), lambda i, where: (0, i))
    piece = pl.BlockSpec((STRIP, 128), lambda i, where: (0, 0))
    return pl.pallas_call(
        turn_kernel,
        grid_spec=pltpu.PrefetchScalarGridSpec(
            num_scalar_prefetch=1,
            grid=(4,),
            in_specs=[pl.BlockSpec((128, MP * FEATURES), lambda i, where: (i, 0)), IN_HBM],
            out_specs=[whole, whole, piece, piece],
            scratch_shapes=[pltpu.VMEM((FEATURES, 128), BF16)],
        ),
        out_shape=[jax.ShapeDtypeStruct((FEATURES, 512), BF16)] * 2
        + [jax.ShapeDtypeStruct((STRIP, 128), BF16)] * 2,
        compiler_params=params(),
        cost_estimate=cost(1, 1),
    )(where, w_out, gate)


def pick_kernel(where, ids, lengths, rows_ref, gate, *outs):
    step = pl.program_id(0)
    reach = lengths[ids[(where[1] + step) & 3]]
    held_at = where[4] * HELD + lax.broadcasted_iota(jnp.int32, (HELD, 1), 0)
    wanted = (held_at < reach) & (held_at >= reach - WINDOW)
    for number, out in enumerate(outs):

        @pl.when(step == number)
        def _(out=out):
            for part in range(2):
                rows = rows_ref[0, :, part, :].astype(F32)
                out[:, part * KV_WIDTH : (part + 1) * KV_WIDTH] = jnp.where(
                    wanted, rows, 0.0
                ).astype(BF16)


def picked_rows(where, ids, lengths, prefix_cache, gate):
    return pl.pallas_call(
        pick_kernel,
        grid_spec=pltpu.PrefetchScalarGridSpec(
            num_scalar_prefetch=3,
            grid=(4,),
            in_specs=[
                pl.BlockSpec(
                    (1, HELD, 2, KV_WIDTH),
                    lambda i, where, ids, lengths: (ids[(where[1] + i) & 3], 0, 0, 0),
                ),
                IN_HBM,
            ],
            out_specs=[pl.BlockSpec((HELD, PAIR), lambda i, *scalars: (0, 0))] * 4,
        ),
        out_shape=[jax.ShapeDtypeStruct((HELD, PAIR), BF16)] * 4,
        compiler_params=params(),
        cost_estimate=cost(1, 1),
    )(where, ids, lengths, prefix_cache, gate)


def order_kernel(where, ids, lengths, mine, twin, out):
    length = lengths[ids[where[1]]]
    row = where[2] * HELD + lax.broadcasted_iota(jnp.int32, (HELD, 1), 0)
    late = ((row - length) & (WINDOW - 1)) >= ROWS
    a = mine[...].astype(F32)
    b = twin[...].astype(F32)
    out[0] = jnp.where(late, b, a).astype(BF16)
    out[1] = jnp.where(late, a, b).astype(BF16)


def ordered_rows(where, ids, lengths, mine, twin):
    part = pl.BlockSpec((HELD, PAIR), lambda i, *scalars: (0, 0))
    return pl.pallas_call(
        order_kernel,
        grid_spec=pltpu.PrefetchScalarGridSpec(
            num_scalar_prefetch=3,
            grid=(1,),
            in_specs=[part, part],
            out_specs=pl.BlockSpec((2, HELD, PAIR), lambda i, *scalars: (0, 0, 0)),
        ),
        out_shape=jax.ShapeDtypeStruct((2, HELD, PAIR), BF16),
        compiler_params=params(),
        cost_estimate=cost(1, 1),
    )(where, ids, lengths, mine, twin)


def near_kernel(c0a, c0b, c1a, c1b, w0, w1, out):
    for half, (c0, c1) in enumerate(((c0a, c1a), (c0b, c1b))):
        out[:, half * HALF : (half + 1) * HALF] = lax.dot_general(
            w0[...], c0[...], NT, preferred_element_type=F32
        ) + lax.dot_general(w1[...], c1[...], NT, preferred_element_type=F32)


def near_output(contexts, weights):
    full = lambda shape: pl.BlockSpec(shape, lambda i: (0, 0))
    strip = pl.BlockSpec((STRIP, 512), lambda i: (i, 0))
    return pl.pallas_call(
        near_kernel,
        grid=(4,),
        in_specs=[full((HALF, 512))] * 4 + [strip] * 2,
        out_specs=strip,
        out_shape=jax.ShapeDtypeStruct((FEATURES, ROWS), F32),
        compiler_params=params(),
        cost_estimate=cost(2 * ROWS * 1024 * FEATURES, 6_000_000),
    )(*contexts, *weights)


def far_kernel(where, c0a, c0b, c1a, c1b, near, p0, p1, p2, p3, out, squares, held, sems):
    z, x = where[3], where[1]
    pending = []
    for j, pieces in enumerate((p0, p1, p2, p3)):
        lanes = pl.multiple_of(((x - j) & 3) * HEAD_DIM, HEAD_DIM)
        for r in range(4):
            rows = pl.multiple_of(((z - r) & 3) * STRIP, 16)
            for b in range(2):
                copy = pltpu.make_async_copy(
                    pieces.at[r, b],
                    held.at[b, pl.ds(rows, STRIP), pl.ds(lanes, HEAD_DIM)],
                    sems.at[j * 8 + r * 2 + b],
                )
                copy.start()
                pending.append(copy)
    for copy in pending:
        copy.wait()
    for half, (c0, c1) in enumerate(((c0a, c1a), (c0b, c1b))):
        cols = slice(half * HALF, (half + 1) * HALF)
        total = jnp.zeros((1, HALF), F32)
        for strip in range(4):
            rows = slice(strip * STRIP, (strip + 1) * STRIP)
            got = (
                near[rows, cols]
                + lax.dot_general(held[0, rows], c0[...], NT, preferred_element_type=F32)
                + lax.dot_general(held[1, rows], c1[...], NT, preferred_element_type=F32)
            )
            out[rows, cols] = got
            total += jnp.sum(got * got, 0, keepdims=True)
        squares[:, cols] = total


def far_output(where, contexts, near, pieces):
    full = lambda shape: pl.BlockSpec(shape, lambda i, where: (0, 0))
    return pl.pallas_call(
        far_kernel,
        grid_spec=pltpu.PrefetchScalarGridSpec(
            num_scalar_prefetch=1,
            grid=(1,),
            in_specs=[full((HALF, 512))] * 4 + [full((FEATURES, ROWS))] + [IN_HBM] * 4,
            out_specs=[full((FEATURES, ROWS)), full((1, ROWS))],
            scratch_shapes=[
                pltpu.VMEM((2, FEATURES, 512), BF16),
                pltpu.SemaphoreType.DMA((32,)),
            ],
        ),
        out_shape=[
            jax.ShapeDtypeStruct((FEATURES, ROWS), F32),
            jax.ShapeDtypeStruct((1, ROWS), F32),
        ],
        compiler_params=params(),
        cost_estimate=cost(2 * ROWS * 1024 * FEATURES, 8_000_000),
    )(where, *contexts, near, *pieces)


def rope_tables(places):
    lane = jnp.arange(HEAD_DIM)
    frequency = rope_base ** (-((lane % 64).astype(F32) * 2.0 / HEAD_DIM))
    angles = places.astype(F32)[:, None] * frequency[None, :]
    return jnp.cos(angles), jnp.where(lane[None, :] < 64, -jnp.sin(angles), jnp.sin(angles))


def shards(
    tokens,
    gain_pre,
    w_query,
    w_key,
    w_value,
    w_out,
    gain_post,
    prefix_cache,
    template_ids,
    prefix_lengths,
    doc_lengths,
):
    member = lax.axis_index("mp")
    place = lax.axis_index("seq")
    doc = place // DOC_SHARDS
    local = place % DOC_SHARDS
    where = jnp.stack(
        [member, doc, local, place % 4, place, member, member ^ 1, member ^ 2, member ^ 3]
    ).astype(jnp.int32)
    scalars = (where, template_ids, prefix_lengths)

    turned_tokens = tokens.T
    near = across_mp(turned_tokens, 1)
    far_a = across_mp(turned_tokens[:, :HALF], 2)

    mine, *others = picked_rows(*scalars, prefix_cache, near)
    for by, other in enumerate(others, 1):
        mine = mine + along_x(other, by)
    ordered = ordered_rows(*scalars, mine, to_twin(mine))
    prefix = [ordered] + [z_flip(ordered, flip) for flip in (1, 2, 3)]

    template = jnp.sum(jnp.where(jnp.arange(DOCS) == doc, template_ids, 0))
    length = jnp.sum(jnp.where(jnp.arange(8) == template, prefix_lengths, 0))
    tables = rope_tables(length + local * ROWS + jnp.arange(ROWS))
    gain = gain_pre.reshape(2 * MP, 1, STEP)
    order = where[5:]
    weights = (w_query, w_key, w_value)
    carried = project_first(order, [turned_tokens, near], gain, *weights)
    far_b = across_mp(after(turned_tokens[:, HALF:], far_a, carried[1]), 2)

    w_own, w_give, piece_a, piece_b = turned_weights(where, w_out, carried[1])
    w_near = across_mp(w_give, 1)
    w_piece = jnp.stack([across_mp(piece_a, 2), across_mp(piece_b, 3)])
    w_line = jnp.stack([w_piece] + [along_z(w_piece, by) for by in (1, 2, 3)])
    w_far = [w_line] + [along_x(w_line, by) for by in (1, 2, 3)]

    gate = near
    q_parts, kv_parts, one_back, two_back = [], [], [], []
    for half, far in enumerate((far_a, far_b)):
        q, kv = project_last(
            half, order, [far, across_mp(far, 1)], gain, *weights, gate, carried, tables
        )
        gate = kv
        q_parts.append(q)
        kv_parts.append(kv)
        one_back.append(within_doc(kv, 1))
        two_back.append(within_doc(kv, 2))
    scalars = (*scalars, doc_lengths)
    c_own, c_near, c_far, c_far_near = [], [], [], []
    for half in range(2):
        context = attention(
            half, scalars, q_parts[half], *kv_parts, *one_back, *two_back, prefix
        )
        c_own.append(context)
        c_far.append(across_mp(context, 2))
        c_near.append(across_mp(context, 1))
        c_far_near.append(across_mp(c_far[-1], 1))
    near_sum = near_output([*c_own, *c_near], [w_own, w_near])
    attended, own_squares = far_output(where, [*c_far, *c_far_near], near_sum, w_far)
    total = own_squares
    for flip in (1, 2, 3):
        total = total + across_mp(own_squares, flip)
    scale = lax.rsqrt(total * (1.0 / (MP * FEATURES)) + epsilon)
    result = turned_tokens.astype(F32) + gain_post[:, None] * attended * scale
    return result.astype(BF16).T


def solution(mesh):
    placed = (
        P("seq", "mp"),
        P(),
        P(None, "mp"),
        P(None, "mp"),
        P(None, "mp"),
        P("mp", None),
        P("mp"),
        P(None, "seq", None, "mp"),
        P(),
        P(),
        P(),
    )
    return jax.shard_map(
        shards, mesh=mesh, in_specs=placed, out_specs=P("seq", "mp"), check_vma=False
    )
```

time: 217 us -> 176 us (0.81)
  the two profiles are of different devices: /device:TPU:43 before, /device:TPU:1 now
where the time goes in v2:
time: 176 us; the launch traced here: 175 us
  Pallas kernels  64.6 us (37%)
  starting transfers between devices  49.4 us (28%)
  waiting for transfers between devices  44 us (25%)
  other arithmetic  10.4 us (6%)
  local copies, waits for them, and re-layouts  6 us (3%)
    ppermute x17, starting transfers between devices, across_mp(): return lax.ppermute(array, 'mp', [(i, i ^ flip) for i in range(MP)])  23.7 us
    ppermute x6, waiting for transfers between devices, along_x(): return lax.ppermute(array, 'seq', pairs)  20.3 us
    ppermute x3, waiting for transfers between devices, z_flip(): lax.ppermute(array, 'seq', [(i, i ^ flip) for i in range(DOCS * DOC_SHARD...  15.3 us
    pallas_call x2, Pallas kernels, project_last(): pl.pallas_call(last_kernel, grid_spec=pltpu.PrefetchScalarGridSpec(num_sc...  14.8 us
    pallas_call x2, Pallas kernels, attention(): pl.pallas_call(functools.partial(attention_kernel, half), grid_spec=pltpu...  14.5 us
    pallas_call x1, Pallas kernels, project_first(): pl.pallas_call(first_kernel, grid_spec=pltpu.PrefetchScalarGridSpec(num_s...  8.73 us
    ppermute x17, waiting for transfers between devices, across_mp(): return lax.ppermute(array, 'mp', [(i, i ^ flip) for i in range(MP)])  8.4 us
    pallas_call x1, Pallas kernels, far_output(): pl.pallas_call(far_kernel, grid_spec=pltpu.PrefetchScalarGridSpec(num_sca...  8.04 us
  transfers between devices with their start and end apart: 34, of which 11 were waited for; matrix products, arithmetic and copies ran while one was open for 5% of the time, Pallas kernels for 32%

profile of v2, /device:TPU:1, one launch (start us, length us, event | category | flops | bytes accessed | tf_op | source)
XLA Modules:
  0.0 175.3 jit_solution(10664074571422371116)
XLA Ops:
  0.0 1.4 collective-permute-start.2
  1.4 1.4 fusion.8
  2.8 3.1 %collective-permute-start = (bf16[1344,256]{1,0:T(8,128)(2,1)S(1)}, bf16[1344,256]{1,0:T(8,128)(2,1)S(1)}, u32[]{:S(2)}, u32[]{:S(2)}) collective-permute-start(bf16[1344,256]{1,0:T(8,128)(2,1)S(1)} %get-tuple-element.40), channel_id=1, source_target_pairs={{0,2},{1,3},{2,0},{3,1},{4,6},{5,7},{6,4},{7,5},{8,10},{9,11},{10,... | collective-permute-start | bytes 2064392 | tf_op jit(solution)/shard_map/ppermute | solution.py:42
  5.9 0.7 reshape.27.gain
  6.6 0.6 pad_add_fusion.order
  7.2 1.1 copy-done.1
  8.3 8.7 %shard_map.109 = (f32[512,1024]{1,0:T(8,128)}, f32[512,128]{1,0:T(8,128)}) custom-call(s32[4]{0:T(128)} %pad_add_fusion.order, bf16[1344,512]{1,0:T(8,128)(2,1)} %bitcast.22, bf16[1344,512]{1,0:T(8,128)(2,1)} %copy-done.1, f32[8,1,672]{2,1,0:T(1,128)} %reshape.27.gain, bf16[5376,512]{1,0:T(8,128)(2,1)} %wq.5, bf16[5376,256]{1,0:T(8,128)(2,1)} %wk.5, ...), custom_call_target="tpu_custom_call" | custom-call | flops 1 | bytes 1 | tf_op jit(solution)/shard_map/pallas_call | solution.py:175
  17.0 4.5 %collective-permute-done.x0 = bf16[1344,256]{1,0:T(8,128)(2,1)S(1)} collective-permute-done((bf16[1344,256]{1,0:T(8,128)(2,1)S(1)}, bf16[1344,256]{1,0:T(8,128)(2,1)S(1)}, u32[]{:S(2)}, u32[]{:S(2)}) %collective-permute-start) | collective-permute-done | bytes 688160 | tf_op jit(solution)/shard_map/ppermute | solution.py:42
  21.5 2.9 %collective-permute-start.3 = (bf16[1344,256]{1,0:T(8,128)(2,1)S(1)}, bf16[1344,256]{1,0:T(8,128)(2,1)S(1)}, u32[]{:S(2)}, u32[]{:S(2)}) collective-permute-start(bf16[1344,256]{1,0:T(8,128)(2,1)S(1)} %get-tuple-element.26), channel_id=1, source_target_pairs={{0,2},{1,3},{2,0},{3,1},{4,6},{5,7},{6,4},{7,5},{8,10},{9,11},{10,... | collective-permute-start | bytes 2064392 | tf_op jit(solution)/shard_map/ppermute | solution.py:42
  24.5 0.6 fusion.1
  25.1 1.2 fusion.2
  26.9 0.6 stack.62.where
  27.5 4.0 %shard_map.112 = (bf16[128,512]{1,0:T(8,128)(2,1)}, bf16[128,512]{1,0:T(8,128)(2,1)}, bf16[128,512]{1,0:T(8,128)(2,1)}, bf16[128,512]{1,0:T(8,128)(2,1)}) custom-call(s32[9]{0:T(128)} %stack.62.where, s32[4]{0:T(128)} %ids.7, s32[8]{0:T(128)} %lengths.7, bf16[8,128,2,256]{3,2,1,0:T(2,128)(2,1)} %rows_ref.1, bf16[1344,512]{1,0:T(8,128)(2,1)} %copy-done.1), custom_call_target="tpu_custom_call" | custom-call | flops 1 | bytes 1 | tf_op jit(solution)/shard_map/pallas_call | solution.py:373
  31.5 2.5 %collective-permute-start.11 = (bf16[128,512]{1,0:T(8,128)(2,1)}, bf16[128,512]{1,0:T(8,128)(2,1)S(1)}, u32[]{:S(2)}, u32[]{:S(2)}) collective-permute-start(bf16[128,512]{1,0:T(8,128)(2,1)} %get-tuple-element.31), channel_id=1, source_target_pairs={{0,96},{4,100},{8,104},{12,108},{16,112},{20,116},{24,120},{28,124... | collective-permute-start | bytes 393224 | tf_op jit(solution)/shard_map/ppermute | solution.py:56
  34.0 1.4 collective-permute-start.1
  35.4 0.5 collective-permute-start.10
  35.9 0.6 collective-permute-start.9
  36.5 6.7 %shard_map.116 = (bf16[1344,512]{1,0:T(8,128)(2,1)}, bf16[1344,512]{1,0:T(8,128)(2,1)}, bf16[336,128]{1,0:T(8,128)(2,1)}, bf16[336,128]{1,0:T(8,128)(2,1)}) custom-call(s32[9]{0:T(128)} %stack.62.where, bf16[512,5376]{1,0:T(8,128)(2,1)} %w_ref.1, f32[512,128]{1,0:T(8,128)} %get-tuple-element.23.squares_in.gate), custom_call_target="tpu_custom_call" | custom-call | flops 1 | bytes 1 | tf_op jit(solution)/shard_map/pallas_call | solution.py:340
  43.1 0.7 collective-permute-start.22
  43.9 0.3 collective-permute-start.24
  44.2 1.1 collective-permute-done.9
  45.3 0.6 copy-done.22
  46.0 0.9 add_add_fusion.mine
  46.9 0.5 collective-permute-start.12
  47.4 1.8 %negate_select_fusion = (f32[512,128]{1,0:T(8,128)}, f32[512,128]{1,0:T(8,128)}) fusion(f32[128]{0:T(128)S(1)} %fusion.6, f32[512]{0:T(512)S(1)} %add_convert_fusion.1, pred[128]{0:T(512)(128)(4,1)S(1)} %iota_compare_fusion), kind=kLoop, calls=%fused_computation.3 | loop fusion | flops 196608 | bytes 526976 | tf_op jit(solution)/shard_map/jit(_where)/select_n | solution.py:499
  49.2 7.5 %shard_map.110 = (bf16[256,512]{1,0:T(8,128)(2,1)}, bf16[256,512]{1,0:T(8,128)(2,1)}) custom-call(s32[4]{0:T(128)} %pad_add_fusion.order, bf16[1344,256]{1,0:T(8,128)(2,1)} %copy-done.16, bf16[1344,256]{1,0:T(8,128)(2,1)} %collective-permute-done.1.x1, f32[8,1,672]{2,1,0:T(1,128)} %reshape.27.gain, bf16[5376,512]{1,0:T(8,128)(2,1)} %wq.5, ...), custom_call_target="tpu_custom_call" | custom-call | flops 1 | bytes 1 | tf_op jit(solution)/shard_map/pallas_call | solution.py:192
  56.7 1.7 collective-permute-start.5
  58.5 3.3 %collective-permute-start.7 = (bf16[256,512]{1,0:T(8,128)(2,1)}, bf16[256,512]{1,0:T(8,128)(2,1)S(1)}, u32[]{:S(2)}, u32[]{:S(2)}) collective-permute-start(bf16[256,512]{1,0:T(8,128)(2,1)} %get-tuple-element.25.gate.own_a), channel_id=1, source_target_pairs={{0,8},{4,12},{8,16},{12,20},{16,24},{20,28},{24,0},{28,4},{32,40},... | collective-permute-start | bytes 786440 | tf_op jit(solution)/shard_map/ppermute | solution.py:84
  61.8 2.4 %shard_map.113.refs_0_ = bf16[2,128,512]{2,1,0:T(8,128)(2,1)} custom-call(s32[9]{0:T(128)} %stack.62.where, s32[4]{0:T(128)} %ids.7, s32[8]{0:T(128)} %lengths.7, bf16[128,512]{1,0:T(8,128)(2,1)} %copy-done.17, bf16[128,512]{1,0:T(8,128)(2,1)} %copy-done.23), custom_call_target="tpu_custom_call" | custom-call | flops 1 | bytes 1 | tf_op jit(solution)/shard_map/pallas_call | solution.py:405
  64.2 2.6 %collective-permute-start.23 = (bf16[336,128]{1,0:T(8,128)(2,1)S(1)}, bf16[336,128]{1,0:T(8,128)(2,1)S(1)}, u32[]{:S(2)}, u32[]{:S(2)}) collective-permute-start(bf16[336,128]{1,0:T(8,128)(2,1)S(1)} %copy-done.28), channel_id=1, source_target_pairs={{0,2},{1,3},{2,0},{3,1},{4,6},{5,7},{6,4},{7,5},{8,10},{9,11},{10,... | collective-permute-start | bytes 258056 | tf_op jit(solution)/shard_map/ppermute | solution.py:42
  66.8 7.3 %shard_map.111 = (bf16[256,512]{1,0:T(8,128)(2,1)}, bf16[256,512]{1,0:T(8,128)(2,1)}) custom-call(s32[4]{0:T(128)} %pad_add_fusion.order, bf16[1344,256]{1,0:T(8,128)(2,1)} %copy-done.13, bf16[1344,256]{1,0:T(8,128)(2,1)} %collective-permute-done.4.x1, f32[8,1,672]{2,1,0:T(1,128)} %reshape.27.gain, bf16[5376,512]{1,0:T(8,128)(2,1)} %wq.5, ...), custom_call_target="tpu_custom_call" | custom-call | flops 1 | bytes 1 | tf_op jit(solution)/shard_map/pallas_call | solution.py:192
  74.1 2.1 %collective-permute-start.14 = (bf16[2,128,512]{2,1,0:T(8,128)(2,1)S(1)}, bf16[2,128,512]{2,1,0:T(8,128)(2,1)S(1)}, u32[]{:S(2)}, u32[]{:S(2)}) collective-permute-start(bf16[2,128,512]{2,1,0:T(8,128)(2,1)S(1)} %copy-done.3), channel_id=1, source_target_pairs={{0,8},{4,12},{8,0},{12,4},{16,24},{20,28},{24,16},{28,20},{32,40},... | collective-permute-start | bytes 786440 | tf_op jit(solution)/shard_map/ppermute | solution.py:75
  76.3 4.3 %collective-permute-start.15 = (bf16[2,128,512]{2,1,0:T(8,128)(2,1)S(1)}, bf16[2,128,512]{2,1,0:T(8,128)(2,1)S(1)}, u32[]{:S(2)}, u32[]{:S(2)}) collective-permute-start(bf16[2,128,512]{2,1,0:T(8,128)(2,1)S(1)} %copy-done.3), channel_id=1, source_target_pairs={{0,12},{4,8},{8,4},{12,0},{16,28},{20,24},{24,20},{28,16},{32,44},... | collective-permute-start | bytes 786440 | tf_op jit(solution)/shard_map/ppermute | solution.py:75
  80.6 0.6 collective-permute-start.6
  81.1 1.8 %collective-permute-start.8 = (bf16[256,512]{1,0:T(8,128)(2,1)}, bf16[256,512]{1,0:T(8,128)(2,1)S(1)}, u32[]{:S(2)}, u32[]{:S(2)}) collective-permute-start(bf16[256,512]{1,0:T(8,128)(2,1)} %get-tuple-element.27.own_b), channel_id=1, source_target_pairs={{0,8},{4,12},{8,16},{12,20},{16,24},{20,28},{24,0},{28,4},{32,40},... | collective-permute-start | bytes 786440 | tf_op jit(solution)/shard_map/ppermute | solution.py:84
  83.0 1.8 %collective-permute-done.14.refs_2_ = bf16[2,128,512]{2,1,0:T(8,128)(2,1)S(1)} collective-permute-done((bf16[2,128,512]{2,1,0:T(8,128)(2,1)S(1)}, bf16[2,128,512]{2,1,0:T(8,128)(2,1)S(1)}, u32[]{:S(2)}, u32[]{:S(2)}) %collective-permute-start.14) | collective-permute-done | bytes 262176 | tf_op jit(solution)/shard_map/ppermute | solution.py:75
  84.8 4.1 %collective-permute-start.27 = (bf16[2,336,128]{2,1,0:T(8,128)(2,1)S(1)}, bf16[2,336,128]{2,1,0:T(8,128)(2,1)S(1)}, u32[]{:S(2)}, u32[]{:S(2)}) collective-permute-start(bf16[2,336,128]{2,1,0:T(8,128)(2,1)S(1)} %get-tuple-element.42), channel_id=1, source_target_pairs={{0,12},{4,0},{8,4},{12,8},{16,28},{20,16},{24,20},{28,24},{32,44},... | collective-permute-start | bytes 516104 | tf_op jit(solution)/shard_map/ppermute | solution.py:66
  88.9 13.5 %collective-permute-done.15.refs_3_ = bf16[2,128,512]{2,1,0:T(8,128)(2,1)S(1)} collective-permute-done((bf16[2,128,512]{2,1,0:T(8,128)(2,1)S(1)}, bf16[2,128,512]{2,1,0:T(8,128)(2,1)S(1)}, u32[]{:S(2)}, u32[]{:S(2)}) %collective-permute-start.15) | collective-permute-done | bytes 262176 | tf_op jit(solution)/shard_map/ppermute | solution.py:75
  102.6 0.5 copy-done.10
  103.4 7.1 %shard_map.114.c0a = bf16[256,512]{1,0:T(8,128)(2,1)} custom-call(s32[9]{0:T(128)} %stack.62.where, s32[4]{0:T(128)} %ids.7, s32[8]{0:T(128)} %lengths.7, s32[4]{0:T(128)} %reals.3, bf16[256,512]{1,0:T(8,128)(2,1)} %get-tuple-element.24.q_ref, bf16[256,512]{1,0:T(8,128)(2,1)} %get-tuple-element.25.gate.own_a, bf16[256,512]{1,0:T(8,128)(2,1)} %get-tuple-element.27.own_b, ...), custom_call_target="tpu_custom_call" | custom-call | flops 805306368 | bytes 2500000 | tf_op jit(solution)/shard_map/pallas_call | solution.py:298
  110.6 7.4 %shard_map.115.c0b = bf16[256,512]{1,0:T(8,128)(2,1)} custom-call(s32[9]{0:T(128)} %stack.62.where, s32[4]{0:T(128)} %ids.7, s32[8]{0:T(128)} %lengths.7, s32[4]{0:T(128)} %reals.3, bf16[256,512]{1,0:T(8,128)(2,1)} %get-tuple-element.32.q_ref, bf16[256,512]{1,0:T(8,128)(2,1)} %get-tuple-element.25.gate.own_a, bf16[256,512]{1,0:T(8,128)(2,1)} %get-tuple-element.27.own_b, ...), custom_call_target="tpu_custom_call" | custom-call | flops 805306368 | bytes 2500000 | tf_op jit(solution)/shard_map/pallas_call | solution.py:298
  118.0 3.0 %collective-permute-start.17 = (bf16[256,512]{1,0:T(8,128)(2,1)}, bf16[256,512]{1,0:T(8,128)(2,1)}, u32[]{:S(2)}, u32[]{:S(2)}) collective-permute-start(bf16[256,512]{1,0:T(8,128)(2,1)} %shard_map.115.c0b), channel_id=1, source_target_pairs={{0,2},{1,3},{2,0},{3,1},{4,6},{5,7},{6,4},{7,5},{8,10},{9,11},{10,... | collective-permute-start | bytes 786440 | tf_op jit(solution)/shard_map/ppermute | solution.py:42
  121.1 1.1 pad_maximum_fusion.p0
  122.2 1.2 collective-permute-start.28
  123.4 2.0 %collective-permute-start.29 = (bf16[4,2,336,128]{3,2,1,0:T(8,128)(2,1)S(1)}, bf16[4,2,336,128]{3,2,1,0:T(8,128)(2,1)S(1)}, u32[]{:S(2)}, u32[]{:S(2)}) collective-permute-start(bf16[4,2,336,128]{3,2,1,0:T(8,128)(2,1)S(1)} %pad_maximum_fusion.p0), channel_id=1, source_target_pairs={{0,64},{4,68},{8,72},{12,76},{16,80},{20,84},{24,88},{28,92},{32,9... | collective-permute-start | bytes 2064392 | tf_op jit(solution)/shard_map/ppermute | solution.py:56
  125.3 0.5 collective-permute-start.30
  125.9 1.9 %collective-permute-start.20 = (bf16[256,512]{1,0:T(8,128)(2,1)S(1)}, bf16[256,512]{1,0:T(8,128)(2,1)S(1)}, u32[]{:S(2)}, u32[]{:S(2)}) collective-permute-start(bf16[256,512]{1,0:T(8,128)(2,1)S(1)} %copy-done.5), channel_id=1, source_target_pairs={{0,1},{1,0},{2,3},{3,2},{4,5},{5,4},{6,7},{7,6},{8,9},{9,8},{10,11... | collective-permute-start | bytes 786440 | tf_op jit(solution)/shard_map/ppermute | solution.py:42
  127.7 0.9 collective-permute-start.21
  128.7 0.2 collective-permute-done.20.c1a
  128.9 0.4 collective-permute-start.18
  129.3 0.9 collective-permute-done.21.c1b
  130.2 0.4 collective-permute-start.19
  130.5 5.4 %shard_map.117.near = f32[1344,512]{1,0:T(8,128)} custom-call(bf16[256,512]{1,0:T(8,128)(2,1)} %shard_map.114.c0a, bf16[256,512]{1,0:T(8,128)(2,1)} %shard_map.115.c0b, bf16[256,512]{1,0:T(8,128)(2,1)} %copy-done.18, bf16[256,512]{1,0:T(8,128)(2,1)} %collective-permute-done.21.c1b, bf16[1344,512]{1,0:T(8,128)(2,1)} %get-tuple-element.33.w0, ...), custom_call_target="tpu_custom_call" | custom-call | flops 1409286144 | bytes 6000000 | tf_op jit(solution)/shard_map/pallas_call | solution.py:429
  135.9 3.2 %collective-permute-done.28.p1 = bf16[4,2,336,128]{3,2,1,0:T(8,128)(2,1)S(1)} collective-permute-done((bf16[4,2,336,128]{3,2,1,0:T(8,128)(2,1)S(1)}, bf16[4,2,336,128]{3,2,1,0:T(8,128)(2,1)S(1)}, u32[]{:S(2)}, u32[]{:S(2)}) %collective-permute-start.28) | collective-permute-done | bytes 688160 | tf_op jit(solution)/shard_map/ppermute | solution.py:56
  139.2 15.1 %collective-permute-done.29.p2 = bf16[4,2,336,128]{3,2,1,0:T(8,128)(2,1)S(1)} collective-permute-done((bf16[4,2,336,128]{3,2,1,0:T(8,128)(2,1)S(1)}, bf16[4,2,336,128]{3,2,1,0:T(8,128)(2,1)S(1)}, u32[]{:S(2)}, u32[]{:S(2)}) %collective-permute-start.29) | collective-permute-done | bytes 688160 | tf_op jit(solution)/shard_map/ppermute | solution.py:56
  154.3 0.8 collective-permute-done.30.p3
  155.2 0.6 copy-done.19
  155.8 8.0 %shard_map.118 = (f32[1344,512]{1,0:T(8,128)}, f32[1,512]{1,0:T(1,128)}) custom-call(s32[9]{0:T(128)} %stack.62.where, bf16[256,512]{1,0:T(8,128)(2,1)} %collective-permute-done.16.c0a, bf16[256,512]{1,0:T(8,128)(2,1)} %collective-permute-done.17.c0b, bf16[256,512]{1,0:T(8,128)(2,1)} %copy-done.19, bf16[256,512]{1,0:T(8,128)(2,1)} %collective-permute-done.19.c1b, ...), custom_call_target="tpu_custom_call" | custom-call | flops 1409286144 | bytes 8000000 | tf_op jit(solution)/shard_map/pallas_call | solution.py:474
  163.9 3.2 %collective-permute-start.33 = (f32[1,512]{1,0:T(1,128)}, f32[1,512]{1,0:T(1,128)S(1)}, u32[]{:S(2)}, u32[]{:S(2)}) collective-permute-start(f32[1,512]{1,0:T(1,128)} %get-tuple-element.38), channel_id=1, source_target_pairs={{0,3},{1,2},{2,1},{3,0},{4,7},{5,6},{6,5},{7,4},{8,11},{9,10},{10,... | collective-permute-start | bytes 6152 | tf_op jit(solution)/shard_map/ppermute | solution.py:42
  167.1 1.4 collective-permute-start.32
  168.5 0.2 collective-permute-done.33
  168.7 2.6 %collective-permute-done.32 = f32[1,512]{1,0:T(1,128)S(1)} collective-permute-done((f32[1,512]{1,0:T(1,128)}, f32[1,512]{1,0:T(1,128)S(1)}, u32[]{:S(2)}, u32[]{:S(2)}) %collective-permute-start.32) | collective-permute-done | bytes 2080 | tf_op jit(solution)/shard_map/ppermute | solution.py:42
  171.2 0.7 add_rsqrt_fusion
  172.0 3.3 %fusion = bf16[512,1344]{0,1:T(8,128)(2,1)} fusion(f32[1344,512]{1,0:T(8,128)} %get-tuple-element.37, f32[512]{0:T(512)S(1)} %bitcast.27, f32[1344]{0:T(1024)S(1)} %copy-done.25, bf16[512,1344]{0,1:T(8,128)(2,1)S(1)} %copy-done), kind=kLoop, calls=%fused_computation.1 | loop fusion | flops 3440640 | bytes 5512448 | tf_op jit(solution)/shard_map/transpose | solution.py:577
  (87 shorter events, 0.8 us)
Async XLA Ops:
  0.0 5.9 %copy-start.24 = (f32[5376]{0:T(1024)S(1)}, f32[5376]{0:T(1024)}, u32[]{:S(2)}) copy-start(f32[5376]{0:T(1024)} %param.12) | copy-start | bytes 64516
  0.0 7.2 %collective-permute-start.2 = (bf16[1344,512]{1,0:T(8,128)(2,1)}, bf16[1344,512]{1,0:T(8,128)(2,1)S(1)}, u32[]{:S(2)}, u32[]{:S(2)}) collective-permute-start(bf16[1344,512]{1,0:T(8,128)(2,1)} %bitcast.20), channel_id=1, source_target_pairs={{0,1},{1,0},{2,3},{3,2},{4,5},{5,4},{6,7},{7,6},{8,9},{9,8},{10,11... | collective-permute-start | bytes 4128776 | tf_op jit(solution)/shard_map/ppermute | solution.py:42
  2.8 18.7 %collective-permute-start = (bf16[1344,256]{1,0:T(8,128)(2,1)S(1)}, bf16[1344,256]{1,0:T(8,128)(2,1)S(1)}, u32[]{:S(2)}, u32[]{:S(2)}) collective-permute-start(bf16[1344,256]{1,0:T(8,128)(2,1)S(1)} %get-tuple-element.40), channel_id=1, source_target_pairs={{0,2},{1,3},{2,0},{3,1},{4,6},{5,7},{6,4},{7,5},{8,10},{9,11},{10,... | collective-permute-start | bytes 2064392 | tf_op jit(solution)/shard_map/ppermute | solution.py:42
  7.2 17.2 %copy-start.26 = (s32[4]{0:T(128)S(1)}, s32[4]{0:T(128)}, u32[]{:S(2)}) copy-start(s32[4]{0:T(128)} %ids.7) | copy-start | bytes 52
  7.2 17.9 %copy-start.27 = (s32[8]{0:T(128)S(1)}, s32[8]{0:T(128)}, u32[]{:S(2)}) copy-start(s32[8]{0:T(128)} %lengths.7) | copy-start | bytes 100
  7.2 1.1 copy-start.1
  21.5 27.7 %copy-start.16 = (bf16[1344,256]{1,0:T(8,128)(2,1)}, bf16[1344,256]{1,0:T(8,128)(2,1)S(1)}, u32[]{:S(2)}) copy-start(bf16[1344,256]{1,0:T(8,128)(2,1)S(1)} %collective-permute-done.x0) | copy-start | bytes 2064388
  21.5 22.3 %collective-permute-start.3 = (bf16[1344,256]{1,0:T(8,128)(2,1)S(1)}, bf16[1344,256]{1,0:T(8,128)(2,1)S(1)}, u32[]{:S(2)}, u32[]{:S(2)}) collective-permute-start(bf16[1344,256]{1,0:T(8,128)(2,1)S(1)} %get-tuple-element.26), channel_id=1, source_target_pairs={{0,2},{1,3},{2,0},{3,1},{4,6},{5,7},{6,4},{7,5},{8,10},{9,11},{10,... | collective-permute-start | bytes 2064392 | tf_op jit(solution)/shard_map/ppermute | solution.py:42
  31.5 11.6 %collective-permute-start.11 = (bf16[128,512]{1,0:T(8,128)(2,1)}, bf16[128,512]{1,0:T(8,128)(2,1)S(1)}, u32[]{:S(2)}, u32[]{:S(2)}) collective-permute-start(bf16[128,512]{1,0:T(8,128)(2,1)} %get-tuple-element.31), channel_id=1, source_target_pairs={{0,96},{4,100},{8,104},{12,108},{16,112},{20,116},{24,120},{28,124... | collective-permute-start | bytes 393224 | tf_op jit(solution)/shard_map/ppermute | solution.py:56
  34.0 15.2 %collective-permute-start.1 = (bf16[1344,256]{1,0:T(8,128)(2,1)S(1)}, bf16[1344,256]{1,0:T(8,128)(2,1)}, u32[]{:S(2)}, u32[]{:S(2)}) collective-permute-start(bf16[1344,256]{1,0:T(8,128)(2,1)S(1)} %collective-permute-done.x0), channel_id=1, source_target_pairs={{0,1},{1,0},{2,3},{3,2},{4,5},{5,4},{6,7},{7,6},{8,9},{9,8},{10,11... | collective-permute-start | bytes 2064392 | tf_op jit(solution)/shard_map/ppermute | solution.py:42
  35.4 8.6 %collective-permute-start.10 = (bf16[128,512]{1,0:T(8,128)(2,1)}, bf16[128,512]{1,0:T(8,128)(2,1)S(1)}, u32[]{:S(2)}, u32[]{:S(2)}) collective-permute-start(bf16[128,512]{1,0:T(8,128)(2,1)} %get-tuple-element.30), channel_id=1, source_target_pairs={{0,64},{4,68},{8,72},{12,76},{16,80},{20,84},{24,88},{28,92},{32,9... | collective-permute-start | bytes 393224 | tf_op jit(solution)/shard_map/ppermute | solution.py:56
  35.9 9.4 %collective-permute-start.9 = (bf16[128,512]{1,0:T(8,128)(2,1)}, bf16[128,512]{1,0:T(8,128)(2,1)S(1)}, u32[]{:S(2)}, u32[]{:S(2)}) collective-permute-start(bf16[128,512]{1,0:T(8,128)(2,1)} %get-tuple-element.29), channel_id=1, source_target_pairs={{0,32},{4,36},{8,40},{12,44},{16,48},{20,52},{24,56},{28,60},{32,6... | collective-permute-start | bytes 393224 | tf_op jit(solution)/shard_map/ppermute | solution.py:56
  36.5 9.5 %copy-start.21 = (bf16[128,512]{1,0:T(8,128)(2,1)S(1)}, bf16[128,512]{1,0:T(8,128)(2,1)}, u32[]{:S(2)}) copy-start(bf16[128,512]{1,0:T(8,128)(2,1)} %get-tuple-element.28) | copy-start | bytes 393220
  43.1 82.2 %collective-permute-start.22 = (bf16[1344,512]{1,0:T(8,128)(2,1)}, bf16[1344,512]{1,0:T(8,128)(2,1)S(1)}, u32[]{:S(2)}, u32[]{:S(2)}) collective-permute-start(bf16[1344,512]{1,0:T(8,128)(2,1)} %get-tuple-element.34), channel_id=1, source_target_pairs={{0,1},{1,0},{2,3},{3,2},{4,5},{5,4},{6,7},{7,6},{8,9},{9,8},{10,11... | collective-permute-start | bytes 4128776 | tf_op jit(solution)/shard_map/ppermute | solution.py:42
  43.8 12.9 %copy-start.13 = (bf16[1344,256]{1,0:T(8,128)(2,1)}, bf16[1344,256]{1,0:T(8,128)(2,1)S(1)}, u32[]{:S(2)}) copy-start(bf16[1344,256]{1,0:T(8,128)(2,1)S(1)} %collective-permute-done.3.x0) | copy-start | bytes 2064388
  43.8 20.4 %collective-permute-start.4 = (bf16[1344,256]{1,0:T(8,128)(2,1)S(1)}, bf16[1344,256]{1,0:T(8,128)(2,1)}, u32[]{:S(2)}, u32[]{:S(2)}) collective-permute-start(bf16[1344,256]{1,0:T(8,128)(2,1)S(1)} %collective-permute-done.3.x0), channel_id=1, source_target_pairs={{0,1},{1,0},{2,3},{3,2},{4,5},{5,4},{6,7},{7,6},{8,9},{9,8},{10,11... | collective-permute-start | bytes 2064392 | tf_op jit(solution)/shard_map/ppermute | solution.py:42
  43.9 20.3 %collective-permute-start.24 = (bf16[336,128]{1,0:T(8,128)(2,1)}, bf16[336,128]{1,0:T(8,128)(2,1)S(1)}, u32[]{:S(2)}, u32[]{:S(2)}) collective-permute-start(bf16[336,128]{1,0:T(8,128)(2,1)} %get-tuple-element.36), channel_id=1, source_target_pairs={{0,3},{1,2},{2,1},{3,0},{4,7},{5,6},{6,5},{7,4},{8,11},{9,10},{10,... | collective-permute-start | bytes 258056 | tf_op jit(solution)/shard_map/ppermute | solution.py:42
  45.3 0.7 copy-start.22
  46.9 9.8 %copy-start.17 = (bf16[128,512]{1,0:T(8,128)(2,1)}, bf16[128,512]{1,0:T(8,128)(2,1)S(1)}, u32[]{:S(2)}) copy-start(bf16[128,512]{1,0:T(8,128)(2,1)S(1)} %add_add_fusion.mine) | copy-start | bytes 393220
  46.9 11.5 %collective-permute-start.12 = (bf16[128,512]{1,0:T(8,128)(2,1)S(1)}, bf16[128,512]{1,0:T(8,128)(2,1)S(1)}, u32[]{:S(2)}, u32[]{:S(2)}) collective-permute-start(bf16[128,512]{1,0:T(8,128)(2,1)S(1)} %add_add_fusion.mine), channel_id=1, source_target_pairs={{0,16},{4,20},{8,24},{12,28},{16,0},{20,4},{24,8},{28,12},{32,48},... | collective-permute-start | bytes 393224 | tf_op jit(solution)/shard_map/ppermute | solution.py:71
  49.2 15.0 %copy-start.28 = (bf16[336,128]{1,0:T(8,128)(2,1)S(1)}, bf16[336,128]{1,0:T(8,128)(2,1)}, u32[]{:S(2)}) copy-start(bf16[336,128]{1,0:T(8,128)(2,1)} %get-tuple-element.35) | copy-start | bytes 258052
  56.7 19.5 %collective-permute-start.5 = (bf16[256,512]{1,0:T(8,128)(2,1)}, bf16[256,512]{1,0:T(8,128)(2,1)S(1)}, u32[]{:S(2)}, u32[]{:S(2)}) collective-permute-start(bf16[256,512]{1,0:T(8,128)(2,1)} %get-tuple-element.25.gate.own_a), channel_id=1, source_target_pairs={{0,4},{4,8},{8,12},{12,16},{16,20},{20,24},{24,28},{28,0},{32,36},... | collective-permute-start | bytes 786440 | tf_op jit(solution)/shard_map/ppermute | solution.py:84
  58.5 3.3 %copy-start.23 = (bf16[128,512]{1,0:T(8,128)(2,1)}, bf16[128,512]{1,0:T(8,128)(2,1)S(1)}, u32[]{:S(2)}) copy-start(bf16[128,512]{1,0:T(8,128)(2,1)S(1)} %collective-permute-done.12.twin) | copy-start | bytes 393220
  58.5 22.1 %collective-permute-start.7 = (bf16[256,512]{1,0:T(8,128)(2,1)}, bf16[256,512]{1,0:T(8,128)(2,1)S(1)}, u32[]{:S(2)}, u32[]{:S(2)}) collective-permute-start(bf16[256,512]{1,0:T(8,128)(2,1)} %get-tuple-element.25.gate.own_a), channel_id=1, source_target_pairs={{0,8},{4,12},{8,16},{12,20},{16,24},{20,28},{24,0},{28,4},{32,40},... | collective-permute-start | bytes 786440 | tf_op jit(solution)/shard_map/ppermute | solution.py:84
  64.2 16.9 %collective-permute-start.13 = (bf16[2,128,512]{2,1,0:T(8,128)(2,1)}, bf16[2,128,512]{2,1,0:T(8,128)(2,1)S(1)}, u32[]{:S(2)}, u32[]{:S(2)}) collective-permute-start(bf16[2,128,512]{2,1,0:T(8,128)(2,1)} %shard_map.113.refs_0_), channel_id=1, source_target_pairs={{0,4},{4,0},{8,12},{12,8},{16,20},{20,16},{24,28},{28,24},{32,36},... | collective-permute-start | bytes 786440 | tf_op jit(solution)/shard_map/ppermute | solution.py:75
  64.2 9.9 %copy-start.3 = (bf16[2,128,512]{2,1,0:T(8,128)(2,1)S(1)}, bf16[2,128,512]{2,1,0:T(8,128)(2,1)}, u32[]{:S(2)}) copy-start(bf16[2,128,512]{2,1,0:T(8,128)(2,1)} %shard_map.113.refs_0_) | copy-start | bytes 786436
  64.2 9.9 %collective-permute-start.23 = (bf16[336,128]{1,0:T(8,128)(2,1)S(1)}, bf16[336,128]{1,0:T(8,128)(2,1)S(1)}, u32[]{:S(2)}, u32[]{:S(2)}) collective-permute-start(bf16[336,128]{1,0:T(8,128)(2,1)S(1)} %copy-done.28), channel_id=1, source_target_pairs={{0,2},{1,3},{2,0},{3,1},{4,6},{5,7},{6,4},{7,5},{8,10},{9,11},{10,... | collective-permute-start | bytes 258056 | tf_op jit(solution)/shard_map/ppermute | solution.py:42
  74.1 10.6 %collective-permute-start.14 = (bf16[2,128,512]{2,1,0:T(8,128)(2,1)S(1)}, bf16[2,128,512]{2,1,0:T(8,128)(2,1)S(1)}, u32[]{:S(2)}, u32[]{:S(2)}) collective-permute-start(bf16[2,128,512]{2,1,0:T(8,128)(2,1)S(1)} %copy-done.3), channel_id=1, source_target_pairs={{0,8},{4,12},{8,0},{12,4},{16,24},{20,28},{24,16},{28,20},{32,40},... | collective-permute-start | bytes 786440 | tf_op jit(solution)/shard_map/ppermute | solution.py:75
  76.3 26.3 %copy-start.6 = (bf16[256,512]{1,0:T(8,128)(2,1)}, bf16[256,512]{1,0:T(8,128)(2,1)S(1)}, u32[]{:S(2)}) copy-start(bf16[256,512]{1,0:T(8,128)(2,1)S(1)} %collective-permute-done.5.one_a) | copy-start | bytes 786436
  76.3 26.1 %collective-permute-start.15 = (bf16[2,128,512]{2,1,0:T(8,128)(2,1)S(1)}, bf16[2,128,512]{2,1,0:T(8,128)(2,1)S(1)}, u32[]{:S(2)}, u32[]{:S(2)}) collective-permute-start(bf16[2,128,512]{2,1,0:T(8,128)(2,1)S(1)} %copy-done.3), channel_id=1, source_target_pairs={{0,12},{4,8},{8,4},{12,0},{16,28},{20,24},{24,20},{28,16},{32,44},... | collective-permute-start | bytes 786440 | tf_op jit(solution)/shard_map/ppermute | solution.py:75
  80.6 22.0 %copy-start.7 = (bf16[256,512]{1,0:T(8,128)(2,1)}, bf16[256,512]{1,0:T(8,128)(2,1)S(1)}, u32[]{:S(2)}) copy-start(bf16[256,512]{1,0:T(8,128)(2,1)S(1)} %collective-permute-done.7.two_a) | copy-start | bytes 786436
  80.6 21.9 %collective-permute-start.6 = (bf16[256,512]{1,0:T(8,128)(2,1)}, bf16[256,512]{1,0:T(8,128)(2,1)S(1)}, u32[]{:S(2)}, u32[]{:S(2)}) collective-permute-start(bf16[256,512]{1,0:T(8,128)(2,1)} %get-tuple-element.27.own_b), channel_id=1, source_target_pairs={{0,4},{4,8},{8,12},{12,16},{16,20},{20,24},{24,28},{28,0},{32,36},... | collective-permute-start | bytes 786440 | tf_op jit(solution)/shard_map/ppermute | solution.py:84
  81.1 21.4 %copy-start.8 = (bf16[2,128,512]{2,1,0:T(8,128)(2,1)}, bf16[2,128,512]{2,1,0:T(8,128)(2,1)S(1)}, u32[]{:S(2)}) copy-start(bf16[2,128,512]{2,1,0:T(8,128)(2,1)S(1)} %collective-permute-done.13.refs_1_) | copy-start | bytes 786436
  81.1 21.4 %collective-permute-start.8 = (bf16[256,512]{1,0:T(8,128)(2,1)}, bf16[256,512]{1,0:T(8,128)(2,1)S(1)}, u32[]{:S(2)}, u32[]{:S(2)}) collective-permute-start(bf16[256,512]{1,0:T(8,128)(2,1)} %get-tuple-element.27.own_b), channel_id=1, source_target_pairs={{0,8},{4,12},{8,16},{12,20},{16,24},{20,28},{24,0},{28,4},{32,40},... | collective-permute-start | bytes 786440 | tf_op jit(solution)/shard_map/ppermute | solution.py:84
  84.8 17.8 %copy-start.9 = (bf16[2,128,512]{2,1,0:T(8,128)(2,1)}, bf16[2,128,512]{2,1,0:T(8,128)(2,1)S(1)}, u32[]{:S(2)}) copy-start(bf16[2,128,512]{2,1,0:T(8,128)(2,1)S(1)} %collective-permute-done.14.refs_2_) | copy-start | bytes 786436
  84.8 33.2 %collective-permute-start.27 = (bf16[2,336,128]{2,1,0:T(8,128)(2,1)S(1)}, bf16[2,336,128]{2,1,0:T(8,128)(2,1)S(1)}, u32[]{:S(2)}, u32[]{:S(2)}) collective-permute-start(bf16[2,336,128]{2,1,0:T(8,128)(2,1)S(1)} %get-tuple-element.42), channel_id=1, source_target_pairs={{0,12},{4,0},{8,4},{12,8},{16,28},{20,16},{24,20},{28,24},{32,44},... | collective-permute-start | bytes 516104 | tf_op jit(solution)/shard_map/ppermute | solution.py:66
  102.4 0.7 copy-start.10
  102.4 18.6 %collective-permute-start.26 = (bf16[2,336,128]{2,1,0:T(8,128)(2,1)S(1)}, bf16[2,336,128]{2,1,0:T(8,128)(2,1)S(1)}, u32[]{:S(2)}, u32[]{:S(2)}) collective-permute-start(bf16[2,336,128]{2,1,0:T(8,128)(2,1)S(1)} %get-tuple-element.42), channel_id=1, source_target_pairs={{0,8},{4,12},{8,0},{12,4},{16,24},{20,28},{24,16},{28,20},{32,40},... | collective-permute-start | bytes 516104 | tf_op jit(solution)/shard_map/ppermute | solution.py:66
  102.4 0.8 copy-start.11
  102.5 18.6 %collective-permute-start.25 = (bf16[2,336,128]{2,1,0:T(8,128)(2,1)S(1)}, bf16[2,336,128]{2,1,0:T(8,128)(2,1)}, u32[]{:S(2)}, u32[]{:S(2)}) collective-permute-start(bf16[2,336,128]{2,1,0:T(8,128)(2,1)S(1)} %get-tuple-element.42), channel_id=1, source_target_pairs={{0,4},{4,8},{8,12},{12,0},{16,20},{20,24},{24,28},{28,16},{32,36},... | collective-permute-start | bytes 516104 | tf_op jit(solution)/shard_map/ppermute | solution.py:66
  102.5 0.8 copy-start.12
  110.5 15.4 %copy-start.5 = (bf16[256,512]{1,0:T(8,128)(2,1)S(1)}, bf16[256,512]{1,0:T(8,128)(2,1)}, u32[]{:S(2)}) copy-start(bf16[256,512]{1,0:T(8,128)(2,1)} %shard_map.114.c0a) | copy-start | bytes 786436
  110.5 15.4 %collective-permute-start.16 = (bf16[256,512]{1,0:T(8,128)(2,1)}, bf16[256,512]{1,0:T(8,128)(2,1)}, u32[]{:S(2)}, u32[]{:S(2)}) collective-permute-start(bf16[256,512]{1,0:T(8,128)(2,1)} %shard_map.114.c0a), channel_id=1, source_target_pairs={{0,2},{1,3},{2,0},{3,1},{4,6},{5,7},{6,4},{7,5},{8,10},{9,11},{10,... | collective-permute-start | bytes 786440 | tf_op jit(solution)/shard_map/ppermute | solution.py:42
  118.0 3.1 %copy-start.20 = (bf16[2,336,128]{2,1,0:T(8,128)(2,1)}, bf16[2,336,128]{2,1,0:T(8,128)(2,1)S(1)}, u32[]{:S(2)}) copy-start(bf16[2,336,128]{2,1,0:T(8,128)(2,1)S(1)} %collective-permute-done.27) | copy-start | bytes 516100
  118.0 9.7 %collective-permute-start.17 = (bf16[256,512]{1,0:T(8,128)(2,1)}, bf16[256,512]{1,0:T(8,128)(2,1)}, u32[]{:S(2)}, u32[]{:S(2)}) collective-permute-start(bf16[256,512]{1,0:T(8,128)(2,1)} %shard_map.115.c0b), channel_id=1, source_target_pairs={{0,2},{1,3},{2,0},{3,1},{4,6},{5,7},{6,4},{7,5},{8,10},{9,11},{10,... | collective-permute-start | bytes 786440 | tf_op jit(solution)/shard_map/ppermute | solution.py:42
  122.2 13.8 %copy-start.2 = (bf16[4,2,336,128]{3,2,1,0:T(8,128)(2,1)}, bf16[4,2,336,128]{3,2,1,0:T(8,128)(2,1)S(1)}, u32[]{:S(2)}) copy-start(bf16[4,2,336,128]{3,2,1,0:T(8,128)(2,1)S(1)} %pad_maximum_fusion.p0) | copy-start | bytes 2064388
  122.2 17.0 %collective-permute-start.28 = (bf16[4,2,336,128]{3,2,1,0:T(8,128)(2,1)S(1)}, bf16[4,2,336,128]{3,2,1,0:T(8,128)(2,1)S(1)}, u32[]{:S(2)}, u32[]{:S(2)}) collective-permute-start(bf16[4,2,336,128]{3,2,1,0:T(8,128)(2,1)S(1)} %pad_maximum_fusion.p0), channel_id=1, source_target_pairs={{0,32},{4,36},{8,40},{12,44},{16,48},{20,52},{24,56},{28,60},{32,6... | collective-permute-start | bytes 2064392 | tf_op jit(solution)/shard_map/ppermute | solution.py:56
  123.4 30.9 %collective-permute-start.29 = (bf16[4,2,336,128]{3,2,1,0:T(8,128)(2,1)S(1)}, bf16[4,2,336,128]{3,2,1,0:T(8,128)(2,1)S(1)}, u32[]{:S(2)}, u32[]{:S(2)}) collective-permute-start(bf16[4,2,336,128]{3,2,1,0:T(8,128)(2,1)S(1)} %pad_maximum_fusion.p0), channel_id=1, source_target_pairs={{0,64},{4,68},{8,72},{12,76},{16,80},{20,84},{24,88},{28,92},{32,9... | collective-permute-start | bytes 2064392 | tf_op jit(solution)/shard_map/ppermute | solution.py:56
  125.3 5.2 %copy-start.4 = (bf16[1344,512]{1,0:T(8,128)(2,1)}, bf16[1344,512]{1,0:T(8,128)(2,1)S(1)}, u32[]{:S(2)}) copy-start(bf16[1344,512]{1,0:T(8,128)(2,1)S(1)} %collective-permute-done.22.w1) | copy-start | bytes 4128772
  125.3 29.8 %collective-permute-start.30 = (bf16[4,2,336,128]{3,2,1,0:T(8,128)(2,1)S(1)}, bf16[4,2,336,128]{3,2,1,0:T(8,128)(2,1)}, u32[]{:S(2)}, u32[]{:S(2)}) collective-permute-start(bf16[4,2,336,128]{3,2,1,0:T(8,128)(2,1)S(1)} %pad_maximum_fusion.p0), channel_id=1, source_target_pairs={{0,96},{4,100},{8,104},{12,108},{16,112},{20,116},{24,120},{28,124... | collective-permute-start | bytes 2064392 | tf_op jit(solution)/shard_map/ppermute | solution.py:56
  125.9 3.1 %collective-permute-start.20 = (bf16[256,512]{1,0:T(8,128)(2,1)S(1)}, bf16[256,512]{1,0:T(8,128)(2,1)S(1)}, u32[]{:S(2)}, u32[]{:S(2)}) collective-permute-start(bf16[256,512]{1,0:T(8,128)(2,1)S(1)} %copy-done.5), channel_id=1, source_target_pairs={{0,1},{1,0},{2,3},{3,2},{4,5},{5,4},{6,7},{7,6},{8,9},{9,8},{10,11... | collective-permute-start | bytes 786440 | tf_op jit(solution)/shard_map/ppermute | solution.py:42
  127.7 2.4 %collective-permute-start.21 = (bf16[256,512]{1,0:T(8,128)(2,1)}, bf16[256,512]{1,0:T(8,128)(2,1)}, u32[]{:S(2)}, u32[]{:S(2)}) collective-permute-start(bf16[256,512]{1,0:T(8,128)(2,1)} %shard_map.115.c0b), channel_id=1, source_target_pairs={{0,1},{1,0},{2,3},{3,2},{4,5},{5,4},{6,7},{7,6},{8,9},{9,8},{10,11... | collective-permute-start | bytes 786440 | tf_op jit(solution)/shard_map/ppermute | solution.py:42
  128.9 1.6 copy-start.18
  128.9 26.2 %collective-permute-start.18 = (bf16[256,512]{1,0:T(8,128)(2,1)}, bf16[256,512]{1,0:T(8,128)(2,1)S(1)}, u32[]{:S(2)}, u32[]{:S(2)}) collective-permute-start(bf16[256,512]{1,0:T(8,128)(2,1)} %collective-permute-done.16.c0a), channel_id=1, source_target_pairs={{0,1},{1,0},{2,3},{3,2},{4,5},{5,4},{6,7},{7,6},{8,9},{9,8},{10,11... | collective-permute-start | bytes 786440 | tf_op jit(solution)/shard_map/ppermute | solution.py:42
  130.2 25.0 %collective-permute-start.19 = (bf16[256,512]{1,0:T(8,128)(2,1)}, bf16[256,512]{1,0:T(8,128)(2,1)}, u32[]{:S(2)}, u32[]{:S(2)}) collective-permute-start(bf16[256,512]{1,0:T(8,128)(2,1)} %collective-permute-done.17.c0b), channel_id=1, source_target_pairs={{0,1},{1,0},{2,3},{3,2},{4,5},{5,4},{6,7},{7,6},{8,9},{9,8},{10,11... | collective-permute-start | bytes 786440 | tf_op jit(solution)/shard_map/ppermute | solution.py:42
  135.9 36.0 %copy-start = (bf16[512,1344]{0,1:T(8,128)(2,1)S(1)}, bf16[512,1344]{0,1:T(8,128)(2,1)}, u32[]{:S(2)}) copy-start(bf16[512,1344]{0,1:T(8,128)(2,1)} %param.11) | copy-start | bytes 4128772
  135.9 36.0 %copy-start.25 = (f32[1344]{0:T(1024)S(1)}, f32[1344]{0:T(1024)}, u32[]{:S(2)}) copy-start(f32[1344]{0:T(1024)} %param.17) | copy-start | bytes 16132
  139.2 16.0 %copy-start.14 = (bf16[4,2,336,128]{3,2,1,0:T(8,128)(2,1)}, bf16[4,2,336,128]{3,2,1,0:T(8,128)(2,1)S(1)}, u32[]{:S(2)}) copy-start(bf16[4,2,336,128]{3,2,1,0:T(8,128)(2,1)S(1)} %collective-permute-done.28.p1) | copy-start | bytes 2064388
  154.3 0.9 copy-start.15
  155.1 0.7 copy-start.19
  163.9 4.8 %collective-permute-start.33 = (f32[1,512]{1,0:T(1,128)}, f32[1,512]{1,0:T(1,128)S(1)}, u32[]{:S(2)}, u32[]{:S(2)}) collective-permute-start(f32[1,512]{1,0:T(1,128)} %get-tuple-element.38), channel_id=1, source_target_pairs={{0,3},{1,2},{2,1},{3,0},{4,7},{5,6},{6,5},{7,4},{8,11},{9,10},{10,... | collective-permute-start | bytes 6152 | tf_op jit(solution)/shard_map/ppermute | solution.py:42
  167.1 4.2 %collective-permute-start.32 = (f32[1,512]{1,0:T(1,128)}, f32[1,512]{1,0:T(1,128)S(1)}, u32[]{:S(2)}, u32[]{:S(2)}) collective-permute-start(f32[1,512]{1,0:T(1,128)} %get-tuple-element.38), channel_id=1, source_target_pairs={{0,2},{1,3},{2,0},{3,1},{4,6},{5,7},{6,4},{7,5},{8,10},{9,11},{10,... | collective-permute-start | bytes 6152 | tf_op jit(solution)/shard_map/ppermute | solution.py:42
  168.5 2.8 %collective-permute-start.31 = (f32[1,512]{1,0:T(1,128)}, f32[1,512]{1,0:T(1,128)S(1)}, u32[]{:S(2)}, u32[]{:S(2)}) collective-permute-start(f32[1,512]{1,0:T(1,128)} %get-tuple-element.38), channel_id=1, source_target_pairs={{0,1},{1,0},{2,3},{3,2},{4,5},{5,4},{6,7},{7,6},{8,9},{9,8},{10,11... | collective-permute-start | bytes 6152 | tf_op jit(solution)/shard_map/ppermute | solution.py:42

commit v3 on v1

v3 whole, which is shorter than its diff:
```python
import functools

import jax
import jax.numpy as jnp
from jax import lax
from jax.experimental import pallas as pl
from jax.experimental.pallas import tpu as pltpu
from jax.sharding import PartitionSpec as P

HEAD_DIM = 128
WINDOW = 1024
DOCS = 4
MP = 4
ROWS = 512
HALF = 256
FEATURES = 1344
STEP = 672
HEADS_LOCAL = 4
KV_WIDTH = 256
PAIR = 2 * KV_WIDTH
DOC_SHARDS = 8
HELD = 128
STRIP = FEATURES // 4
VMEM_LIMIT = 63 * 1024 * 1024

epsilon = 1e-06
query_scalar = 168.0
rope_base = 10000.0
F32 = jnp.float32
BF16 = jnp.bfloat16


def cost(flops, moved, exps=0):
    return pl.CostEstimate(flops=flops, bytes_accessed=moved, transcendentals=exps)


def params():
    return pltpu.CompilerParams(vmem_limit_bytes=VMEM_LIMIT)


def across_mp(array, flip):
    return lax.ppermute(array, "mp", [(i, i ^ flip) for i in range(MP)])


def seq_place(x, y_lo, z):
    return x * 8 + y_lo * 4 + z


def along_x(array, by):
    pairs = [
        (seq_place(x, y, z), seq_place((x + by) % 4, y, z))
        for x in range(4)
        for y in range(2)
        for z in range(4)
    ]
    return lax.ppermute(array, "seq", pairs)


def along_z(array, by):
    pairs = [
        (seq_place(x, y, z), seq_place(x, y, (z + by) % 4))
        for x in range(4)
        for y in range(2)
        for z in range(4)
    ]
    return lax.ppermute(array, "seq", pairs)


def to_twin(array):
    pairs = [(i, i ^ 4) for i in range(DOCS * DOC_SHARDS)]
    return lax.ppermute(array, "seq", pairs)


def z_flip(array, flip):
    return lax.ppermute(array, "seq", [(i, i ^ flip) for i in range(DOCS * DOC_SHARDS)])


def within_doc(array, by):
    pairs = [
        (d * DOC_SHARDS + i, d * DOC_SHARDS + (i + by) % DOC_SHARDS)
        for d in range(DOCS)
        for i in range(DOC_SHARDS)
    ]
    return lax.ppermute(array, "seq", pairs)


def after(array, *others):
    return lax.optimization_barrier((array, *others))[0]


TN = (((0,), (0,)), ((), ()))
NT = (((1,), (1,)), ((), ()))


IN_HBM = pl.BlockSpec(memory_space=pltpu.HBM)


def project_kernel(chunks, first, last, order, *refs):
    step = pl.program_id(0)
    xs, refs = refs[:chunks], refs[chunks:]
    gain, wq, wk, wv = refs[:4]
    if last:
        acc_in, squares_in, cosine, sine, q_ref, kv_ref, acc, squares = refs[-8:]
    elif first:
        acc, squares = refs[-2:]
    else:
        acc_in, squares_in, acc, squares = refs[-4:]

    for number in range(chunks):

        @pl.when(step // 2 == number)
        def _(number=number):
            x = jnp.transpose(xs[number][...]).astype(F32)
            scaled = (x * gain[0]).astype(BF16)
            parts = (
                jnp.dot(scaled, wq[...], preferred_element_type=F32),
                jnp.dot(scaled, wk[...], preferred_element_type=F32),
                jnp.dot(scaled, wv[...], preferred_element_type=F32),
                jnp.broadcast_to(jnp.sum(x * x, 1, keepdims=True), squares.shape),
            )

            def put(sources):
                at = 0
                for part, source in zip(parts[:3], sources):
                    cols = slice(at, at + part.shape[1])
                    acc[:, cols] = part if source is None else source[:, cols] + part
                    at = cols.stop
                squares[...] = parts[3] if sources[3] is None else sources[3][...] + parts[3]

            if number:
                put((acc, acc, acc, squares))
            else:

                @pl.when(step == 0)
                def _():
                    put((None,) * 4 if first else (acc_in, acc_in, acc_in, squares_in))

                @pl.when(step == 1)
                def _():
                    put((acc, acc, acc, squares))

    if last:

        @pl.when(step == 2 * chunks - 1)
        def _():
            scale = lax.rsqrt(squares[...] * (1.0 / (MP * FEATURES)) + epsilon)
            cos_all = cosine[...]
            sin_all = sine[...]
            for head in range(6):
                cols = slice(head * HEAD_DIM, (head + 1) * HEAD_DIM)
                part = acc[:, cols] * scale
                turned = part * cos_all + pltpu.roll(part, 64, 1) * sin_all
                if head < HEADS_LOCAL:
                    q_ref[:, cols] = (turned * query_scalar ** (-0.5)).astype(BF16)
                else:
                    at = (head - HEADS_LOCAL) * HEAD_DIM
                    kv_ref[:, at : at + HEAD_DIM] = turned.astype(BF16)
            for head in range(2):
                at = KV_WIDTH + head * HEAD_DIM
                part = acc[:, 768 + head * HEAD_DIM : 896 + head * HEAD_DIM] * scale
                kv_ref[:, at : at + HEAD_DIM] = part.astype(BF16)


def project(order, start, xs, gain, weights, gates=(), carried=(), tables=()):
    chunks = len(xs)
    full = lambda shape: pl.BlockSpec(shape, lambda i, order: (0,) * len(shape))
    at = lambda i, order: order[5 + start + i // 2] * 2 + i % 2
    acc_shapes = [(ROWS, 1024), (ROWS, HEAD_DIM)]
    if tables:
        out_shape = [jax.ShapeDtypeStruct((ROWS, 512), BF16)] * 2
        scratch = [pltpu.VMEM(shape, F32) for shape in acc_shapes]
    else:
        out_shape = [jax.ShapeDtypeStruct(shape, F32) for shape in acc_shapes]
        scratch = []
    return pl.pallas_call(
        functools.partial(project_kernel, chunks, not carried, bool(tables)),
        grid_spec=pltpu.PrefetchScalarGridSpec(
            num_scalar_prefetch=1,
            grid=(2 * chunks,),
            in_specs=[
                pl.BlockSpec((STEP, ROWS), lambda i, order, k=k: (jnp.clip(i - 2 * k, 0, 1), 0))
                for k in range(chunks)
            ]
            + [pl.BlockSpec((1, 1, STEP), lambda i, order: (at(i, order), 0, 0))]
            + [
                pl.BlockSpec((STEP, width), lambda i, order: (at(i, order), 0))
                for width in (512, 256, 256)
            ]
            + [IN_HBM] * len(gates)
            + [full(one.shape) for one in (*carried, *tables)],
            out_specs=[full(one.shape) for one in out_shape],
            scratch_shapes=scratch,
        ),
        out_shape=out_shape,
        compiler_params=params(),
        cost_estimate=cost(6_000_000_000, 20_000_000) if tables else cost(1, 1),
    )(order, *xs, gain, *weights, *gates, *carried, *tables)


def attention_kernel(where, ids, lengths, reals, q_ref, own, one_back, two_back, *refs):
    prefix, twin, _, _, _, out, held, lines, sems = refs
    local = where[2]
    length = lengths[ids[where[1]]]
    real = reals[where[1]]

    def fetch(pairs):
        copies = [pltpu.make_async_copy(a, b, sems.at[i]) for i, (a, b) in enumerate(pairs)]
        for one in copies:
            one.start()
        for one in copies:
            one.wait()

    def fetch_prefix():
        fetch(
            [
                (
                    source.at[r],
                    lines.at[side, pl.ds(pl.multiple_of((where[3] ^ r) * HELD, HELD), HELD)],
                )
                for side, source in enumerate((prefix, twin))
                for r in range(4)
            ]
        )

    def picked(late_part):
        row = lax.broadcasted_iota(jnp.int32, (ROWS, 1), 0)
        late = ((row - length) & (WINDOW - 1)) >= ROWS
        low = lines[0].astype(F32)
        high = lines[1].astype(F32)
        return (jnp.where(late, low, high) if late_part else jnp.where(late, high, low)).astype(
            BF16
        )

    @pl.when(local == 0)
    def _():
        fetch_prefix()
        held[:ROWS] = picked(False)
        held[ROWS:] = picked(True)

    @pl.when(local == 1)
    def _():
        fetch_prefix()
        held[:ROWS] = picked(True)
        fetch([(one_back, held.at[pl.ds(ROWS, ROWS)])])

    @pl.when(local >= 2)
    def _():
        fetch([(two_back, held.at[pl.ds(0, ROWS)]), (one_back, held.at[pl.ds(ROWS, ROWS)])])

    column = lax.broadcasted_iota(jnp.int32, (1, ROWS), 1)
    shift_two = jnp.where(local < 2, length, 0)
    limit_two = jnp.where(local < 2, WINDOW - ROWS * local - length, 0)
    shift_one = jnp.where(local < 1, length, 0)
    limit_one = jnp.where(local < 1, ROWS - length, 0)
    place_two = (column - shift_two) & (ROWS - 1)
    place_one = (column - shift_one) & (ROWS - 1)
    one_ok = place_one >= limit_one
    for half in range(2):
        mine = slice(half * HALF, (half + 1) * HALF)
        row = half * HALF + (lax.broadcasted_iota(jnp.int32, (2 * HALF, 1), 0) & (HALF - 1))
        two_ok = place_two > jnp.maximum(row, limit_two - 1)
        own_ok = column[:, mine] <= row
        row_real = row + local * ROWS < real
        for head in range(2):
            k_cols = slice(head * HEAD_DIM, (head + 1) * HEAD_DIM)
            v_cols = slice(KV_WIDTH + k_cols.start, KV_WIDTH + k_cols.stop)
            firsts = [(2 * head + i) * HEAD_DIM for i in range(2)]
            q = jnp.concatenate([q_ref[mine, at : at + HEAD_DIM] for at in firsts], 0)
            parts = [
                (two_ok, held[:ROWS, k_cols], held[:ROWS, v_cols]),
                (one_ok, held[ROWS:, k_cols], held[ROWS:, v_cols]),
            ]
            if half:
                parts.append((None, own[:HALF, k_cols], own[:HALF, v_cols]))
            parts.append((own_ok, own[mine, k_cols], own[mine, v_cols]))
            scores = []
            for ok, keys, _ in parts:
                s = lax.dot_general(q, keys, NT, preferred_element_type=F32)
                scores.append(s if ok is None else jnp.where(ok, s, -1e30))
            top = functools.reduce(jnp.maximum, [jnp.max(s, 1, keepdims=True) for s in scores])
            total = 0.0
            got = 0.0
            for s, (_, _, values) in zip(scores, parts):
                weights = jnp.exp(s - top)
                total += jnp.sum(weights, 1, keepdims=True)
                got += jnp.dot(weights.astype(BF16), values, preferred_element_type=F32)
            got = jnp.where(row_real, got / total, 0.0).astype(BF16)
            for i, at in enumerate(firsts):
                out[mine, at : at + HEAD_DIM] = got[i * HALF : (i + 1) * HALF]


def attention(scalars, q, own, one_back, two_back, prefix, gates):
    full = pl.BlockSpec((ROWS, 512), lambda i, *scalars: (0, 0))
    return pl.pallas_call(
        attention_kernel,
        grid_spec=pltpu.PrefetchScalarGridSpec(
            num_scalar_prefetch=4,
            grid=(1,),
            in_specs=[full] * 2 + [IN_HBM] * 7,
            out_specs=full,
            scratch_shapes=[
                pltpu.VMEM((2 * ROWS, PAIR), BF16),
                pltpu.VMEM((2, ROWS, PAIR), BF16),
                pltpu.SemaphoreType.DMA((8,)),
            ],
        ),
        out_shape=jax.ShapeDtypeStruct((ROWS, 512), BF16),
        compiler_params=params(),
        cost_estimate=cost(1, 1),
    )(*scalars, q, own, one_back, two_back, *prefix, *gates)


def piece_kernel(where, w_ref, gate, piece_a, piece_b, turned):
    strip = pl.ds(pl.multiple_of(where[3] * STRIP, 16), STRIP)
    for m in range(MP):

        @pl.when(where[0] == m)
        def _(m=m):
            for flip, piece in ((2, piece_a), (3, piece_b)):
                at = (m ^ flip) * FEATURES
                turned[...] = jnp.transpose(w_ref[:, at : at + FEATURES])
                piece[...] = turned[strip, :]


def turned_pieces(where, w_out, gate):
    piece = pl.BlockSpec((STRIP, 128), lambda i, where: (0, 0))
    return pl.pallas_call(
        piece_kernel,
        grid_spec=pltpu.PrefetchScalarGridSpec(
            num_scalar_prefetch=1,
            grid=(1,),
            in_specs=[pl.BlockSpec((128, MP * FEATURES), lambda i, where: (where[1], 0)), IN_HBM],
            out_specs=[piece, piece],
            scratch_shapes=[pltpu.VMEM((FEATURES, 128), BF16)],
        ),
        out_shape=[jax.ShapeDtypeStruct((STRIP, 128), BF16)] * 2,
        compiler_params=params(),
        cost_estimate=cost(1, 1),
    )(where, w_out, gate)


def turn_kernel(where, w_ref, gate, own, near):
    for m in range(MP):

        @pl.when(where[0] == m)
        def _(m=m):
            for flip, out in ((0, own), (1, near)):
                at = (m ^ flip) * FEATURES
                out[...] = jnp.transpose(w_ref[:, at : at + FEATURES])


def turned_weights(where, w_out, gate):
    whole = pl.BlockSpec((FEATURES, 128), lambda i, where: (0, i))
    return pl.pallas_call(
        turn_kernel,
        grid_spec=pltpu.PrefetchScalarGridSpec(
            num_scalar_prefetch=1,
            grid=(4,),
            in_specs=[pl.BlockSpec((128, MP * FEATURES), lambda i, where: (i, 0)), IN_HBM],
            out_specs=[whole, whole],
        ),
        out_shape=[jax.ShapeDtypeStruct((FEATURES, 512), BF16)] * 2,
        compiler_params=params(),
        cost_estimate=cost(1, 1),
    )(where, w_out, gate)


def pick_kernel(where, ids, lengths, rows_ref, gate, places, *outs):
    step = pl.program_id(0)

    @pl.when(step == 0)
    def _():
        first = lengths[ids[where[1]]] + where[2] * ROWS
        row = lax.broadcasted_iota(jnp.int32, (ROWS, HEAD_DIM), 0)
        places[...] = (row + first).astype(F32)

    reach = lengths[ids[(where[1] + step) & 3]]
    held_at = where[4] * HELD + lax.broadcasted_iota(jnp.int32, (HELD, 1), 0)
    wanted = (held_at < reach) & (held_at >= reach - WINDOW)
    for number, out in enumerate(outs):

        @pl.when(step == number)
        def _(out=out):
            for part in range(2):
                rows = rows_ref[0, :, part, :].astype(F32)
                out[:, part * KV_WIDTH : (part + 1) * KV_WIDTH] = jnp.where(
                    wanted, rows, 0.0
                ).astype(BF16)


def picked_rows(where, ids, lengths, prefix_cache, gate):
    return pl.pallas_call(
        pick_kernel,
        grid_spec=pltpu.PrefetchScalarGridSpec(
            num_scalar_prefetch=3,
            grid=(4,),
            in_specs=[
                pl.BlockSpec(
                    (1, HELD, 2, KV_WIDTH),
                    lambda i, where, ids, lengths: (ids[(where[1] + i) & 3], 0, 0, 0),
                ),
                IN_HBM,
            ],
            out_specs=[pl.BlockSpec((ROWS, HEAD_DIM), lambda i, *scalars: (0, 0))]
            + [pl.BlockSpec((HELD, PAIR), lambda i, *scalars: (0, 0))] * 4,
        ),
        out_shape=[jax.ShapeDtypeStruct((ROWS, HEAD_DIM), F32)]
        + [jax.ShapeDtypeStruct((HELD, PAIR), BF16)] * 4,
        compiler_params=params(),
        cost_estimate=cost(1, 1),
    )(where, ids, lengths, prefix_cache, gate)


def near_kernel(c0, c1, w0, w1, out):
    out[...] = lax.dot_general(
        w0[...], c0[...], NT, preferred_element_type=F32
    ) + lax.dot_general(w1[...], c1[...], NT, preferred_element_type=F32)


def near_output(contexts, weights):
    full = lambda shape: pl.BlockSpec(shape, lambda i: (0, 0))
    strip = pl.BlockSpec((STRIP, 512), lambda i: (i, 0))
    return pl.pallas_call(
        near_kernel,
        grid=(4,),
        in_specs=[full((ROWS, 512))] * 2 + [strip] * 2,
        out_specs=strip,
        out_shape=jax.ShapeDtypeStruct((FEATURES, ROWS), F32),
        compiler_params=params(),
        cost_estimate=cost(1, 1),
    )(*contexts, *weights)


def far_kernel(where, c0, c1, near, p0, p1, p2, p3, out, squares, held):
    step = pl.program_id(0)

    @pl.when(step == 0)
    def _():
        squares[...] = jnp.zeros_like(squares)

    for j, piece in enumerate((p0, p1, p2, p3)):
        lanes = pl.multiple_of(((where[1] - j) & 3) * HEAD_DIM, HEAD_DIM)
        for b in range(2):
            held[b, :, pl.ds(lanes, HEAD_DIM)] = piece[0, b]
    got = (
        near[...]
        + lax.dot_general(held[0], c0[...], NT, preferred_element_type=F32)
        + lax.dot_general(held[1], c1[...], NT, preferred_element_type=F32)
    )
    out[...] = got
    squares[...] += jnp.sum(got * got, 0, keepdims=True)


def far_output(where, contexts, near, pieces):
    full = lambda shape: pl.BlockSpec(shape, lambda i, where: (0, 0))
    strip = pl.BlockSpec((STRIP, ROWS), lambda i, where: (i, 0))
    piece = pl.BlockSpec(
        (1, 2, STRIP, HEAD_DIM), lambda i, where: ((where[3] - i) & 3, 0, 0, 0)
    )
    return pl.pallas_call(
        far_kernel,
        grid_spec=pltpu.PrefetchScalarGridSpec(
            num_scalar_prefetch=1,
            grid=(4,),
            in_specs=[full((ROWS, 512))] * 2 + [strip] + [piece] * 4,
            out_specs=[strip, full((1, ROWS))],
            scratch_shapes=[pltpu.VMEM((2, STRIP, 512), BF16)],
        ),
        out_shape=[
            jax.ShapeDtypeStruct((FEATURES, ROWS), F32),
            jax.ShapeDtypeStruct((1, ROWS), F32),
        ],
        compiler_params=params(),
        cost_estimate=cost(2 * ROWS * 1024 * FEATURES, 8_000_000),
    )(where, *contexts, near, *pieces)


def rope_tables(places):
    lane = jnp.arange(HEAD_DIM)
    frequency = rope_base ** (-((lane % 64).astype(F32) * 2.0 / HEAD_DIM))
    angles = places * frequency[None, :]
    return jnp.cos(angles), jnp.where(lane[None, :] < 64, -jnp.sin(angles), jnp.sin(angles))


def shards(
    tokens,
    gain_pre,
    w_query,
    w_key,
    w_value,
    w_out,
    gain_post,
    prefix_cache,
    template_ids,
    prefix_lengths,
    doc_lengths,
):
    member = lax.axis_index("mp")
    place = lax.axis_index("seq")
    doc = place // DOC_SHARDS
    local = place % DOC_SHARDS
    where = jnp.stack(
        [member, doc, local, place % 4, place, member, member ^ 1, member ^ 2, member ^ 3]
    ).astype(jnp.int32)
    scalars = (where, template_ids, prefix_lengths)

    turned_tokens = tokens.T
    near = across_mp(turned_tokens, 1)
    far = across_mp(turned_tokens, 2)

    places, mine, *others = picked_rows(*scalars, prefix_cache, near)
    for by, other in enumerate(others, 1):
        mine = mine + along_x(other, by)
    prefix = jnp.stack([mine] + [z_flip(mine, flip) for flip in (1, 2, 3)])
    tables = rope_tables(places)

    piece_a, piece_b = turned_pieces(where, w_out, others[0])
    crossed = (across_mp(piece_a, 2), across_mp(piece_b, 3))

    gain = gain_pre.reshape(2 * MP, 1, STEP)
    weights = (w_query, w_key, w_value)
    carried = project(where, 0, [turned_tokens, near], gain, weights, (piece_a,))
    far, piece_a, piece_b, prefix, *_ = lax.optimization_barrier(
        (far, *crossed, prefix, *carried, *tables)
    )
    w_piece = jnp.stack([piece_a, piece_b])
    prefix_twin = to_twin(prefix)
    queries, own = project(
        where, 2, [far, across_mp(far, 1)], gain, weights, (), carried, tables
    )
    w_parts = [w_piece] + [along_z(w_piece, by) for by in (1, 2, 3)]
    sent, *w_parts = lax.optimization_barrier((own, *w_parts, prefix_twin))[:5]
    one_back = within_doc(sent, 1)
    two_back = within_doc(sent, 2)
    w_line = jnp.stack(w_parts)
    w_next = along_x(w_line, 1)
    w_far = [w_line, w_next, along_x(w_next, 1), along_x(w_line, 3)]
    w_own, w_give = turned_weights(where, w_out, w_line)
    w_near = across_mp(w_give, 1)
    context = attention(
        (*scalars, doc_lengths), queries, own, one_back, two_back, (prefix, prefix_twin), (w_give, w_far[1], w_far[3])
    )
    c_far = across_mp(context, 2)
    c_near = across_mp(context, 1)
    near_sum = near_output([context, c_near], [w_own, w_near])
    attended, own_squares = far_output(where, [c_far, across_mp(c_far, 1)], near_sum, w_far)
    total = own_squares
    for flip in (1, 2, 3):
        total = total + across_mp(own_squares, flip)
    scale = lax.rsqrt(total * (1.0 / (MP * FEATURES)) + epsilon)
    result = turned_tokens.astype(F32) + gain_post[:, None] * attended * scale
    return result.astype(BF16).T


def solution(mesh):
    placed = (
        P("seq", "mp"),
        P(),
        P(None, "mp"),
        P(None, "mp"),
        P(None, "mp"),
        P("mp", None),
        P("mp"),
        P(None, "seq", None, "mp"),
        P(),
        P(),
        P(),
    )
    return jax.shard_map(
        shards, mesh=mesh, in_specs=placed, out_specs=P("seq", "mp"), check_vma=False
    )
```

time: 217 us -> 147 us (0.68)
  the two profiles are of different devices: /device:TPU:43 before, /device:TPU:33 now
where the time goes in v3:
time: 147 us
  Pallas kernels  54.9 us (37%)
  starting transfers between devices  44.9 us (31%)
  waiting for transfers between devices  36.3 us (25%)
  other arithmetic  7.37 us (5%)
  local copies, waits for them, and re-layouts  2.9 us (2%)
    ppermute x12, starting transfers between devices, across_mp(): return lax.ppermute(array, 'mp', [(i, i ^ flip) for i in range(MP)])  25.8 us
    ppermute x2, waiting for transfers between devices, within_doc(): return lax.ppermute(array, 'seq', pairs)  20.8 us
    pallas_call x2, Pallas kernels, project(): pl.pallas_call(functools.partial(project_kernel, chunks, not carried, boo...  19.1 us
    ppermute x12, waiting for transfers between devices, across_mp(): return lax.ppermute(array, 'mp', [(i, i ^ flip) for i in range(MP)])  10.4 us
    pallas_call x1, Pallas kernels, attention(): pl.pallas_call(attention_kernel, grid_spec=pltpu.PrefetchScalarGridSpec(n...  10.2 us
    ppermute x6, starting transfers between devices, along_x(): return lax.ppermute(array, 'seq', pairs)  7.56 us
    pallas_call x1, Pallas kernels, far_output(): pl.pallas_call(far_kernel, grid_spec=pltpu.PrefetchScalarGridSpec(num_sca...  6.95 us
    pallas_call x1, Pallas kernels, turned_weights(): pl.pallas_call(turn_kernel, grid_spec=pltpu.PrefetchScalarGridSpec(num_sc...  6.03 us
  transfers between devices with their start and end apart: 27, of which 9 were waited for; matrix products, arithmetic and copies ran while one was open for 3% of the time, Pallas kernels for 33%

profile of v3, /device:TPU:33, one launch (start us, length us, event | category | flops | bytes accessed | tf_op | source)
XLA Modules:
  0.0 146.5 jit_solution(1977119251181462155)
XLA Ops:
  0.0 0.7 collective-permute-start.1
  0.7 2.9 %collective-permute-start = (bf16[1344,512]{1,0:T(8,128)(2,1)}, bf16[1344,512]{1,0:T(8,128)(2,1)}, u32[]{:S(2)}, u32[]{:S(2)}) collective-permute-start(bf16[1344,512]{1,0:T(8,128)(2,1)} %bitcast.24), channel_id=1, source_target_pairs={{0,2},{1,3},{2,0},{3,1},{4,6},{5,7},{6,4},{7,5},{8,10},{9,11},{10,... | collective-permute-start | bytes 4128776 | tf_op jit(solution)/shard_map/ppermute | solution.py:42
  3.6 0.6 stack.75.where.order
  4.2 0.0 collective-permute-done.1.gate.refs_1_
  4.2 4.1 %shard_map.109 = (f32[512,128]{1,0:T(8,128)}, bf16[128,512]{1,0:T(8,128)(2,1)}, bf16[128,512]{1,0:T(8,128)(2,1)}, bf16[128,512]{1,0:T(8,128)(2,1)}, bf16[128,512]{1,0:T(8,128)(2,1)}) custom-call(s32[9]{0:T(128)} %stack.75.where.order, s32[4]{0:T(128)} %ids.3, s32[8]{0:T(128)} %lengths.3, bf16[8,128,2,256]{3,2,1,0:T(2,128)(2,1)} %rows_ref.1, ...), custom_call_target="tpu_custom_call" | custom-call | flops 1 | bytes 1 | tf_op jit(solution)/shard_map/pallas_call | solution.py:392
  8.3 1.2 collective-permute-start.4
  9.5 2.5 %collective-permute-start.5 = (bf16[128,512]{1,0:T(8,128)(2,1)}, bf16[128,512]{1,0:T(8,128)(2,1)S(1)}, u32[]{:S(2)}, u32[]{:S(2)}) collective-permute-start(bf16[128,512]{1,0:T(8,128)(2,1)} %get-tuple-element.33), channel_id=1, source_target_pairs={{0,64},{4,68},{8,72},{12,76},{16,80},{20,84},{24,88},{28,92},{32,9... | collective-permute-start | bytes 393224 | tf_op jit(solution)/shard_map/ppermute | solution.py:56
  12.0 1.2 collective-permute-start.6
  13.1 1.4 reshape.22.refs_2_
  14.6 3.1 %shard_map.110 = (bf16[336,128]{1,0:T(8,128)(2,1)}, bf16[336,128]{1,0:T(8,128)(2,1)}) custom-call(s32[9]{0:T(128)} %stack.75.where.order, bf16[512,5376]{1,0:T(8,128)(2,1)} %w_ref.3, bf16[128,512]{1,0:T(8,128)(2,1)} %get-tuple-element.29.gate), custom_call_target="tpu_custom_call" | custom-call | flops 1 | bytes 1 | tf_op jit(solution)/shard_map/pallas_call | solution.py:327
  17.7 2.5 %collective-permute-start.2 = (bf16[336,128]{1,0:T(8,128)(2,1)}, bf16[336,128]{1,0:T(8,128)(2,1)S(1)}, u32[]{:S(2)}, u32[]{:S(2)}) collective-permute-start(bf16[336,128]{1,0:T(8,128)(2,1)} %get-tuple-element.30.refs_6_), channel_id=1, source_target_pairs={{0,2},{1,3},{2,0},{3,1},{4,6},{5,7},{6,4},{7,5},{8,10},{9,11},{10,... | collective-permute-start | bytes 258056 | tf_op jit(solution)/shard_map/ppermute | solution.py:42
  20.1 9.0 %shard_map.111 = (f32[512,1024]{1,0:T(8,128)}, f32[512,128]{1,0:T(8,128)}) custom-call(s32[9]{0:T(128)} %stack.75.where.order, bf16[1344,512]{1,0:T(8,128)(2,1)} %bitcast.25, bf16[1344,512]{1,0:T(8,128)(2,1)} %collective-permute-done.1.gate.refs_1_, f32[8,1,672]{2,1,0:T(1,128)} %reshape.22.refs_2_, bf16[5376,512]{1,0:T(8,128)(2,1)} %refs_3_.3, ...), custom_call_target="tpu_custom_call" | custom-call | flops 1 | bytes 1 | tf_op jit(solution)/shard_map/pallas_call | solution.py:175
  29.2 0.0 collective-permute-done.4
  29.2 0.0 collective-permute-done.5
  29.2 0.0 collective-permute-done.6
  29.2 0.1 collective-permute-start.7
  29.3 2.8 %collective-permute-start.8 = (bf16[128,512]{1,0:T(8,128)(2,1)S(1)}, bf16[128,512]{1,0:T(8,128)(2,1)S(1)}, u32[]{:S(2)}, u32[]{:S(2)}) collective-permute-start(bf16[128,512]{1,0:T(8,128)(2,1)S(1)} %add_add_fusion), channel_id=1, source_target_pairs={{0,8},{4,12},{8,0},{12,4},{16,24},{20,28},{24,16},{28,20},{32,40},... | collective-permute-start | bytes 393224 | tf_op jit(solution)/shard_map/ppermute | solution.py:75
  32.1 0.2 collective-permute-start.9
  32.3 1.7 %negate_select_fusion = (f32[512,128]{1,0:T(8,128)}, f32[512,128]{1,0:T(8,128)}) fusion(f32[512,128]{1,0:T(8,128)S(1)} %copy-done.3, f32[128]{0:T(128)S(1)} %fusion.4, pred[128]{0:T(512)(128)(4,1)S(1)} %iota_compare_fusion), kind=kLoop, calls=%fused_computation.4 | loop fusion | flops 196608 | bytes 787072 | tf_op jit(solution)/shard_map/jit(_where)/select_n | solution.py:482
  34.0 0.0 collective-permute-done.7
  34.0 2.3 %collective-permute-start.3 = (bf16[336,128]{1,0:T(8,128)(2,1)}, bf16[336,128]{1,0:T(8,128)(2,1)S(1)}, u32[]{:S(2)}, u32[]{:S(2)}) collective-permute-start(bf16[336,128]{1,0:T(8,128)(2,1)} %get-tuple-element.31), channel_id=1, source_target_pairs={{0,3},{1,2},{2,1},{3,0},{4,7},{5,6},{6,5},{7,4},{8,11},{9,10},{10,... | collective-permute-start | bytes 258056 | tf_op jit(solution)/shard_map/ppermute | solution.py:42
  36.3 0.3 collective-permute-done.8
  36.7 2.5 %collective-permute-done.9 = bf16[128,512]{1,0:T(8,128)(2,1)S(1)} collective-permute-done((bf16[128,512]{1,0:T(8,128)(2,1)S(1)}, bf16[128,512]{1,0:T(8,128)(2,1)S(1)}, u32[]{:S(2)}, u32[]{:S(2)}) %collective-permute-start.9) | collective-permute-done | bytes 131104 | tf_op jit(solution)/shard_map/ppermute | solution.py:75
  39.1 0.1 pad_maximum_fusion.1.refs_0_
  39.2 0.0 collective-permute-done.refs_0_
  39.2 0.0 collective-permute-done.2
  39.3 0.3 collective-permute-done.3
  39.6 2.0 %collective-permute-start.10 = (bf16[1344,512]{1,0:T(8,128)(2,1)}, bf16[1344,512]{1,0:T(8,128)(2,1)}, u32[]{:S(2)}, u32[]{:S(2)}) collective-permute-start(bf16[1344,512]{1,0:T(8,128)(2,1)} %collective-permute-done.refs_0_), channel_id=1, source_target_pairs={{0,1},{1,0},{2,3},{3,2},{4,5},{5,4},{6,7},{7,6},{8,9},{9,8},{10,11... | collective-permute-start | bytes 4128776 | tf_op jit(solution)/shard_map/ppermute | solution.py:42
  41.7 2.3 %collective-permute-start.11 = (bf16[2,336,128]{2,1,0:T(8,128)(2,1)S(1)}, bf16[2,336,128]{2,1,0:T(8,128)(2,1)}, u32[]{:S(2)}, u32[]{:S(2)}) collective-permute-start(bf16[2,336,128]{2,1,0:T(8,128)(2,1)S(1)} %pad_maximum_fusion.2), channel_id=1, source_target_pairs={{0,4},{4,8},{8,12},{12,0},{16,20},{20,24},{24,28},{28,16},{32,36},... | collective-permute-start | bytes 516104 | tf_op jit(solution)/shard_map/ppermute | solution.py:66
  44.0 1.7 %collective-permute-start.12 = (bf16[2,336,128]{2,1,0:T(8,128)(2,1)S(1)}, bf16[2,336,128]{2,1,0:T(8,128)(2,1)}, u32[]{:S(2)}, u32[]{:S(2)}) collective-permute-start(bf16[2,336,128]{2,1,0:T(8,128)(2,1)S(1)} %pad_maximum_fusion.2), channel_id=1, source_target_pairs={{0,8},{4,12},{8,0},{12,4},{16,24},{20,28},{24,16},{28,20},{32,40},... | collective-permute-start | bytes 516104 | tf_op jit(solution)/shard_map/ppermute | solution.py:66
  45.7 2.0 %collective-permute-start.13 = (bf16[2,336,128]{2,1,0:T(8,128)(2,1)S(1)}, bf16[2,336,128]{2,1,0:T(8,128)(2,1)}, u32[]{:S(2)}, u32[]{:S(2)}) collective-permute-start(bf16[2,336,128]{2,1,0:T(8,128)(2,1)S(1)} %pad_maximum_fusion.2), channel_id=1, source_target_pairs={{0,12},{4,0},{8,4},{12,8},{16,28},{20,16},{24,20},{28,24},{32,44},... | collective-permute-start | bytes 516104 | tf_op jit(solution)/shard_map/ppermute | solution.py:66
  47.7 0.4 collective-permute-start.14
  48.1 0.0 collective-permute-done.10.refs_1_
  48.1 10.1 %shard_map.112 = (bf16[512,512]{1,0:T(8,128)(2,1)}, bf16[512,512]{1,0:T(8,128)(2,1)}) custom-call(s32[9]{0:T(128)} %stack.75.where.order, bf16[1344,512]{1,0:T(8,128)(2,1)} %collective-permute-done.refs_0_, bf16[1344,512]{1,0:T(8,128)(2,1)} %collective-permute-done.10.refs_1_, f32[8,1,672]{2,1,0:T(1,128)} %reshape.22.refs_2_, bf16[5376,512]{1,0:T(8,128)(2,1)} %refs_3_.3, ...), custom_call_target="tpu_custom_call" | custom-call | flops 6000000000 | bytes 20000000 | tf_op jit(solution)/shard_map/pallas_call | solution.py:175
  58.2 0.0 collective-permute-done.12
  58.2 0.0 collective-permute-done.13
  58.2 2.2 %collective-permute-done.14.refs_1_ = bf16[4,128,512]{2,1,0:T(8,128)(2,1)} collective-permute-done((bf16[4,128,512]{2,1,0:T(8,128)(2,1)S(1)}, bf16[4,128,512]{2,1,0:T(8,128)(2,1)}, u32[]{:S(2)}, u32[]{:S(2)}) %collective-permute-start.14) | collective-permute-done | bytes 524320 | tf_op jit(solution)/shard_map/ppermute | solution.py:71
  60.4 1.2 pad_maximum_fusion.gate.p0
  61.5 0.4 collective-permute-start.17
  61.9 2.4 %collective-permute-start.18 = (bf16[4,2,336,128]{3,2,1,0:T(8,128)(2,1)S(1)}, bf16[4,2,336,128]{3,2,1,0:T(8,128)(2,1)}, u32[]{:S(2)}, u32[]{:S(2)}) collective-permute-start(bf16[4,2,336,128]{3,2,1,0:T(8,128)(2,1)S(1)} %pad_maximum_fusion.gate.p0), channel_id=1, source_target_pairs={{0,96},{4,100},{8,104},{12,108},{16,112},{20,116},{24,120},{28,124... | collective-permute-start | bytes 2064392 | tf_op jit(solution)/shard_map/ppermute | solution.py:56
  64.3 0.0 collective-permute-start.15
  64.3 2.1 %collective-permute-start.16 = (bf16[512,512]{1,0:T(8,128)(2,1)}, bf16[512,512]{1,0:T(8,128)(2,1)}, u32[]{:S(2)}, u32[]{:S(2)}) collective-permute-start(bf16[512,512]{1,0:T(8,128)(2,1)} %get-tuple-element.44.own), channel_id=1, source_target_pairs={{0,8},{4,12},{8,16},{12,20},{16,24},{20,28},{24,0},{28,4},{32,40},... | collective-permute-start | bytes 1572872 | tf_op jit(solution)/shard_map/ppermute | solution.py:84
  66.4 6.0 %shard_map.113 = (bf16[1344,512]{1,0:T(8,128)(2,1)}, bf16[1344,512]{1,0:T(8,128)(2,1)}) custom-call(s32[9]{0:T(128)} %stack.75.where.order, bf16[512,5376]{1,0:T(8,128)(2,1)} %w_ref.3, bf16[4,2,336,128]{3,2,1,0:T(8,128)(2,1)} %copy-done), custom_call_target="tpu_custom_call" | custom-call | flops 1 | bytes 1 | tf_op jit(solution)/shard_map/pallas_call | solution.py:354
  72.4 2.9 %collective-permute-start.22 = (bf16[1344,512]{1,0:T(8,128)(2,1)}, bf16[1344,512]{1,0:T(8,128)(2,1)}, u32[]{:S(2)}, u32[]{:S(2)}) collective-permute-start(bf16[1344,512]{1,0:T(8,128)(2,1)} %get-tuple-element.49.refs_2_), channel_id=1, source_target_pairs={{0,1},{1,0},{2,3},{3,2},{4,5},{5,4},{6,7},{7,6},{8,9},{9,8},{10,11... | collective-permute-start | bytes 4128776 | tf_op jit(solution)/shard_map/ppermute | solution.py:42
  75.3 0.5 collective-permute-done.15.one_back
  75.7 20.4 %collective-permute-done.16.two_back = bf16[512,512]{1,0:T(8,128)(2,1)} collective-permute-done((bf16[512,512]{1,0:T(8,128)(2,1)}, bf16[512,512]{1,0:T(8,128)(2,1)}, u32[]{:S(2)}, u32[]{:S(2)}) %collective-permute-start.16) | collective-permute-done | bytes 524320 | tf_op jit(solution)/shard_map/ppermute | solution.py:84
  96.1 10.2 %shard_map.114.c0 = bf16[512,512]{1,0:T(8,128)(2,1)} custom-call(s32[9]{0:T(128)} %stack.75.where.order, s32[4]{0:T(128)} %ids.3, s32[8]{0:T(128)} %lengths.3, s32[4]{0:T(128)} %reals.1, bf16[512,512]{1,0:T(8,128)(2,1)} %get-tuple-element.39.q_ref, bf16[512,512]{1,0:T(8,128)(2,1)} %get-tuple-element.44.own, ...), custom_call_target="tpu_custom_call" | custom-call | flops 1 | bytes 1 | tf_op jit(solution)/shard_map/pallas_call | solution.py:294
  106.3 1.3 collective-permute-start.19
  107.6 0.0 collective-permute-start.23
  107.6 3.4 %collective-permute-start.21 = (bf16[512,512]{1,0:T(8,128)(2,1)}, bf16[512,512]{1,0:T(8,128)(2,1)}, u32[]{:S(2)}, u32[]{:S(2)}) collective-permute-start(bf16[512,512]{1,0:T(8,128)(2,1)} %shard_map.114.c0), channel_id=1, source_target_pairs={{0,1},{1,0},{2,3},{3,2},{4,5},{5,4},{6,7},{7,6},{8,9},{9,8},{10,11... | collective-permute-start | bytes 1572872 | tf_op jit(solution)/shard_map/ppermute | solution.py:42
  111.0 7.4 %collective-permute-done.19.c0 = bf16[512,512]{1,0:T(8,128)(2,1)} collective-permute-done((bf16[512,512]{1,0:T(8,128)(2,1)}, bf16[512,512]{1,0:T(8,128)(2,1)}, u32[]{:S(2)}, u32[]{:S(2)}) %collective-permute-start.19) | collective-permute-done | bytes 524320 | tf_op jit(solution)/shard_map/ppermute | solution.py:42
  118.4 4.1 %collective-permute-start.20 = (bf16[512,512]{1,0:T(8,128)(2,1)}, bf16[512,512]{1,0:T(8,128)(2,1)}, u32[]{:S(2)}, u32[]{:S(2)}) collective-permute-start(bf16[512,512]{1,0:T(8,128)(2,1)} %collective-permute-done.19.c0), channel_id=1, source_target_pairs={{0,1},{1,0},{2,3},{3,2},{4,5},{5,4},{6,7},{7,6},{8,9},{9,8},{10,11... | collective-permute-start | bytes 1572872 | tf_op jit(solution)/shard_map/ppermute | solution.py:42
  122.5 5.4 %shard_map.115.near = f32[1344,512]{1,0:T(8,128)} custom-call(bf16[512,512]{1,0:T(8,128)(2,1)} %shard_map.114.c0, bf16[512,512]{1,0:T(8,128)(2,1)} %collective-permute-done.21.c1, bf16[1344,512]{1,0:T(8,128)(2,1)} %get-tuple-element.50.w0, bf16[1344,512]{1,0:T(8,128)(2,1)} %collective-permute-done.22.w1), custom_call_target="tpu_custom_call" | custom-call | flops 1 | bytes 1 | tf_op jit(solution)/shard_map/pallas_call | solution.py:423
  128.0 0.0 copy-start.2
  128.0 0.0 collective-permute-done.20.c1
  128.0 0.8 copy-done.2
  128.8 6.9 %shard_map.116 = (f32[1344,512]{1,0:T(8,128)}, f32[1,512]{1,0:T(1,128)}) custom-call(s32[9]{0:T(128)} %stack.75.where.order, bf16[512,512]{1,0:T(8,128)(2,1)} %collective-permute-done.19.c0, bf16[512,512]{1,0:T(8,128)(2,1)} %collective-permute-done.20.c1, f32[1344,512]{1,0:T(8,128)} %shard_map.115.near, bf16[4,2,336,128]{3,2,1,0:T(8,128)(2,1)} %copy-done, ...), custom_call_target="tpu_custom_call" | custom-call | flops 1409286144 | bytes 8000000 | tf_op jit(solution)/shard_map/pallas_call | solution.py:460
  135.8 0.0 collective-permute-start.24
  135.8 1.3 collective-permute-start.25
  137.1 2.3 %collective-permute-start.26 = (f32[1,512]{1,0:T(1,128)}, f32[1,512]{1,0:T(1,128)S(1)}, u32[]{:S(2)}, u32[]{:S(2)}) collective-permute-start(f32[1,512]{1,0:T(1,128)} %get-tuple-element.52), channel_id=1, source_target_pairs={{0,3},{1,2},{2,1},{3,0},{4,7},{5,6},{6,5},{7,4},{8,11},{9,10},{10,... | collective-permute-start | bytes 6152 | tf_op jit(solution)/shard_map/ppermute | solution.py:42
  139.4 0.6 collective-permute-done.25
  140.0 2.1 %collective-permute-done.26 = f32[1,512]{1,0:T(1,128)S(1)} collective-permute-done((f32[1,512]{1,0:T(1,128)}, f32[1,512]{1,0:T(1,128)S(1)}, u32[]{:S(2)}, u32[]{:S(2)}) %collective-permute-start.26) | collective-permute-done | bytes 2080 | tf_op jit(solution)/shard_map/ppermute | solution.py:42
  142.1 0.7 add_rsqrt_fusion
  142.8 3.7 %fusion = bf16[512,1344]{0,1:T(8,128)(2,1)} fusion(f32[1344,512]{1,0:T(8,128)} %get-tuple-element.51, f32[512]{0:T(512)S(1)} %bitcast.33, f32[1344]{0:T(1024)S(1)} %copy-done.5, bf16[512,1344]{0,1:T(8,128)(2,1)} %param.11), kind=kLoop, calls=%fused_computation.1 | loop fusion | flops 3440640 | bytes 5512448 | tf_op jit(solution)/shard_map/transpose | solution.py:552
  (21 shorter events, 0.1 us)
Async XLA Ops:
  0.0 4.2 %collective-permute-start.1 = (bf16[1344,512]{1,0:T(8,128)(2,1)}, bf16[1344,512]{1,0:T(8,128)(2,1)}, u32[]{:S(2)}, u32[]{:S(2)}) collective-permute-start(bf16[1344,512]{1,0:T(8,128)(2,1)} %bitcast.23), channel_id=1, source_target_pairs={{0,1},{1,0},{2,3},{3,2},{4,5},{5,4},{6,7},{7,6},{8,9},{9,8},{10,11... | collective-permute-start | bytes 4128776 | tf_op jit(solution)/shard_map/ppermute | solution.py:42
  0.7 38.6 %collective-permute-start = (bf16[1344,512]{1,0:T(8,128)(2,1)}, bf16[1344,512]{1,0:T(8,128)(2,1)}, u32[]{:S(2)}, u32[]{:S(2)}) collective-permute-start(bf16[1344,512]{1,0:T(8,128)(2,1)} %bitcast.24), channel_id=1, source_target_pairs={{0,2},{1,3},{2,0},{3,1},{4,6},{5,7},{6,4},{7,5},{8,10},{9,11},{10,... | collective-permute-start | bytes 4128776 | tf_op jit(solution)/shard_map/ppermute | solution.py:42
  8.3 20.9 %collective-permute-start.4 = (bf16[128,512]{1,0:T(8,128)(2,1)}, bf16[128,512]{1,0:T(8,128)(2,1)S(1)}, u32[]{:S(2)}, u32[]{:S(2)}) collective-permute-start(bf16[128,512]{1,0:T(8,128)(2,1)} %get-tuple-element.29.gate), channel_id=1, source_target_pairs={{0,32},{4,36},{8,40},{12,44},{16,48},{20,52},{24,56},{28,60},{32,6... | collective-permute-start | bytes 393224 | tf_op jit(solution)/shard_map/ppermute | solution.py:56
  9.5 19.6 %collective-permute-start.5 = (bf16[128,512]{1,0:T(8,128)(2,1)}, bf16[128,512]{1,0:T(8,128)(2,1)S(1)}, u32[]{:S(2)}, u32[]{:S(2)}) collective-permute-start(bf16[128,512]{1,0:T(8,128)(2,1)} %get-tuple-element.33), channel_id=1, source_target_pairs={{0,64},{4,68},{8,72},{12,76},{16,80},{20,84},{24,88},{28,92},{32,9... | collective-permute-start | bytes 393224 | tf_op jit(solution)/shard_map/ppermute | solution.py:56
  12.0 17.2 %collective-permute-start.6 = (bf16[128,512]{1,0:T(8,128)(2,1)}, bf16[128,512]{1,0:T(8,128)(2,1)S(1)}, u32[]{:S(2)}, u32[]{:S(2)}) collective-permute-start(bf16[128,512]{1,0:T(8,128)(2,1)} %get-tuple-element.34), channel_id=1, source_target_pairs={{0,96},{4,100},{8,104},{12,108},{16,112},{20,116},{24,120},{28,124... | collective-permute-start | bytes 393224 | tf_op jit(solution)/shard_map/ppermute | solution.py:56
  17.7 11.5 %copy-start.4 = (bf16[128,512]{1,0:T(8,128)(2,1)S(1)}, bf16[128,512]{1,0:T(8,128)(2,1)}, u32[]{:S(2)}) copy-start(bf16[128,512]{1,0:T(8,128)(2,1)} %get-tuple-element.32) | copy-start | bytes 393220
  17.7 14.6 %copy-start.3 = (f32[512,128]{1,0:T(8,128)S(1)}, f32[512,128]{1,0:T(8,128)}, u32[]{:S(2)}) copy-start(f32[512,128]{1,0:T(8,128)} %get-tuple-element.37) | copy-start | bytes 786436
  17.7 21.6 %collective-permute-start.2 = (bf16[336,128]{1,0:T(8,128)(2,1)}, bf16[336,128]{1,0:T(8,128)(2,1)S(1)}, u32[]{:S(2)}, u32[]{:S(2)}) collective-permute-start(bf16[336,128]{1,0:T(8,128)(2,1)} %get-tuple-element.30.refs_6_), channel_id=1, source_target_pairs={{0,2},{1,3},{2,0},{3,1},{4,6},{5,7},{6,4},{7,5},{8,10},{9,11},{10,... | collective-permute-start | bytes 258056 | tf_op jit(solution)/shard_map/ppermute | solution.py:42
  29.2 4.7 %collective-permute-start.7 = (bf16[128,512]{1,0:T(8,128)(2,1)S(1)}, bf16[128,512]{1,0:T(8,128)(2,1)S(1)}, u32[]{:S(2)}, u32[]{:S(2)}) collective-permute-start(bf16[128,512]{1,0:T(8,128)(2,1)S(1)} %add_add_fusion), channel_id=1, source_target_pairs={{0,4},{4,0},{8,12},{12,8},{16,20},{20,16},{24,28},{28,24},{32,36},... | collective-permute-start | bytes 393224 | tf_op jit(solution)/shard_map/ppermute | solution.py:75
  29.3 7.3 %collective-permute-start.8 = (bf16[128,512]{1,0:T(8,128)(2,1)S(1)}, bf16[128,512]{1,0:T(8,128)(2,1)S(1)}, u32[]{:S(2)}, u32[]{:S(2)}) collective-permute-start(bf16[128,512]{1,0:T(8,128)(2,1)S(1)} %add_add_fusion), channel_id=1, source_target_pairs={{0,8},{4,12},{8,0},{12,4},{16,24},{20,28},{24,16},{28,20},{32,40},... | collective-permute-start | bytes 393224 | tf_op jit(solution)/shard_map/ppermute | solution.py:75
  32.1 7.0 %collective-permute-start.9 = (bf16[128,512]{1,0:T(8,128)(2,1)S(1)}, bf16[128,512]{1,0:T(8,128)(2,1)S(1)}, u32[]{:S(2)}, u32[]{:S(2)}) collective-permute-start(bf16[128,512]{1,0:T(8,128)(2,1)S(1)} %add_add_fusion), channel_id=1, source_target_pairs={{0,12},{4,8},{8,4},{12,0},{16,28},{20,24},{24,20},{28,16},{32,44},... | collective-permute-start | bytes 393224 | tf_op jit(solution)/shard_map/ppermute | solution.py:75
  34.0 5.6 %collective-permute-start.3 = (bf16[336,128]{1,0:T(8,128)(2,1)}, bf16[336,128]{1,0:T(8,128)(2,1)S(1)}, u32[]{:S(2)}, u32[]{:S(2)}) collective-permute-start(bf16[336,128]{1,0:T(8,128)(2,1)} %get-tuple-element.31), channel_id=1, source_target_pairs={{0,3},{1,2},{2,1},{3,0},{4,7},{5,6},{6,5},{7,4},{8,11},{9,10},{10,... | collective-permute-start | bytes 258056 | tf_op jit(solution)/shard_map/ppermute | solution.py:42
  39.2 18.9 %copy-start.1 = (bf16[4,128,512]{2,1,0:T(8,128)(2,1)}, bf16[4,128,512]{2,1,0:T(8,128)(2,1)S(1)}, u32[]{:S(2)}) copy-start(bf16[4,128,512]{2,1,0:T(8,128)(2,1)S(1)} %pad_maximum_fusion.1.refs_0_) | copy-start | bytes 1572868
  39.6 8.5 %collective-permute-start.10 = (bf16[1344,512]{1,0:T(8,128)(2,1)}, bf16[1344,512]{1,0:T(8,128)(2,1)}, u32[]{:S(2)}, u32[]{:S(2)}) collective-permute-start(bf16[1344,512]{1,0:T(8,128)(2,1)} %collective-permute-done.refs_0_), channel_id=1, source_target_pairs={{0,1},{1,0},{2,3},{3,2},{4,5},{5,4},{6,7},{7,6},{8,9},{9,8},{10,11... | collective-permute-start | bytes 4128776 | tf_op jit(solution)/shard_map/ppermute | solution.py:42
  41.7 16.5 %collective-permute-start.11 = (bf16[2,336,128]{2,1,0:T(8,128)(2,1)S(1)}, bf16[2,336,128]{2,1,0:T(8,128)(2,1)}, u32[]{:S(2)}, u32[]{:S(2)}) collective-permute-start(bf16[2,336,128]{2,1,0:T(8,128)(2,1)S(1)} %pad_maximum_fusion.2), channel_id=1, source_target_pairs={{0,4},{4,8},{8,12},{12,0},{16,20},{20,24},{24,28},{28,16},{32,36},... | collective-permute-start | bytes 516104 | tf_op jit(solution)/shard_map/ppermute | solution.py:66
  44.0 14.2 %collective-permute-start.12 = (bf16[2,336,128]{2,1,0:T(8,128)(2,1)S(1)}, bf16[2,336,128]{2,1,0:T(8,128)(2,1)}, u32[]{:S(2)}, u32[]{:S(2)}) collective-permute-start(bf16[2,336,128]{2,1,0:T(8,128)(2,1)S(1)} %pad_maximum_fusion.2), channel_id=1, source_target_pairs={{0,8},{4,12},{8,0},{12,4},{16,24},{20,28},{24,16},{28,20},{32,40},... | collective-permute-start | bytes 516104 | tf_op jit(solution)/shard_map/ppermute | solution.py:66
  45.7 12.5 %collective-permute-start.13 = (bf16[2,336,128]{2,1,0:T(8,128)(2,1)S(1)}, bf16[2,336,128]{2,1,0:T(8,128)(2,1)}, u32[]{:S(2)}, u32[]{:S(2)}) collective-permute-start(bf16[2,336,128]{2,1,0:T(8,128)(2,1)S(1)} %pad_maximum_fusion.2), channel_id=1, source_target_pairs={{0,12},{4,0},{8,4},{12,8},{16,28},{20,16},{24,20},{28,24},{32,44},... | collective-permute-start | bytes 516104 | tf_op jit(solution)/shard_map/ppermute | solution.py:66
  47.7 12.7 %collective-permute-start.14 = (bf16[4,128,512]{2,1,0:T(8,128)(2,1)S(1)}, bf16[4,128,512]{2,1,0:T(8,128)(2,1)}, u32[]{:S(2)}, u32[]{:S(2)}) collective-permute-start(bf16[4,128,512]{2,1,0:T(8,128)(2,1)S(1)} %pad_maximum_fusion.1.refs_0_), channel_id=1, source_target_pairs={{0,16},{4,20},{8,24},{12,28},{16,0},{20,4},{24,8},{28,12},{32,48},... | collective-permute-start | bytes 1572872 | tf_op jit(solution)/shard_map/ppermute | solution.py:71
  61.5 4.8 %copy-start = (bf16[4,2,336,128]{3,2,1,0:T(8,128)(2,1)}, bf16[4,2,336,128]{3,2,1,0:T(8,128)(2,1)S(1)}, u32[]{:S(2)}) copy-start(bf16[4,2,336,128]{3,2,1,0:T(8,128)(2,1)S(1)} %pad_maximum_fusion.gate.p0) | copy-start | bytes 2064388
  61.5 34.6 %collective-permute-start.17 = (bf16[4,2,336,128]{3,2,1,0:T(8,128)(2,1)S(1)}, bf16[4,2,336,128]{3,2,1,0:T(8,128)(2,1)}, u32[]{:S(2)}, u32[]{:S(2)}) collective-permute-start(bf16[4,2,336,128]{3,2,1,0:T(8,128)(2,1)S(1)} %pad_maximum_fusion.gate.p0), channel_id=1, source_target_pairs={{0,32},{4,36},{8,40},{12,44},{16,48},{20,52},{24,56},{28,60},{32,6... | collective-permute-start | bytes 2064392 | tf_op jit(solution)/shard_map/ppermute | solution.py:56
  61.9 34.2 %collective-permute-start.18 = (bf16[4,2,336,128]{3,2,1,0:T(8,128)(2,1)S(1)}, bf16[4,2,336,128]{3,2,1,0:T(8,128)(2,1)}, u32[]{:S(2)}, u32[]{:S(2)}) collective-permute-start(bf16[4,2,336,128]{3,2,1,0:T(8,128)(2,1)S(1)} %pad_maximum_fusion.gate.p0), channel_id=1, source_target_pairs={{0,96},{4,100},{8,104},{12,108},{16,112},{20,116},{24,120},{28,124... | collective-permute-start | bytes 2064392 | tf_op jit(solution)/shard_map/ppermute | solution.py:56
  64.3 11.4 %collective-permute-start.15 = (bf16[512,512]{1,0:T(8,128)(2,1)}, bf16[512,512]{1,0:T(8,128)(2,1)}, u32[]{:S(2)}, u32[]{:S(2)}) collective-permute-start(bf16[512,512]{1,0:T(8,128)(2,1)} %get-tuple-element.44.own), channel_id=1, source_target_pairs={{0,4},{4,8},{8,12},{12,16},{16,20},{20,24},{24,28},{28,0},{32,36},... | collective-permute-start | bytes 1572872 | tf_op jit(solution)/shard_map/ppermute | solution.py:84
  64.3 31.8 %collective-permute-start.16 = (bf16[512,512]{1,0:T(8,128)(2,1)}, bf16[512,512]{1,0:T(8,128)(2,1)}, u32[]{:S(2)}, u32[]{:S(2)}) collective-permute-start(bf16[512,512]{1,0:T(8,128)(2,1)} %get-tuple-element.44.own), channel_id=1, source_target_pairs={{0,8},{4,12},{8,16},{12,20},{16,24},{20,28},{24,0},{28,4},{32,40},... | collective-permute-start | bytes 1572872 | tf_op jit(solution)/shard_map/ppermute | solution.py:84
  72.4 50.1 %collective-permute-start.22 = (bf16[1344,512]{1,0:T(8,128)(2,1)}, bf16[1344,512]{1,0:T(8,128)(2,1)}, u32[]{:S(2)}, u32[]{:S(2)}) collective-permute-start(bf16[1344,512]{1,0:T(8,128)(2,1)} %get-tuple-element.49.refs_2_), channel_id=1, source_target_pairs={{0,1},{1,0},{2,3},{3,2},{4,5},{5,4},{6,7},{7,6},{8,9},{9,8},{10,11... | collective-permute-start | bytes 4128776 | tf_op jit(solution)/shard_map/ppermute | solution.py:42
  106.3 12.2 %collective-permute-start.19 = (bf16[512,512]{1,0:T(8,128)(2,1)}, bf16[512,512]{1,0:T(8,128)(2,1)}, u32[]{:S(2)}, u32[]{:S(2)}) collective-permute-start(bf16[512,512]{1,0:T(8,128)(2,1)} %shard_map.114.c0), channel_id=1, source_target_pairs={{0,2},{1,3},{2,0},{3,1},{4,6},{5,7},{6,4},{7,5},{8,10},{9,11},{10,... | collective-permute-start | bytes 1572872 | tf_op jit(solution)/shard_map/ppermute | solution.py:42
  107.6 20.4 %collective-permute-start.23 = (bf16[4,2,336,128]{3,2,1,0:T(8,128)(2,1)}, bf16[4,2,336,128]{3,2,1,0:T(8,128)(2,1)S(1)}, u32[]{:S(2)}, u32[]{:S(2)}) collective-permute-start(bf16[4,2,336,128]{3,2,1,0:T(8,128)(2,1)} %collective-permute-done.17.refs_3_.p1), channel_id=1, source_target_pairs={{0,32},{4,36},{8,40},{12,44},{16,48},{20,52},{24,56},{28,60},{32,6... | collective-permute-start | bytes 2064392 | tf_op jit(solution)/shard_map/ppermute | solution.py:56
  107.6 14.9 %collective-permute-start.21 = (bf16[512,512]{1,0:T(8,128)(2,1)}, bf16[512,512]{1,0:T(8,128)(2,1)}, u32[]{:S(2)}, u32[]{:S(2)}) collective-permute-start(bf16[512,512]{1,0:T(8,128)(2,1)} %shard_map.114.c0), channel_id=1, source_target_pairs={{0,1},{1,0},{2,3},{3,2},{4,5},{5,4},{6,7},{7,6},{8,9},{9,8},{10,11... | collective-permute-start | bytes 1572872 | tf_op jit(solution)/shard_map/ppermute | solution.py:42
  118.4 9.5 %collective-permute-start.20 = (bf16[512,512]{1,0:T(8,128)(2,1)}, bf16[512,512]{1,0:T(8,128)(2,1)}, u32[]{:S(2)}, u32[]{:S(2)}) collective-permute-start(bf16[512,512]{1,0:T(8,128)(2,1)} %collective-permute-done.19.c0), channel_id=1, source_target_pairs={{0,1},{1,0},{2,3},{3,2},{4,5},{5,4},{6,7},{7,6},{8,9},{9,8},{10,11... | collective-permute-start | bytes 1572872 | tf_op jit(solution)/shard_map/ppermute | solution.py:42
  128.0 14.8 %copy-start.5 = (f32[1344]{0:T(1024)S(1)}, f32[1344]{0:T(1024)}, u32[]{:S(2)}) copy-start(f32[1344]{0:T(1024)} %param.17) | copy-start | bytes 16132
  128.0 0.8 copy-start.2
  135.8 3.6 %collective-permute-start.24 = (f32[1,512]{1,0:T(1,128)}, f32[1,512]{1,0:T(1,128)S(1)}, u32[]{:S(2)}, u32[]{:S(2)}) collective-permute-start(f32[1,512]{1,0:T(1,128)} %get-tuple-element.52), channel_id=1, source_target_pairs={{0,1},{1,0},{2,3},{3,2},{4,5},{5,4},{6,7},{7,6},{8,9},{9,8},{10,11... | collective-permute-start | bytes 6152 | tf_op jit(solution)/shard_map/ppermute | solution.py:42
  135.8 4.2 %collective-permute-start.25 = (f32[1,512]{1,0:T(1,128)}, f32[1,512]{1,0:T(1,128)S(1)}, u32[]{:S(2)}, u32[]{:S(2)}) collective-permute-start(f32[1,512]{1,0:T(1,128)} %get-tuple-element.52), channel_id=1, source_target_pairs={{0,2},{1,3},{2,0},{3,1},{4,6},{5,7},{6,4},{7,5},{8,10},{9,11},{10,... | collective-permute-start | bytes 6152 | tf_op jit(solution)/shard_map/ppermute | solution.py:42
  137.1 5.0 %collective-permute-start.26 = (f32[1,512]{1,0:T(1,128)}, f32[1,512]{1,0:T(1,128)S(1)}, u32[]{:S(2)}, u32[]{:S(2)}) collective-permute-start(f32[1,512]{1,0:T(1,128)} %get-tuple-element.52), channel_id=1, source_target_pairs={{0,3},{1,2},{2,1},{3,0},{4,7},{5,6},{6,5},{7,4},{8,11},{9,10},{10,... | collective-permute-start | bytes 6152 | tf_op jit(solution)/shard_map/ppermute | solution.py:42

commit v4 on v3

--- a/solution.py
+++ b/solution.py
@@ -198,7 +198,7 @@
 
 
 def attention_kernel(where, ids, lengths, reals, q_ref, own, one_back, two_back, *refs):
-    prefix, twin, _, _, _, out, held, lines, sems = refs
+    prefix, twin, _, out, held, lines, sems = refs
     local = where[2]
     length = lengths[ids[where[1]]]
     real = reals[where[1]]
@@ -296,7 +296,7 @@
         grid_spec=pltpu.PrefetchScalarGridSpec(
             num_scalar_prefetch=4,
             grid=(1,),
-            in_specs=[full] * 2 + [IN_HBM] * 7,
+            in_specs=[full] * 2 + [IN_HBM] * 5,
             out_specs=full,
             scratch_shapes=[
                 pltpu.VMEM((2 * ROWS, PAIR), BF16),
@@ -411,27 +411,7 @@
     )(where, ids, lengths, prefix_cache, gate)
 
 
-def near_kernel(c0, c1, w0, w1, out):
-    out[...] = lax.dot_general(
-        w0[...], c0[...], NT, preferred_element_type=F32
-    ) + lax.dot_general(w1[...], c1[...], NT, preferred_element_type=F32)
-
-
-def near_output(contexts, weights):
-    full = lambda shape: pl.BlockSpec(shape, lambda i: (0, 0))
-    strip = pl.BlockSpec((STRIP, 512), lambda i: (i, 0))
-    return pl.pallas_call(
-        near_kernel,
-        grid=(4,),
-        in_specs=[full((ROWS, 512))] * 2 + [strip] * 2,
-        out_specs=strip,
-        out_shape=jax.ShapeDtypeStruct((FEATURES, ROWS), F32),
-        compiler_params=params(),
-        cost_estimate=cost(1, 1),
-    )(*contexts, *weights)
-
-
-def far_kernel(where, c0, c1, near, p0, p1, p2, p3, out, squares, held):
+def output_kernel(where, c0, c1, c2, c3, w0, w1, p0, p1, p2, p3, out, squares, held):
     step = pl.program_id(0)
 
     @pl.when(step == 0)
@@ -442,27 +422,26 @@
         lanes = pl.multiple_of(((where[1] - j) & 3) * HEAD_DIM, HEAD_DIM)
         for b in range(2):
             held[b, :, pl.ds(lanes, HEAD_DIM)] = piece[0, b]
-    got = (
-        near[...]
-        + lax.dot_general(held[0], c0[...], NT, preferred_element_type=F32)
-        + lax.dot_general(held[1], c1[...], NT, preferred_element_type=F32)
-    )
+    got = lax.dot_general(w0[...], c0[...], NT, preferred_element_type=F32)
+    got += lax.dot_general(w1[...], c1[...], NT, preferred_element_type=F32)
+    got += lax.dot_general(held[0], c2[...], NT, preferred_element_type=F32)
+    got += lax.dot_general(held[1], c3[...], NT, preferred_element_type=F32)
     out[...] = got
     squares[...] += jnp.sum(got * got, 0, keepdims=True)
 
 
-def far_output(where, contexts, near, pieces):
+def output(where, contexts, weights, pieces):
     full = lambda shape: pl.BlockSpec(shape, lambda i, where: (0, 0))
     strip = pl.BlockSpec((STRIP, ROWS), lambda i, where: (i, 0))
     piece = pl.BlockSpec(
         (1, 2, STRIP, HEAD_DIM), lambda i, where: ((where[3] - i) & 3, 0, 0, 0)
     )
     return pl.pallas_call(
-        far_kernel,
+        output_kernel,
         grid_spec=pltpu.PrefetchScalarGridSpec(
             num_scalar_prefetch=1,
             grid=(4,),
-            in_specs=[full((ROWS, 512))] * 2 + [strip] + [piece] * 4,
+            in_specs=[full((ROWS, 512))] * 4 + [strip] * 2 + [piece] * 4,
             out_specs=[strip, full((1, ROWS))],
             scratch_shapes=[pltpu.VMEM((2, STRIP, 512), BF16)],
         ),
@@ -471,8 +450,8 @@
             jax.ShapeDtypeStruct((1, ROWS), F32),
         ],
         compiler_params=params(),
-        cost_estimate=cost(2 * ROWS * 1024 * FEATURES, 8_000_000),
-    )(where, *contexts, near, *pieces)
+        cost_estimate=cost(4 * ROWS * 1024 * FEATURES, 8_000_000),
+    )(where, *contexts, *weights, *pieces)
 
 
 def rope_tables(places):
@@ -529,21 +508,21 @@
         where, 2, [far, across_mp(far, 1)], gain, weights, (), carried, tables
     )
     w_parts = [w_piece] + [along_z(w_piece, by) for by in (1, 2, 3)]
-    sent, *w_parts = lax.optimization_barrier((own, *w_parts, prefix_twin))[:5]
-    one_back = within_doc(sent, 1)
-    two_back = within_doc(sent, 2)
+    one_back = within_doc(own, 1)
+    two_back = within_doc(own, 2)
+    w_parts = lax.optimization_barrier((*w_parts, own))[:4]
     w_line = jnp.stack(w_parts)
     w_next = along_x(w_line, 1)
     w_far = [w_line, w_next, along_x(w_next, 1), along_x(w_line, 3)]
     w_own, w_give = turned_weights(where, w_out, w_line)
     w_near = across_mp(w_give, 1)
     context = attention(
-        (*scalars, doc_lengths), queries, own, one_back, two_back, (prefix, prefix_twin), (w_give, w_far[1], w_far[3])
+        (*scalars, doc_lengths), queries, own, one_back, two_back, (prefix, prefix_twin), (w_give,)
     )
     c_far = across_mp(context, 2)
     c_near = across_mp(context, 1)
-    near_sum = near_output([context, c_near], [w_own, w_near])
-    attended, own_squares = far_output(where, [c_far, across_mp(c_far, 1)], near_sum, w_far)
+    contexts = [context, c_near, c_far, across_mp(c_far, 1)]
+    attended, own_squares = output(where, contexts, [w_own, w_near], w_far)
     total = own_squares
     for flip in (1, 2, 3):
         total = total + across_mp(own_squares, flip)

time: 147 us -> 141 us (0.959)
  the two profiles are of different devices: /device:TPU:33 before, /device:TPU:1 now
where the time goes in v4:
time: 141 us
  Pallas kernels  50 us (35%)
  starting transfers between devices  45.3 us (32%)
  waiting for transfers between devices  33.2 us (24%)
  other arithmetic  8.16 us (6%)
  local copies, waits for them, and re-layouts  3.76 us (3%)
    ppermute x12, starting transfers between devices, across_mp(): return lax.ppermute(array, 'mp', [(i, i ^ flip) for i in range(MP)])  26.4 us
    pallas_call x2, Pallas kernels, project(): pl.pallas_call(functools.partial(project_kernel, chunks, not carried, boo...  19.1 us
    ppermute x2, waiting for transfers between devices, within_doc(): return lax.ppermute(array, 'seq', pairs)  15 us
    ppermute x12, waiting for transfers between devices, across_mp(): return lax.ppermute(array, 'mp', [(i, i ^ flip) for i in range(MP)])  12.5 us
    pallas_call x1, Pallas kernels, attention(): pl.pallas_call(attention_kernel, grid_spec=pltpu.PrefetchScalarGridSpec(n...  9.24 us
    pallas_call x1, Pallas kernels, output(): pl.pallas_call(output_kernel, grid_spec=pltpu.PrefetchScalarGridSpec(num_...  8.46 us
    ppermute x6, starting transfers between devices, along_x(): return lax.ppermute(array, 'seq', pairs)  6.63 us
    pallas_call x1, Pallas kernels, turned_weights(): pl.pallas_call(turn_kernel, grid_spec=pltpu.PrefetchScalarGridSpec(num_sc...  6.03 us
  transfers between devices with their start and end apart: 27, of which 8 were waited for; matrix products, arithmetic and copies ran while one was open for 4% of the time, Pallas kernels for 30%

profile of v4, /device:TPU:1, one launch (start us, length us, event | category | flops | bytes accessed | tf_op | source)
XLA Modules:
  0.0 140.5 jit_solution(17781115934246169629)
XLA Ops:
  0.0 1.4 %collective-permute-start.1 = (bf16[1344,512]{1,0:T(8,128)(2,1)}, bf16[1344,512]{1,0:T(8,128)(2,1)}, u32[]{:S(2)}, u32[]{:S(2)}) collective-permute-start(bf16[1344,512]{1,0:T(8,128)(2,1)} %bitcast.23), channel_id=1, source_target_pairs={{0,1},{1,0},{2,3},{3,2},{4,5},{5,4},{6,7},{7,6},{8,9},{9,8},{10,11... | collective-permute-start | bytes 4128776 | tf_op jit(solution)/shard_map/ppermute | solution.py:42
  1.4 3.0 %collective-permute-start = (bf16[1344,512]{1,0:T(8,128)(2,1)}, bf16[1344,512]{1,0:T(8,128)(2,1)}, u32[]{:S(2)}, u32[]{:S(2)}) collective-permute-start(bf16[1344,512]{1,0:T(8,128)(2,1)} %bitcast.24), channel_id=1, source_target_pairs={{0,2},{1,3},{2,0},{3,1},{4,6},{5,7},{6,4},{7,5},{8,10},{9,11},{10,... | collective-permute-start | bytes 4128776 | tf_op jit(solution)/shard_map/ppermute | solution.py:42
  4.4 0.6 stack.75.where.order
  5.1 0.0 collective-permute-done.1.gate.refs_1_
  5.1 4.1 %shard_map.109 = (f32[512,128]{1,0:T(8,128)}, bf16[128,512]{1,0:T(8,128)(2,1)}, bf16[128,512]{1,0:T(8,128)(2,1)}, bf16[128,512]{1,0:T(8,128)(2,1)}, bf16[128,512]{1,0:T(8,128)(2,1)}) custom-call(s32[9]{0:T(128)} %stack.75.where.order, s32[4]{0:T(128)} %ids.3, s32[8]{0:T(128)} %lengths.3, bf16[8,128,2,256]{3,2,1,0:T(2,128)(2,1)} %rows_ref.1, ...), custom_call_target="tpu_custom_call" | custom-call | flops 1 | bytes 1 | tf_op jit(solution)/shard_map/pallas_call | solution.py:392
  9.1 2.8 %collective-permute-start.5 = (bf16[128,512]{1,0:T(8,128)(2,1)}, bf16[128,512]{1,0:T(8,128)(2,1)S(1)}, u32[]{:S(2)}, u32[]{:S(2)}) collective-permute-start(bf16[128,512]{1,0:T(8,128)(2,1)} %get-tuple-element.32), channel_id=1, source_target_pairs={{0,64},{4,68},{8,72},{12,76},{16,80},{20,84},{24,88},{28,92},{32,9... | collective-permute-start | bytes 393224 | tf_op jit(solution)/shard_map/ppermute | solution.py:56
  11.9 0.8 collective-permute-start.6
  12.7 0.6 collective-permute-start.4
  13.4 1.4 %reshape.22.refs_2_ = f32[8,1,672]{2,1,0:T(1,128)} reshape(f32[5376]{0:T(1024)} %param.12) | data formatting | bytes 43008 | tf_op jit(solution)/shard_map/reshape | solution.py:499
  14.8 3.1 %shard_map.110 = (bf16[336,128]{1,0:T(8,128)(2,1)}, bf16[336,128]{1,0:T(8,128)(2,1)}) custom-call(s32[9]{0:T(128)} %stack.75.where.order, bf16[512,5376]{1,0:T(8,128)(2,1)} %w_ref.3, bf16[128,512]{1,0:T(8,128)(2,1)} %get-tuple-element.28.gate), custom_call_target="tpu_custom_call" | custom-call | flops 1 | bytes 1 | tf_op jit(solution)/shard_map/pallas_call | solution.py:327
  17.9 2.5 %collective-permute-start.2 = (bf16[336,128]{1,0:T(8,128)(2,1)}, bf16[336,128]{1,0:T(8,128)(2,1)S(1)}, u32[]{:S(2)}, u32[]{:S(2)}) collective-permute-start(bf16[336,128]{1,0:T(8,128)(2,1)} %get-tuple-element.29.refs_6_), channel_id=1, source_target_pairs={{0,2},{1,3},{2,0},{3,1},{4,6},{5,7},{6,4},{7,5},{8,10},{9,11},{10,... | collective-permute-start | bytes 258056 | tf_op jit(solution)/shard_map/ppermute | solution.py:42
  20.4 9.0 %shard_map.111 = (f32[512,1024]{1,0:T(8,128)}, f32[512,128]{1,0:T(8,128)}) custom-call(s32[9]{0:T(128)} %stack.75.where.order, bf16[1344,512]{1,0:T(8,128)(2,1)} %bitcast.25, bf16[1344,512]{1,0:T(8,128)(2,1)} %collective-permute-done.1.gate.refs_1_, f32[8,1,672]{2,1,0:T(1,128)} %reshape.22.refs_2_, bf16[5376,512]{1,0:T(8,128)(2,1)} %refs_3_.3, ...), custom_call_target="tpu_custom_call" | custom-call | flops 1 | bytes 1 | tf_op jit(solution)/shard_map/pallas_call | solution.py:175
  29.4 0.0 collective-permute-done.5
  29.4 0.0 collective-permute-done.6
  29.4 0.0 collective-permute-done.4
  29.5 3.8 %collective-permute-start.9 = (bf16[128,512]{1,0:T(8,128)(2,1)S(1)}, bf16[128,512]{1,0:T(8,128)(2,1)S(1)}, u32[]{:S(2)}, u32[]{:S(2)}) collective-permute-start(bf16[128,512]{1,0:T(8,128)(2,1)S(1)} %add_add_fusion), channel_id=1, source_target_pairs={{0,12},{4,8},{8,4},{12,0},{16,28},{20,24},{24,20},{28,16},{32,44},... | collective-permute-start | bytes 393224 | tf_op jit(solution)/shard_map/ppermute | solution.py:75
  33.3 0.0 collective-permute-start.8
  33.3 0.7 collective-permute-start.7
  34.0 1.7 %negate_select_fusion = (f32[512,128]{1,0:T(8,128)}, f32[512,128]{1,0:T(8,128)}) fusion(f32[512,128]{1,0:T(8,128)S(1)} %copy-done.1, f32[128]{0:T(128)S(1)} %fusion.4, pred[128]{0:T(512)(128)(4,1)S(1)} %iota_compare_fusion), kind=kLoop, calls=%fused_computation.4 | loop fusion | flops 196608 | bytes 787072 | tf_op jit(solution)/shard_map/jit(_where)/select_n | solution.py:461
  35.7 2.4 %collective-permute-done.9 = bf16[128,512]{1,0:T(8,128)(2,1)S(1)} collective-permute-done((bf16[128,512]{1,0:T(8,128)(2,1)S(1)}, bf16[128,512]{1,0:T(8,128)(2,1)S(1)}, u32[]{:S(2)}, u32[]{:S(2)}) %collective-permute-start.9) | collective-permute-done | bytes 131104 | tf_op jit(solution)/shard_map/ppermute | solution.py:75
  38.0 2.2 %collective-permute-start.3 = (bf16[336,128]{1,0:T(8,128)(2,1)S(1)}, bf16[336,128]{1,0:T(8,128)(2,1)S(1)}, u32[]{:S(2)}, u32[]{:S(2)}) collective-permute-start(bf16[336,128]{1,0:T(8,128)(2,1)S(1)} %copy-done.9), channel_id=1, source_target_pairs={{0,3},{1,2},{2,1},{3,0},{4,7},{5,6},{6,5},{7,4},{8,11},{9,10},{10,... | collective-permute-start | bytes 258056 | tf_op jit(solution)/shard_map/ppermute | solution.py:42
  40.3 0.0 collective-permute-done.8
  40.3 0.0 collective-permute-done.7
  40.3 0.1 pad_maximum_fusion.1.refs_0_
  40.4 0.0 collective-permute-done.refs_0_
  40.4 3.1 %collective-permute-done.3 = bf16[336,128]{1,0:T(8,128)(2,1)S(1)} collective-permute-done((bf16[336,128]{1,0:T(8,128)(2,1)S(1)}, bf16[336,128]{1,0:T(8,128)(2,1)S(1)}, u32[]{:S(2)}, u32[]{:S(2)}) %collective-permute-start.3) | collective-permute-done | bytes 86048 | tf_op jit(solution)/shard_map/ppermute | solution.py:42
  43.5 0.0 collective-permute-done.2
  43.5 1.8 %collective-permute-start.10 = (bf16[1344,512]{1,0:T(8,128)(2,1)}, bf16[1344,512]{1,0:T(8,128)(2,1)}, u32[]{:S(2)}, u32[]{:S(2)}) collective-permute-start(bf16[1344,512]{1,0:T(8,128)(2,1)} %collective-permute-done.refs_0_), channel_id=1, source_target_pairs={{0,1},{1,0},{2,3},{3,2},{4,5},{5,4},{6,7},{7,6},{8,9},{9,8},{10,11... | collective-permute-start | bytes 4128776 | tf_op jit(solution)/shard_map/ppermute | solution.py:42
  45.3 4.0 %collective-permute-start.16 = (bf16[2,336,128]{2,1,0:T(8,128)(2,1)S(1)}, bf16[2,336,128]{2,1,0:T(8,128)(2,1)S(1)}, u32[]{:S(2)}, u32[]{:S(2)}) collective-permute-start(bf16[2,336,128]{2,1,0:T(8,128)(2,1)S(1)} %pad_maximum_fusion.2), channel_id=1, source_target_pairs={{0,12},{4,0},{8,4},{12,8},{16,28},{20,16},{24,20},{28,24},{32,44},... | collective-permute-start | bytes 516104 | tf_op jit(solution)/shard_map/ppermute | solution.py:66
  49.3 0.0 collective-permute-start.15
  49.3 0.7 collective-permute-start.14
  50.0 0.4 collective-permute-start.13
  50.4 0.0 collective-permute-done.10.refs_1_
  50.4 10.1 %shard_map.112 = (bf16[512,512]{1,0:T(8,128)(2,1)}, bf16[512,512]{1,0:T(8,128)(2,1)}) custom-call(s32[9]{0:T(128)} %stack.75.where.order, bf16[1344,512]{1,0:T(8,128)(2,1)} %collective-permute-done.refs_0_, bf16[1344,512]{1,0:T(8,128)(2,1)} %collective-permute-done.10.refs_1_, f32[8,1,672]{2,1,0:T(1,128)} %reshape.22.refs_2_, bf16[5376,512]{1,0:T(8,128)(2,1)} %refs_3_.3, ...), custom_call_target="tpu_custom_call" | custom-call | flops 6000000000 | bytes 20000000 | tf_op jit(solution)/shard_map/pallas_call | solution.py:175
  60.5 2.4 %collective-permute-start.12 = (bf16[512,512]{1,0:T(8,128)(2,1)}, bf16[512,512]{1,0:T(8,128)(2,1)}, u32[]{:S(2)}, u32[]{:S(2)}) collective-permute-start(bf16[512,512]{1,0:T(8,128)(2,1)} %get-tuple-element.39.own), channel_id=1, source_target_pairs={{0,8},{4,12},{8,16},{12,20},{16,24},{20,28},{24,0},{28,4},{32,40},... | collective-permute-start | bytes 1572872 | tf_op jit(solution)/shard_map/ppermute | solution.py:84
  62.9 0.0 collective-permute-done.16
  62.9 0.3 collective-permute-start.11
  63.2 0.0 collective-permute-done.15
  63.2 0.0 collective-permute-done.14
  63.2 1.9 %pad_maximum_fusion.gate.p0 = bf16[4,2,336,128]{3,2,1,0:T(8,128)(2,1)} fusion(bf16[1,2,336,128]{3,2,1,0:T(8,128)(2,1)S(1)} %bitcast.28, bf16[1,2,336,128]{3,2,1,0:T(8,128)(2,1)} %bitcast.17, bf16[1,2,336,128]{3,2,1,0:T(8,128)(2,1)} %bitcast.16, bf16[1,2,336,128]{3,2,1,0:T(8,128)(2,1)S(1)} %bitcast.26), kind=kLoop, calls=%fused_computation.2 | loop fusion | flops 1032192 | bytes 1376256 | tf_op jit(solution)/shard_map/stack | solution.py:514
  65.1 0.3 collective-permute-start.21
  65.5 6.0 %shard_map.113 = (bf16[1344,512]{1,0:T(8,128)(2,1)}, bf16[1344,512]{1,0:T(8,128)(2,1)}) custom-call(s32[9]{0:T(128)} %stack.75.where.order, bf16[512,5376]{1,0:T(8,128)(2,1)} %w_ref.3, bf16[4,2,336,128]{3,2,1,0:T(8,128)(2,1)} %pad_maximum_fusion.gate.p0), custom_call_target="tpu_custom_call" | custom-call | flops 1 | bytes 1 | tf_op jit(solution)/shard_map/pallas_call | solution.py:354
  71.5 1.7 %collective-permute-start.20 = (bf16[1344,512]{1,0:T(8,128)(2,1)}, bf16[1344,512]{1,0:T(8,128)(2,1)}, u32[]{:S(2)}, u32[]{:S(2)}) collective-permute-start(bf16[1344,512]{1,0:T(8,128)(2,1)} %get-tuple-element.47.refs_2_), channel_id=1, source_target_pairs={{0,1},{1,0},{2,3},{3,2},{4,5},{5,4},{6,7},{7,6},{8,9},{9,8},{10,11... | collective-permute-start | bytes 4128776 | tf_op jit(solution)/shard_map/ppermute | solution.py:42
  73.2 2.9 %collective-permute-done.12.two_back = bf16[512,512]{1,0:T(8,128)(2,1)} collective-permute-done((bf16[512,512]{1,0:T(8,128)(2,1)}, bf16[512,512]{1,0:T(8,128)(2,1)}, u32[]{:S(2)}, u32[]{:S(2)}) %collective-permute-start.12) | collective-permute-done | bytes 524320 | tf_op jit(solution)/shard_map/ppermute | solution.py:84
  76.1 12.1 %collective-permute-done.11.one_back = bf16[512,512]{1,0:T(8,128)(2,1)} collective-permute-done((bf16[512,512]{1,0:T(8,128)(2,1)}, bf16[512,512]{1,0:T(8,128)(2,1)}, u32[]{:S(2)}, u32[]{:S(2)}) %collective-permute-start.11) | collective-permute-done | bytes 524320 | tf_op jit(solution)/shard_map/ppermute | solution.py:84
  88.2 9.2 %shard_map.114.c0 = bf16[512,512]{1,0:T(8,128)(2,1)} custom-call(s32[9]{0:T(128)} %stack.75.where.order, s32[4]{0:T(128)} %ids.3, s32[8]{0:T(128)} %lengths.3, s32[4]{0:T(128)} %reals.1, bf16[512,512]{1,0:T(8,128)(2,1)} %get-tuple-element.38.q_ref, bf16[512,512]{1,0:T(8,128)(2,1)} %get-tuple-element.39.own, ...), custom_call_target="tpu_custom_call" | custom-call | flops 1 | bytes 1 | tf_op jit(solution)/shard_map/pallas_call | solution.py:294
  97.5 1.7 %collective-permute-start.18 = (bf16[512,512]{1,0:T(8,128)(2,1)}, bf16[512,512]{1,0:T(8,128)(2,1)S(1)}, u32[]{:S(2)}, u32[]{:S(2)}) collective-permute-start(bf16[512,512]{1,0:T(8,128)(2,1)} %shard_map.114.c0), channel_id=1, source_target_pairs={{0,2},{1,3},{2,0},{3,1},{4,6},{5,7},{6,4},{7,5},{8,10},{9,11},{10,... | collective-permute-start | bytes 1572872 | tf_op jit(solution)/shard_map/ppermute | solution.py:42
  99.1 2.1 %collective-permute-start.23 = (bf16[4,2,336,128]{3,2,1,0:T(8,128)(2,1)}, bf16[4,2,336,128]{3,2,1,0:T(8,128)(2,1)S(1)}, u32[]{:S(2)}, u32[]{:S(2)}) collective-permute-start(bf16[4,2,336,128]{3,2,1,0:T(8,128)(2,1)} %pad_maximum_fusion.gate.p0), channel_id=1, source_target_pairs={{0,96},{4,100},{8,104},{12,108},{16,112},{20,116},{24,120},{28,124... | collective-permute-start | bytes 2064392 | tf_op jit(solution)/shard_map/ppermute | solution.py:56
  101.2 0.0 collective-permute-start.22
  101.2 2.6 %collective-permute-start.17 = (bf16[512,512]{1,0:T(8,128)(2,1)}, bf16[512,512]{1,0:T(8,128)(2,1)S(1)}, u32[]{:S(2)}, u32[]{:S(2)}) collective-permute-start(bf16[512,512]{1,0:T(8,128)(2,1)} %shard_map.114.c0), channel_id=1, source_target_pairs={{0,1},{1,0},{2,3},{3,2},{4,5},{5,4},{6,7},{7,6},{8,9},{9,8},{10,11... | collective-permute-start | bytes 1572872 | tf_op jit(solution)/shard_map/ppermute | solution.py:42
  103.8 6.8 %collective-permute-done.18.c2 = bf16[512,512]{1,0:T(8,128)(2,1)S(1)} collective-permute-done((bf16[512,512]{1,0:T(8,128)(2,1)}, bf16[512,512]{1,0:T(8,128)(2,1)S(1)}, u32[]{:S(2)}, u32[]{:S(2)}) %collective-permute-start.18) | collective-permute-done | bytes 524320 | tf_op jit(solution)/shard_map/ppermute | solution.py:42
  110.6 3.0 %collective-permute-start.19 = (bf16[512,512]{1,0:T(8,128)(2,1)S(1)}, bf16[512,512]{1,0:T(8,128)(2,1)S(1)}, u32[]{:S(2)}, u32[]{:S(2)}) collective-permute-start(bf16[512,512]{1,0:T(8,128)(2,1)S(1)} %collective-permute-done.18.c2), channel_id=1, source_target_pairs={{0,1},{1,0},{2,3},{3,2},{4,5},{5,4},{6,7},{7,6},{8,9},{9,8},{10,11... | collective-permute-start | bytes 1572872 | tf_op jit(solution)/shard_map/ppermute | solution.py:42
  113.6 0.3 collective-permute-done.23.p3
  114.0 3.0 %collective-permute-done.22.p2 = bf16[4,2,336,128]{3,2,1,0:T(8,128)(2,1)S(1)} collective-permute-done((bf16[4,2,336,128]{3,2,1,0:T(8,128)(2,1)}, bf16[4,2,336,128]{3,2,1,0:T(8,128)(2,1)S(1)}, u32[]{:S(2)}, u32[]{:S(2)}) %collective-permute-start.22) | collective-permute-done | bytes 688160 | tf_op jit(solution)/shard_map/ppermute | solution.py:56
  117.0 0.0 collective-permute-done.20.w1
  117.0 0.8 copy-done.5
  117.8 0.8 copy-done.8
  118.7 8.5 %shard_map.115 = (f32[1344,512]{1,0:T(8,128)}, f32[1,512]{1,0:T(1,128)}) custom-call(s32[9]{0:T(128)} %stack.75.where.order, bf16[512,512]{1,0:T(8,128)(2,1)} %shard_map.114.c0, bf16[512,512]{1,0:T(8,128)(2,1)} %copy-done.7, bf16[512,512]{1,0:T(8,128)(2,1)} %copy-done.6, bf16[512,512]{1,0:T(8,128)(2,1)} %copy-done.8, ...), custom_call_target="tpu_custom_call" | custom-call | flops 2818572288 | bytes 8000000 | tf_op jit(solution)/shard_map/pallas_call | solution.py:439
  127.1 4.8 %collective-permute-start.26 = (f32[1,512]{1,0:T(1,128)}, f32[1,512]{1,0:T(1,128)S(1)}, u32[]{:S(2)}, u32[]{:S(2)}) collective-permute-start(f32[1,512]{1,0:T(1,128)} %get-tuple-element.50), channel_id=1, source_target_pairs={{0,3},{1,2},{2,1},{3,0},{4,7},{5,6},{6,5},{7,4},{8,11},{9,10},{10,... | collective-permute-start | bytes 6152 | tf_op jit(solution)/shard_map/ppermute | solution.py:42
  132.0 1.6 %collective-permute-start.25 = (f32[1,512]{1,0:T(1,128)}, f32[1,512]{1,0:T(1,128)S(1)}, u32[]{:S(2)}, u32[]{:S(2)}) collective-permute-start(f32[1,512]{1,0:T(1,128)} %get-tuple-element.50), channel_id=1, source_target_pairs={{0,2},{1,3},{2,0},{3,1},{4,6},{5,7},{6,4},{7,5},{8,10},{9,11},{10,... | collective-permute-start | bytes 6152 | tf_op jit(solution)/shard_map/ppermute | solution.py:42
  133.6 2.6 %collective-permute-done.25 = f32[1,512]{1,0:T(1,128)S(1)} collective-permute-done((f32[1,512]{1,0:T(1,128)}, f32[1,512]{1,0:T(1,128)S(1)}, u32[]{:S(2)}, u32[]{:S(2)}) %collective-permute-start.25) | collective-permute-done | bytes 2080 | tf_op jit(solution)/shard_map/ppermute | solution.py:42
  136.1 0.0 collective-permute-done.24
  136.1 0.7 add_rsqrt_fusion
  136.8 3.7 %fusion = bf16[512,1344]{0,1:T(8,128)(2,1)} fusion(f32[1344,512]{1,0:T(8,128)} %get-tuple-element.49, f32[512]{0:T(512)S(1)} %bitcast.34, f32[1344]{0:T(1024)S(1)} %copy-done.3, bf16[512,1344]{0,1:T(8,128)(2,1)} %param.11), kind=kLoop, calls=%fused_computation.1 | loop fusion | flops 3440640 | bytes 5512448 | tf_op jit(solution)/shard_map/transpose | solution.py:531
  (28 shorter events, 0.1 us)
Async XLA Ops:
  0.0 5.1 %collective-permute-start.1 = (bf16[1344,512]{1,0:T(8,128)(2,1)}, bf16[1344,512]{1,0:T(8,128)(2,1)}, u32[]{:S(2)}, u32[]{:S(2)}) collective-permute-start(bf16[1344,512]{1,0:T(8,128)(2,1)} %bitcast.23), channel_id=1, source_target_pairs={{0,1},{1,0},{2,3},{3,2},{4,5},{5,4},{6,7},{7,6},{8,9},{9,8},{10,11... | collective-permute-start | bytes 4128776 | tf_op jit(solution)/shard_map/ppermute | solution.py:42
  1.4 39.0 %collective-permute-start = (bf16[1344,512]{1,0:T(8,128)(2,1)}, bf16[1344,512]{1,0:T(8,128)(2,1)}, u32[]{:S(2)}, u32[]{:S(2)}) collective-permute-start(bf16[1344,512]{1,0:T(8,128)(2,1)} %bitcast.24), channel_id=1, source_target_pairs={{0,2},{1,3},{2,0},{3,1},{4,6},{5,7},{6,4},{7,5},{8,10},{9,11},{10,... | collective-permute-start | bytes 4128776 | tf_op jit(solution)/shard_map/ppermute | solution.py:42
  9.1 20.3 %collective-permute-start.5 = (bf16[128,512]{1,0:T(8,128)(2,1)}, bf16[128,512]{1,0:T(8,128)(2,1)S(1)}, u32[]{:S(2)}, u32[]{:S(2)}) collective-permute-start(bf16[128,512]{1,0:T(8,128)(2,1)} %get-tuple-element.32), channel_id=1, source_target_pairs={{0,64},{4,68},{8,72},{12,76},{16,80},{20,84},{24,88},{28,92},{32,9... | collective-permute-start | bytes 393224 | tf_op jit(solution)/shard_map/ppermute | solution.py:56
  11.9 17.5 %collective-permute-start.6 = (bf16[128,512]{1,0:T(8,128)(2,1)}, bf16[128,512]{1,0:T(8,128)(2,1)S(1)}, u32[]{:S(2)}, u32[]{:S(2)}) collective-permute-start(bf16[128,512]{1,0:T(8,128)(2,1)} %get-tuple-element.33), channel_id=1, source_target_pairs={{0,96},{4,100},{8,104},{12,108},{16,112},{20,116},{24,120},{28,124... | collective-permute-start | bytes 393224 | tf_op jit(solution)/shard_map/ppermute | solution.py:56
  12.7 16.7 %collective-permute-start.4 = (bf16[128,512]{1,0:T(8,128)(2,1)}, bf16[128,512]{1,0:T(8,128)(2,1)S(1)}, u32[]{:S(2)}, u32[]{:S(2)}) collective-permute-start(bf16[128,512]{1,0:T(8,128)(2,1)} %get-tuple-element.28.gate), channel_id=1, source_target_pairs={{0,32},{4,36},{8,40},{12,44},{16,48},{20,52},{24,56},{28,60},{32,6... | collective-permute-start | bytes 393224 | tf_op jit(solution)/shard_map/ppermute | solution.py:56
  17.9 11.5 %copy-start.2 = (bf16[128,512]{1,0:T(8,128)(2,1)S(1)}, bf16[128,512]{1,0:T(8,128)(2,1)}, u32[]{:S(2)}) copy-start(bf16[128,512]{1,0:T(8,128)(2,1)} %get-tuple-element.31) | copy-start | bytes 393220
  17.9 16.1 %copy-start.1 = (f32[512,128]{1,0:T(8,128)S(1)}, f32[512,128]{1,0:T(8,128)}, u32[]{:S(2)}) copy-start(f32[512,128]{1,0:T(8,128)} %get-tuple-element.36) | copy-start | bytes 786436
  17.9 20.1 %copy-start.9 = (bf16[336,128]{1,0:T(8,128)(2,1)S(1)}, bf16[336,128]{1,0:T(8,128)(2,1)}, u32[]{:S(2)}) copy-start(bf16[336,128]{1,0:T(8,128)(2,1)} %get-tuple-element.30) | copy-start | bytes 258052
  17.9 25.5 %collective-permute-start.2 = (bf16[336,128]{1,0:T(8,128)(2,1)}, bf16[336,128]{1,0:T(8,128)(2,1)S(1)}, u32[]{:S(2)}, u32[]{:S(2)}) collective-permute-start(bf16[336,128]{1,0:T(8,128)(2,1)} %get-tuple-element.29.refs_6_), channel_id=1, source_target_pairs={{0,2},{1,3},{2,0},{3,1},{4,6},{5,7},{6,4},{7,5},{8,10},{9,11},{10,... | collective-permute-start | bytes 258056 | tf_op jit(solution)/shard_map/ppermute | solution.py:42
  29.5 8.5 %collective-permute-start.9 = (bf16[128,512]{1,0:T(8,128)(2,1)S(1)}, bf16[128,512]{1,0:T(8,128)(2,1)S(1)}, u32[]{:S(2)}, u32[]{:S(2)}) collective-permute-start(bf16[128,512]{1,0:T(8,128)(2,1)S(1)} %add_add_fusion), channel_id=1, source_target_pairs={{0,12},{4,8},{8,4},{12,0},{16,28},{20,24},{24,20},{28,16},{32,44},... | collective-permute-start | bytes 393224 | tf_op jit(solution)/shard_map/ppermute | solution.py:75
  33.3 7.0 %collective-permute-start.8 = (bf16[128,512]{1,0:T(8,128)(2,1)S(1)}, bf16[128,512]{1,0:T(8,128)(2,1)S(1)}, u32[]{:S(2)}, u32[]{:S(2)}) collective-permute-start(bf16[128,512]{1,0:T(8,128)(2,1)S(1)} %add_add_fusion), channel_id=1, source_target_pairs={{0,8},{4,12},{8,0},{12,4},{16,24},{20,28},{24,16},{28,20},{32,40},... | collective-permute-start | bytes 393224 | tf_op jit(solution)/shard_map/ppermute | solution.py:75
  33.3 7.0 %collective-permute-start.7 = (bf16[128,512]{1,0:T(8,128)(2,1)S(1)}, bf16[128,512]{1,0:T(8,128)(2,1)S(1)}, u32[]{:S(2)}, u32[]{:S(2)}) collective-permute-start(bf16[128,512]{1,0:T(8,128)(2,1)S(1)} %add_add_fusion), channel_id=1, source_target_pairs={{0,4},{4,0},{8,12},{12,8},{16,20},{20,16},{24,28},{28,24},{32,36},... | collective-permute-start | bytes 393224 | tf_op jit(solution)/shard_map/ppermute | solution.py:75
  38.0 5.4 %collective-permute-start.3 = (bf16[336,128]{1,0:T(8,128)(2,1)S(1)}, bf16[336,128]{1,0:T(8,128)(2,1)S(1)}, u32[]{:S(2)}, u32[]{:S(2)}) collective-permute-start(bf16[336,128]{1,0:T(8,128)(2,1)S(1)} %copy-done.9), channel_id=1, source_target_pairs={{0,3},{1,2},{2,1},{3,0},{4,7},{5,6},{6,5},{7,4},{8,11},{9,10},{10,... | collective-permute-start | bytes 258056 | tf_op jit(solution)/shard_map/ppermute | solution.py:42
  40.4 20.1 %copy-start = (bf16[4,128,512]{2,1,0:T(8,128)(2,1)}, bf16[4,128,512]{2,1,0:T(8,128)(2,1)S(1)}, u32[]{:S(2)}) copy-start(bf16[4,128,512]{2,1,0:T(8,128)(2,1)S(1)} %pad_maximum_fusion.1.refs_0_) | copy-start | bytes 1572868
  43.5 6.9 %collective-permute-start.10 = (bf16[1344,512]{1,0:T(8,128)(2,1)}, bf16[1344,512]{1,0:T(8,128)(2,1)}, u32[]{:S(2)}, u32[]{:S(2)}) collective-permute-start(bf16[1344,512]{1,0:T(8,128)(2,1)} %collective-permute-done.refs_0_), channel_id=1, source_target_pairs={{0,1},{1,0},{2,3},{3,2},{4,5},{5,4},{6,7},{7,6},{8,9},{9,8},{10,11... | collective-permute-start | bytes 4128776 | tf_op jit(solution)/shard_map/ppermute | solution.py:42
  45.3 17.6 %collective-permute-start.16 = (bf16[2,336,128]{2,1,0:T(8,128)(2,1)S(1)}, bf16[2,336,128]{2,1,0:T(8,128)(2,1)S(1)}, u32[]{:S(2)}, u32[]{:S(2)}) collective-permute-start(bf16[2,336,128]{2,1,0:T(8,128)(2,1)S(1)} %pad_maximum_fusion.2), channel_id=1, source_target_pairs={{0,12},{4,0},{8,4},{12,8},{16,28},{20,16},{24,20},{28,24},{32,44},... | collective-permute-start | bytes 516104 | tf_op jit(solution)/shard_map/ppermute | solution.py:66
  49.3 13.8 %collective-permute-start.15 = (bf16[2,336,128]{2,1,0:T(8,128)(2,1)S(1)}, bf16[2,336,128]{2,1,0:T(8,128)(2,1)}, u32[]{:S(2)}, u32[]{:S(2)}) collective-permute-start(bf16[2,336,128]{2,1,0:T(8,128)(2,1)S(1)} %pad_maximum_fusion.2), channel_id=1, source_target_pairs={{0,8},{4,12},{8,0},{12,4},{16,24},{20,28},{24,16},{28,20},{32,40},... | collective-permute-start | bytes 516104 | tf_op jit(solution)/shard_map/ppermute | solution.py:66
  49.3 13.8 %collective-permute-start.14 = (bf16[2,336,128]{2,1,0:T(8,128)(2,1)S(1)}, bf16[2,336,128]{2,1,0:T(8,128)(2,1)}, u32[]{:S(2)}, u32[]{:S(2)}) collective-permute-start(bf16[2,336,128]{2,1,0:T(8,128)(2,1)S(1)} %pad_maximum_fusion.2), channel_id=1, source_target_pairs={{0,4},{4,8},{8,12},{12,0},{16,20},{20,24},{24,28},{28,16},{32,36},... | collective-permute-start | bytes 516104 | tf_op jit(solution)/shard_map/ppermute | solution.py:66
  50.0 23.2 %collective-permute-start.13 = (bf16[4,128,512]{2,1,0:T(8,128)(2,1)S(1)}, bf16[4,128,512]{2,1,0:T(8,128)(2,1)}, u32[]{:S(2)}, u32[]{:S(2)}) collective-permute-start(bf16[4,128,512]{2,1,0:T(8,128)(2,1)S(1)} %pad_maximum_fusion.1.refs_0_), channel_id=1, source_target_pairs={{0,16},{4,20},{8,24},{12,28},{16,0},{20,4},{24,8},{28,12},{32,48},... | collective-permute-start | bytes 1572872 | tf_op jit(solution)/shard_map/ppermute | solution.py:71
  60.5 15.6 %collective-permute-start.12 = (bf16[512,512]{1,0:T(8,128)(2,1)}, bf16[512,512]{1,0:T(8,128)(2,1)}, u32[]{:S(2)}, u32[]{:S(2)}) collective-permute-start(bf16[512,512]{1,0:T(8,128)(2,1)} %get-tuple-element.39.own), channel_id=1, source_target_pairs={{0,8},{4,12},{8,16},{12,20},{16,24},{20,28},{24,0},{28,4},{32,40},... | collective-permute-start | bytes 1572872 | tf_op jit(solution)/shard_map/ppermute | solution.py:84
  62.9 25.3 %collective-permute-start.11 = (bf16[512,512]{1,0:T(8,128)(2,1)}, bf16[512,512]{1,0:T(8,128)(2,1)}, u32[]{:S(2)}, u32[]{:S(2)}) collective-permute-start(bf16[512,512]{1,0:T(8,128)(2,1)} %get-tuple-element.39.own), channel_id=1, source_target_pairs={{0,4},{4,8},{8,12},{12,16},{16,20},{20,24},{24,28},{28,0},{32,36},... | collective-permute-start | bytes 1572872 | tf_op jit(solution)/shard_map/ppermute | solution.py:84
  65.1 36.1 %collective-permute-start.21 = (bf16[4,2,336,128]{3,2,1,0:T(8,128)(2,1)}, bf16[4,2,336,128]{3,2,1,0:T(8,128)(2,1)}, u32[]{:S(2)}, u32[]{:S(2)}) collective-permute-start(bf16[4,2,336,128]{3,2,1,0:T(8,128)(2,1)} %pad_maximum_fusion.gate.p0), channel_id=1, source_target_pairs={{0,32},{4,36},{8,40},{12,44},{16,48},{20,52},{24,56},{28,60},{32,6... | collective-permute-start | bytes 2064392 | tf_op jit(solution)/shard_map/ppermute | solution.py:56
  71.5 45.5 %collective-permute-start.20 = (bf16[1344,512]{1,0:T(8,128)(2,1)}, bf16[1344,512]{1,0:T(8,128)(2,1)}, u32[]{:S(2)}, u32[]{:S(2)}) collective-permute-start(bf16[1344,512]{1,0:T(8,128)(2,1)} %get-tuple-element.47.refs_2_), channel_id=1, source_target_pairs={{0,1},{1,0},{2,3},{3,2},{4,5},{5,4},{6,7},{7,6},{8,9},{9,8},{10,11... | collective-permute-start | bytes 4128776 | tf_op jit(solution)/shard_map/ppermute | solution.py:42
  97.5 13.2 %collective-permute-start.18 = (bf16[512,512]{1,0:T(8,128)(2,1)}, bf16[512,512]{1,0:T(8,128)(2,1)S(1)}, u32[]{:S(2)}, u32[]{:S(2)}) collective-permute-start(bf16[512,512]{1,0:T(8,128)(2,1)} %shard_map.114.c0), channel_id=1, source_target_pairs={{0,2},{1,3},{2,0},{3,1},{4,6},{5,7},{6,4},{7,5},{8,10},{9,11},{10,... | collective-permute-start | bytes 1572872 | tf_op jit(solution)/shard_map/ppermute | solution.py:42
  99.1 14.8 %collective-permute-start.23 = (bf16[4,2,336,128]{3,2,1,0:T(8,128)(2,1)}, bf16[4,2,336,128]{3,2,1,0:T(8,128)(2,1)S(1)}, u32[]{:S(2)}, u32[]{:S(2)}) collective-permute-start(bf16[4,2,336,128]{3,2,1,0:T(8,128)(2,1)} %pad_maximum_fusion.gate.p0), channel_id=1, source_target_pairs={{0,96},{4,100},{8,104},{12,108},{16,112},{20,116},{24,120},{28,124... | collective-permute-start | bytes 2064392 | tf_op jit(solution)/shard_map/ppermute | solution.py:56
  101.2 15.7 %collective-permute-start.22 = (bf16[4,2,336,128]{3,2,1,0:T(8,128)(2,1)}, bf16[4,2,336,128]{3,2,1,0:T(8,128)(2,1)S(1)}, u32[]{:S(2)}, u32[]{:S(2)}) collective-permute-start(bf16[4,2,336,128]{3,2,1,0:T(8,128)(2,1)} %collective-permute-done.21.p1), channel_id=1, source_target_pairs={{0,32},{4,36},{8,40},{12,44},{16,48},{20,52},{24,56},{28,60},{32,6... | collective-permute-start | bytes 2064392 | tf_op jit(solution)/shard_map/ppermute | solution.py:56
  101.2 12.7 %collective-permute-start.17 = (bf16[512,512]{1,0:T(8,128)(2,1)}, bf16[512,512]{1,0:T(8,128)(2,1)S(1)}, u32[]{:S(2)}, u32[]{:S(2)}) collective-permute-start(bf16[512,512]{1,0:T(8,128)(2,1)} %shard_map.114.c0), channel_id=1, source_target_pairs={{0,1},{1,0},{2,3},{3,2},{4,5},{5,4},{6,7},{7,6},{8,9},{9,8},{10,11... | collective-permute-start | bytes 1572872 | tf_op jit(solution)/shard_map/ppermute | solution.py:42
  110.6 6.3 %copy-start.6 = (bf16[512,512]{1,0:T(8,128)(2,1)}, bf16[512,512]{1,0:T(8,128)(2,1)S(1)}, u32[]{:S(2)}) copy-start(bf16[512,512]{1,0:T(8,128)(2,1)S(1)} %collective-permute-done.18.c2) | copy-start | bytes 1572868
  110.6 6.3 %collective-permute-start.19 = (bf16[512,512]{1,0:T(8,128)(2,1)S(1)}, bf16[512,512]{1,0:T(8,128)(2,1)S(1)}, u32[]{:S(2)}, u32[]{:S(2)}) collective-permute-start(bf16[512,512]{1,0:T(8,128)(2,1)S(1)} %collective-permute-done.18.c2), channel_id=1, source_target_pairs={{0,1},{1,0},{2,3},{3,2},{4,5},{5,4},{6,7},{7,6},{8,9},{9,8},{10,11... | collective-permute-start | bytes 1572872 | tf_op jit(solution)/shard_map/ppermute | solution.py:42
  114.0 4.7 %copy-start.4 = (bf16[4,2,336,128]{3,2,1,0:T(8,128)(2,1)}, bf16[4,2,336,128]{3,2,1,0:T(8,128)(2,1)S(1)}, u32[]{:S(2)}) copy-start(bf16[4,2,336,128]{3,2,1,0:T(8,128)(2,1)S(1)} %collective-permute-done.23.p3) | copy-start | bytes 2064388
  114.0 3.0 %copy-start.7 = (bf16[512,512]{1,0:T(8,128)(2,1)}, bf16[512,512]{1,0:T(8,128)(2,1)S(1)}, u32[]{:S(2)}) copy-start(bf16[512,512]{1,0:T(8,128)(2,1)S(1)} %collective-permute-done.17.c1) | copy-start | bytes 1572868
  117.0 0.9 copy-start.5
  117.8 0.8 copy-start.8
  118.7 18.1 %copy-start.3 = (f32[1344]{0:T(1024)S(1)}, f32[1344]{0:T(1024)}, u32[]{:S(2)}) copy-start(f32[1344]{0:T(1024)} %param.17) | copy-start | bytes 16132
  127.1 6.4 %collective-permute-start.26 = (f32[1,512]{1,0:T(1,128)}, f32[1,512]{1,0:T(1,128)S(1)}, u32[]{:S(2)}, u32[]{:S(2)}) collective-permute-start(f32[1,512]{1,0:T(1,128)} %get-tuple-element.50), channel_id=1, source_target_pairs={{0,3},{1,2},{2,1},{3,0},{4,7},{5,6},{6,5},{7,4},{8,11},{9,10},{10,... | collective-permute-start | bytes 6152 | tf_op jit(solution)/shard_map/ppermute | solution.py:42
  132.0 4.2 %collective-permute-start.25 = (f32[1,512]{1,0:T(1,128)}, f32[1,512]{1,0:T(1,128)S(1)}, u32[]{:S(2)}, u32[]{:S(2)}) collective-permute-start(f32[1,512]{1,0:T(1,128)} %get-tuple-element.50), channel_id=1, source_target_pairs={{0,2},{1,3},{2,0},{3,1},{4,6},{5,7},{6,4},{7,5},{8,10},{9,11},{10,... | collective-permute-start | bytes 6152 | tf_op jit(solution)/shard_map/ppermute | solution.py:42
  133.5 2.6 %collective-permute-start.24 = (f32[1,512]{1,0:T(1,128)}, f32[1,512]{1,0:T(1,128)S(1)}, u32[]{:S(2)}, u32[]{:S(2)}) collective-permute-start(f32[1,512]{1,0:T(1,128)} %get-tuple-element.50), channel_id=1, source_target_pairs={{0,1},{1,0},{2,3},{3,2},{4,5},{5,4},{6,7},{7,6},{8,9},{9,8},{10,11... | collective-permute-start | bytes 6152 | tf_op jit(solution)/shard_map/ppermute | solution.py:42

commit v5 on v4

--- a/solution.py
+++ b/solution.py
@@ -95,16 +95,16 @@
 IN_HBM = pl.BlockSpec(memory_space=pltpu.HBM)
 
 
-def project_kernel(chunks, first, last, order, *refs):
+def project_kernel(chunks, groups, first, kind, order, *refs):
     step = pl.program_id(0)
-    xs, refs = refs[:chunks], refs[chunks:]
-    gain, wq, wk, wv = refs[:4]
-    if last:
-        acc_in, squares_in, cosine, sine, q_ref, kv_ref, acc, squares = refs[-8:]
-    elif first:
-        acc, squares = refs[-2:]
+    count = sum(groups)
+    xs, gain, weights = refs[:chunks], refs[chunks], refs[chunks + 1 : chunks + 1 + count]
+    held = len(groups) + 1
+    accs = refs[-held:]
+    if kind:
+        carried, cosine, sine, out = refs[-2 * held - 3 : -held - 3], *refs[-held - 3 : -held]
     else:
-        acc_in, squares_in, acc, squares = refs[-4:]
+        carried = (None,) * held if first else refs[-2 * held : -held]
 
     for number in range(chunks):
 
@@ -112,68 +112,60 @@
         def _(number=number):
             x = jnp.transpose(xs[number][...]).astype(F32)
             scaled = (x * gain[0]).astype(BF16)
-            parts = (
-                jnp.dot(scaled, wq[...], preferred_element_type=F32),
-                jnp.dot(scaled, wk[...], preferred_element_type=F32),
-                jnp.dot(scaled, wv[...], preferred_element_type=F32),
-                jnp.broadcast_to(jnp.sum(x * x, 1, keepdims=True), squares.shape),
-            )
+            parts = [jnp.dot(scaled, w[...], preferred_element_type=F32) for w in weights]
+            square = jnp.broadcast_to(jnp.sum(x * x, 1, keepdims=True), accs[-1].shape)
 
             def put(sources):
                 at = 0
-                for part, source in zip(parts[:3], sources):
-                    cols = slice(at, at + part.shape[1])
-                    acc[:, cols] = part if source is None else source[:, cols] + part
-                    at = cols.stop
-                squares[...] = parts[3] if sources[3] is None else sources[3][...] + parts[3]
+                for group, acc, source in zip(groups, accs, sources):
+                    left = 0
+                    for part in parts[at : at + group]:
+                        cols = slice(left, left + part.shape[1])
+                        acc[:, cols] = part if source is None else source[:, cols] + part
+                        left = cols.stop
+                    at += group
+                accs[-1][...] = square if sources[-1] is None else sources[-1][...] + square
 
             if number:
-                put((acc, acc, acc, squares))
+                put(accs)
             else:
 
                 @pl.when(step == 0)
                 def _():
-                    put((None,) * 4 if first else (acc_in, acc_in, acc_in, squares_in))
+                    put(carried)
 
                 @pl.when(step == 1)
                 def _():
-                    put((acc, acc, acc, squares))
-
-    if last:
+                    put(accs)
+
+    if kind:
 
         @pl.when(step == 2 * chunks - 1)
         def _():
-            scale = lax.rsqrt(squares[...] * (1.0 / (MP * FEATURES)) + epsilon)
-            cos_all = cosine[...]
-            sin_all = sine[...]
-            for head in range(6):
+            scale = lax.rsqrt(accs[-1][...] * (1.0 / (MP * FEATURES)) + epsilon)
+            for head in range(4):
                 cols = slice(head * HEAD_DIM, (head + 1) * HEAD_DIM)
-                part = acc[:, cols] * scale
-                turned = part * cos_all + pltpu.roll(part, 64, 1) * sin_all
-                if head < HEADS_LOCAL:
-                    q_ref[:, cols] = (turned * query_scalar ** (-0.5)).astype(BF16)
-                else:
-                    at = (head - HEADS_LOCAL) * HEAD_DIM
-                    kv_ref[:, at : at + HEAD_DIM] = turned.astype(BF16)
-            for head in range(2):
-                at = KV_WIDTH + head * HEAD_DIM
-                part = acc[:, 768 + head * HEAD_DIM : 896 + head * HEAD_DIM] * scale
-                kv_ref[:, at : at + HEAD_DIM] = part.astype(BF16)
-
-
-def project(order, start, xs, gain, weights, gates=(), carried=(), tables=()):
+                part = accs[0][:, cols] * scale
+                if kind == "queries" or head < 2:
+                    part = part * cosine[...] + pltpu.roll(part, 64, 1) * sine[...]
+                if kind == "queries":
+                    part = part * query_scalar ** (-0.5)
+                out[:, cols] = part.astype(BF16)
+
+
+def project(order, start, xs, gain, weights, groups, gates=(), carried=(), tables=(), kind=None):
     chunks = len(xs)
     full = lambda shape: pl.BlockSpec(shape, lambda i, order: (0,) * len(shape))
     at = lambda i, order: order[5 + start + i // 2] * 2 + i % 2
-    acc_shapes = [(ROWS, 1024), (ROWS, HEAD_DIM)]
-    if tables:
-        out_shape = [jax.ShapeDtypeStruct((ROWS, 512), BF16)] * 2
+    acc_shapes = [(ROWS, 512)] * len(groups) + [(ROWS, HEAD_DIM)]
+    if kind:
+        out_shape = [jax.ShapeDtypeStruct((ROWS, 512), BF16)]
         scratch = [pltpu.VMEM(shape, F32) for shape in acc_shapes]
     else:
         out_shape = [jax.ShapeDtypeStruct(shape, F32) for shape in acc_shapes]
         scratch = []
     return pl.pallas_call(
-        functools.partial(project_kernel, chunks, not carried, bool(tables)),
+        functools.partial(project_kernel, chunks, groups, not carried, kind),
         grid_spec=pltpu.PrefetchScalarGridSpec(
             num_scalar_prefetch=1,
             grid=(2 * chunks,),
@@ -182,10 +174,7 @@
                 for k in range(chunks)
             ]
             + [pl.BlockSpec((1, 1, STEP), lambda i, order: (at(i, order), 0, 0))]
-            + [
-                pl.BlockSpec((STEP, width), lambda i, order: (at(i, order), 0))
-                for width in (512, 256, 256)
-            ]
+            + [pl.BlockSpec((STEP, w.shape[1]), lambda i, order: (at(i, order), 0)) for w in weights]
             + [IN_HBM] * len(gates)
             + [full(one.shape) for one in (*carried, *tables)],
             out_specs=[full(one.shape) for one in out_shape],
@@ -193,7 +182,7 @@
         ),
         out_shape=out_shape,
         compiler_params=params(),
-        cost_estimate=cost(6_000_000_000, 20_000_000) if tables else cost(1, 1),
+        cost_estimate=cost(3_000_000_000, 10_000_000) if kind else cost(1, 1),
     )(order, *xs, gain, *weights, *gates, *carried, *tables)
 
 
@@ -490,28 +479,39 @@
     places, mine, *others = picked_rows(*scalars, prefix_cache, near)
     for by, other in enumerate(others, 1):
         mine = mine + along_x(other, by)
-    prefix = jnp.stack([mine] + [z_flip(mine, flip) for flip in (1, 2, 3)])
     tables = rope_tables(places)
 
     piece_a, piece_b = turned_pieces(where, w_out, others[0])
     crossed = (across_mp(piece_a, 2), across_mp(piece_b, 3))
 
     gain = gain_pre.reshape(2 * MP, 1, STEP)
-    weights = (w_query, w_key, w_value)
-    carried = project(where, 0, [turned_tokens, near], gain, weights, (piece_a,))
-    far, piece_a, piece_b, prefix, *_ = lax.optimization_barrier(
-        (far, *crossed, prefix, *carried, *tables)
-    )
-    w_piece = jnp.stack([piece_a, piece_b])
+    carried = project(
+        where,
+        0,
+        [turned_tokens, near],
+        gain,
+        (w_query, w_key, w_value),
+        (1, 2),
+        (piece_a,),
+    )
+    mine = after(mine, carried[2])
+    prefix_parts = [mine] + [z_flip(mine, flip) for flip in (1, 2, 3)]
+    far, *parts = lax.optimization_barrier((far, *crossed, *prefix_parts, *carried, *tables))
+    w_piece = jnp.stack(parts[:2])
+    prefix = jnp.stack(parts[2:6])
     prefix_twin = to_twin(prefix)
-    queries, own = project(
-        where, 2, [far, across_mp(far, 1)], gain, weights, (), carried, tables
-    )
     w_parts = [w_piece] + [along_z(w_piece, by) for by in (1, 2, 3)]
+    fars = [far, across_mp(far, 1)]
+    (own,) = project(
+        where, 2, fars, gain, (w_key, w_value), (2,), (), carried[1:], tables, "keys"
+    )
     one_back = within_doc(own, 1)
     two_back = within_doc(own, 2)
-    w_parts = lax.optimization_barrier((*w_parts, own))[:4]
-    w_line = jnp.stack(w_parts)
+    (queries,) = project(
+        where, 2, fars, gain, (w_query,), (1,), (own,), carried[::2], tables, "queries"
+    )
+
+    w_line = jnp.stack(lax.optimization_barrier((*w_parts, queries))[:4])
     w_next = along_x(w_line, 1)
     w_far = [w_line, w_next, along_x(w_next, 1), along_x(w_line, 3)]
     w_own, w_give = turned_weights(where, w_out, w_line)

time: 141 us -> 137 us (0.972)
  waiting for transfers between devices: 33.2 us -> 26.1 us
  Pallas kernels: 50 us -> 54.7 us
  starting transfers between devices: 45.3 us -> 43.3 us
    ppermute x2, waiting for transfers between devices: 15 us -> 8.7 us  [within_doc(): return lax.ppermute(array, 'seq', pairs)]
    pallas_call x2 -> x3, Pallas kernels: 19.1 us -> 23.9 us  [project(): pl.pallas_call(functools.partial(project_kernel, chunks, groups, not carr...]
    ppermute x12, waiting for transfers between devices: 12.5 us -> 8.9 us  [across_mp(): return lax.ppermute(array, 'mp', [(i, i ^ flip) for i in range(MP)])]
    ppermute x12, starting transfers between devices: 26.4 us -> 23.5 us  [across_mp(): return lax.ppermute(array, 'mp', [(i, i ^ flip) for i in range(MP)])]
    ppermute x3, waiting for transfers between devices: 2.37 us -> 3.89 us  [z_flip(): lax.ppermute(array, 'seq', [(i, i ^ flip) for i in range(DOCS * DOC_SHARD...]
  transfers between devices with their start and end apart: 27 -> 27, of which waited for: 8 -> 9; matrix products, arithmetic and copies ran while one was open for 4% -> 4% of each run, Pallas kernels for 30% -> 34%
where the time goes in v5:
time: 137 us; the launch traced here: 136 us
  Pallas kernels  54.7 us (40%)
  starting transfers between devices  43.3 us (32%)
  waiting for transfers between devices  26.1 us (19%)
  other arithmetic  8.13 us (6%)
  local copies, waits for them, and re-layouts  3.81 us (3%)
    pallas_call x3, Pallas kernels, project(): pl.pallas_call(functools.partial(project_kernel, chunks, groups, not carr...  23.9 us
    ppermute x12, starting transfers between devices, across_mp(): return lax.ppermute(array, 'mp', [(i, i ^ flip) for i in range(MP)])  23.5 us
    pallas_call x1, Pallas kernels, attention(): pl.pallas_call(attention_kernel, grid_spec=pltpu.PrefetchScalarGridSpec(n...  9.26 us
    ppermute x12, waiting for transfers between devices, across_mp(): return lax.ppermute(array, 'mp', [(i, i ^ flip) for i in range(MP)])  8.9 us
    ppermute x2, waiting for transfers between devices, within_doc(): return lax.ppermute(array, 'seq', pairs)  8.7 us
    pallas_call x1, Pallas kernels, output(): pl.pallas_call(output_kernel, grid_spec=pltpu.PrefetchScalarGridSpec(num_...  8.4 us
    ppermute x6, starting transfers between devices, along_x(): return lax.ppermute(array, 'seq', pairs)  7.68 us
    pallas_call x1, Pallas kernels, turned_weights(): pl.pallas_call(turn_kernel, grid_spec=pltpu.PrefetchScalarGridSpec(num_sc...  6 us
  transfers between devices with their start and end apart: 27, of which 9 were waited for; matrix products, arithmetic and copies ran while one was open for 4% of the time, Pallas kernels for 34%

profile of v5, /device:TPU:1, one launch (start us, length us, event | category | flops | bytes accessed | tf_op | source)
XLA Modules:
  0.0 136.2 jit_solution(12914849544500373390)
XLA Ops:
  0.0 1.4 %collective-permute-start.1 = (bf16[1344,512]{1,0:T(8,128)(2,1)}, bf16[1344,512]{1,0:T(8,128)(2,1)}, u32[]{:S(2)}, u32[]{:S(2)}) collective-permute-start(bf16[1344,512]{1,0:T(8,128)(2,1)} %bitcast.23), channel_id=1, source_target_pairs={{0,1},{1,0},{2,3},{3,2},{4,5},{5,4},{6,7},{7,6},{8,9},{9,8},{10,11... | collective-permute-start | bytes 4128776 | tf_op jit(solution)/shard_map/ppermute | solution.py:42
  1.4 3.0 %collective-permute-start = (bf16[1344,512]{1,0:T(8,128)(2,1)}, bf16[1344,512]{1,0:T(8,128)(2,1)}, u32[]{:S(2)}, u32[]{:S(2)}) collective-permute-start(bf16[1344,512]{1,0:T(8,128)(2,1)} %bitcast.24), channel_id=1, source_target_pairs={{0,2},{1,3},{2,0},{3,1},{4,6},{5,7},{6,4},{7,5},{8,10},{9,11},{10,... | collective-permute-start | bytes 4128776 | tf_op jit(solution)/shard_map/ppermute | solution.py:42
  4.4 0.7 stack.75.where.order
  5.1 0.0 collective-permute-done.1.gate.refs_1_
  5.1 4.1 %shard_map.109 = (f32[512,128]{1,0:T(8,128)}, bf16[128,512]{1,0:T(8,128)(2,1)}, bf16[128,512]{1,0:T(8,128)(2,1)}, bf16[128,512]{1,0:T(8,128)(2,1)}, bf16[128,512]{1,0:T(8,128)(2,1)}) custom-call(s32[9]{0:T(128)} %stack.75.where.order, s32[4]{0:T(128)} %ids.3, s32[8]{0:T(128)} %lengths.3, bf16[8,128,2,256]{3,2,1,0:T(2,128)(2,1)} %rows_ref.1, ...), custom_call_target="tpu_custom_call" | custom-call | flops 1 | bytes 1 | tf_op jit(solution)/shard_map/pallas_call | solution.py:381
  9.2 2.8 %collective-permute-start.5 = (bf16[128,512]{1,0:T(8,128)(2,1)}, bf16[128,512]{1,0:T(8,128)(2,1)S(1)}, u32[]{:S(2)}, u32[]{:S(2)}) collective-permute-start(bf16[128,512]{1,0:T(8,128)(2,1)} %get-tuple-element.35), channel_id=1, source_target_pairs={{0,64},{4,68},{8,72},{12,76},{16,80},{20,84},{24,88},{28,92},{32,9... | collective-permute-start | bytes 393224 | tf_op jit(solution)/shard_map/ppermute | solution.py:56
  12.0 0.9 collective-permute-start.6
  12.8 0.6 collective-permute-start.4
  13.4 1.4 %reshape.22.refs_2_ = f32[8,1,672]{2,1,0:T(1,128)} reshape(f32[5376]{0:T(1024)} %param.12) | data formatting | bytes 43008 | tf_op jit(solution)/shard_map/reshape | solution.py:487
  14.9 3.1 %shard_map.110 = (bf16[336,128]{1,0:T(8,128)(2,1)}, bf16[336,128]{1,0:T(8,128)(2,1)}) custom-call(s32[9]{0:T(128)} %stack.75.where.order, bf16[512,5376]{1,0:T(8,128)(2,1)} %w_ref.3, bf16[128,512]{1,0:T(8,128)(2,1)} %get-tuple-element.31.gate), custom_call_target="tpu_custom_call" | custom-call | flops 1 | bytes 1 | tf_op jit(solution)/shard_map/pallas_call | solution.py:316
  18.0 2.5 %collective-permute-start.2 = (bf16[336,128]{1,0:T(8,128)(2,1)}, bf16[336,128]{1,0:T(8,128)(2,1)S(1)}, u32[]{:S(2)}, u32[]{:S(2)}) collective-permute-start(bf16[336,128]{1,0:T(8,128)(2,1)} %get-tuple-element.32.refs_6_), channel_id=1, source_target_pairs={{0,2},{1,3},{2,0},{3,1},{4,6},{5,7},{6,4},{7,5},{8,10},{9,11},{10,... | collective-permute-start | bytes 258056 | tf_op jit(solution)/shard_map/ppermute | solution.py:42
  20.4 8.9 %shard_map.111 = (f32[512,512]{1,0:T(8,128)}, f32[512,512]{1,0:T(8,128)}, f32[512,128]{1,0:T(8,128)}) custom-call(s32[9]{0:T(128)} %stack.75.where.order, bf16[1344,512]{1,0:T(8,128)(2,1)} %bitcast.25, bf16[1344,512]{1,0:T(8,128)(2,1)} %collective-permute-done.1.gate.refs_1_, f32[8,1,672]{2,1,0:T(1,128)} %reshape.22.refs_2_, bf16[5376,512]{1,0:T(8,128)(2,1)} %refs_3_.5, ...), custom_call_target="tpu_custom_call" | custom-call | flops 1 | bytes 1 | tf_op jit(solution)/shard_map/pallas_call | solution.py:167
  29.4 0.0 collective-permute-done.5
  29.4 1.9 %collective-permute-start.3 = (bf16[336,128]{1,0:T(8,128)(2,1)S(1)}, bf16[336,128]{1,0:T(8,128)(2,1)S(1)}, u32[]{:S(2)}, u32[]{:S(2)}) collective-permute-start(bf16[336,128]{1,0:T(8,128)(2,1)S(1)} %copy-done.9), channel_id=1, source_target_pairs={{0,3},{1,2},{2,1},{3,0},{4,7},{5,6},{6,5},{7,4},{8,11},{9,10},{10,... | collective-permute-start | bytes 258056 | tf_op jit(solution)/shard_map/ppermute | solution.py:42
  31.3 0.0 collective-permute-done.6
  31.3 0.0 collective-permute-done.4
  31.4 3.8 %collective-permute-start.9 = (bf16[128,512]{1,0:T(8,128)(2,1)S(1)}, bf16[128,512]{1,0:T(8,128)(2,1)S(1)}, u32[]{:S(2)}, u32[]{:S(2)}) collective-permute-start(bf16[128,512]{1,0:T(8,128)(2,1)S(1)} %add_add_fusion), channel_id=1, source_target_pairs={{0,12},{4,8},{8,4},{12,0},{16,28},{20,24},{24,20},{28,16},{32,44},... | collective-permute-start | bytes 393224 | tf_op jit(solution)/shard_map/ppermute | solution.py:75
  35.2 0.0 collective-permute-start.8
  35.2 0.0 collective-permute-done.refs_0_
  35.2 1.6 %collective-permute-start.7 = (bf16[128,512]{1,0:T(8,128)(2,1)S(1)}, bf16[128,512]{1,0:T(8,128)(2,1)S(1)}, u32[]{:S(2)}, u32[]{:S(2)}) collective-permute-start(bf16[128,512]{1,0:T(8,128)(2,1)S(1)} %add_add_fusion), channel_id=1, source_target_pairs={{0,4},{4,0},{8,12},{12,8},{16,20},{20,16},{24,28},{28,24},{32,36},... | collective-permute-start | bytes 393224 | tf_op jit(solution)/shard_map/ppermute | solution.py:75
  36.8 1.7 %negate_select_fusion = (f32[512,128]{1,0:T(8,128)}, f32[512,128]{1,0:T(8,128)}) fusion(f32[512,128]{1,0:T(8,128)S(1)} %copy-done.1, f32[128]{0:T(128)S(1)} %fusion.4, pred[128]{0:T(512)(128)(4,1)S(1)} %iota_compare_fusion), kind=kLoop, calls=%fused_computation.4 | loop fusion | flops 196608 | bytes 787072 | tf_op jit(solution)/shard_map/jit(_where)/select_n | solution.py:450
  38.5 0.3 collective-permute-done.3
  38.8 0.0 collective-permute-done.2
  38.8 2.4 %collective-permute-done.9 = bf16[128,512]{1,0:T(8,128)(2,1)S(1)} collective-permute-done((bf16[128,512]{1,0:T(8,128)(2,1)S(1)}, bf16[128,512]{1,0:T(8,128)(2,1)S(1)}, u32[]{:S(2)}, u32[]{:S(2)}) %collective-permute-start.9) | collective-permute-done | bytes 131104 | tf_op jit(solution)/shard_map/ppermute | solution.py:75
  41.2 0.7 collective-permute-done.8
  41.9 0.7 collective-permute-done.7
  42.7 0.5 collective-permute-start.10
  43.2 2.6 %collective-permute-start.16 = (bf16[2,336,128]{2,1,0:T(8,128)(2,1)S(1)}, bf16[2,336,128]{2,1,0:T(8,128)(2,1)S(1)}, u32[]{:S(2)}, u32[]{:S(2)}) collective-permute-start(bf16[2,336,128]{2,1,0:T(8,128)(2,1)S(1)} %pad_maximum_fusion.2), channel_id=1, source_target_pairs={{0,12},{4,0},{8,4},{12,8},{16,28},{20,16},{24,20},{28,24},{32,44},... | collective-permute-start | bytes 516104 | tf_op jit(solution)/shard_map/ppermute | solution.py:66
  45.8 0.1 collective-permute-start.15
  45.9 0.7 collective-permute-start.14
  46.5 0.1 pad_maximum_fusion.1.refs_0_
  46.6 0.9 collective-permute-start.13
  47.5 7.4 %shard_map.112.refs_4_.own = bf16[512,512]{1,0:T(8,128)(2,1)} custom-call(s32[9]{0:T(128)} %stack.75.where.order, bf16[1344,512]{1,0:T(8,128)(2,1)} %collective-permute-done.refs_0_, bf16[1344,512]{1,0:T(8,128)(2,1)} %collective-permute-done.10.refs_1_, f32[8,1,672]{2,1,0:T(1,128)} %reshape.22.refs_2_, bf16[5376,256]{1,0:T(8,128)(2,1)} %refs_3_.4, ...), custom_call_target="tpu_custom_call" | custom-call | flops 3000000000 | bytes 10000000 | tf_op jit(solution)/shard_map/pallas_call | solution.py:167
  54.9 2.3 %collective-permute-start.12 = (bf16[512,512]{1,0:T(8,128)(2,1)}, bf16[512,512]{1,0:T(8,128)(2,1)}, u32[]{:S(2)}, u32[]{:S(2)}) collective-permute-start(bf16[512,512]{1,0:T(8,128)(2,1)} %shard_map.112.refs_4_.own), channel_id=1, source_target_pairs={{0,8},{4,12},{8,16},{12,20},{16,24},{20,28},{24,0},{28,4},{32,40},... | collective-permute-start | bytes 1572872 | tf_op jit(solution)/shard_map/ppermute | solution.py:84
  57.2 0.0 collective-permute-done.16
  57.2 0.3 collective-permute-start.11
  57.5 7.5 %shard_map.113.q_ref = bf16[512,512]{1,0:T(8,128)(2,1)} custom-call(s32[9]{0:T(128)} %stack.75.where.order, bf16[1344,512]{1,0:T(8,128)(2,1)} %collective-permute-done.refs_0_, bf16[1344,512]{1,0:T(8,128)(2,1)} %collective-permute-done.10.refs_1_, f32[8,1,672]{2,1,0:T(1,128)} %reshape.22.refs_2_, bf16[5376,512]{1,0:T(8,128)(2,1)} %refs_3_.5, ...), custom_call_target="tpu_custom_call" | custom-call | flops 3000000000 | bytes 10000000 | tf_op jit(solution)/shard_map/pallas_call | solution.py:167
  65.0 1.9 %pad_maximum_fusion.gate.p0 = bf16[4,2,336,128]{3,2,1,0:T(8,128)(2,1)} fusion(bf16[1,2,336,128]{3,2,1,0:T(8,128)(2,1)S(1)} %bitcast.28, bf16[1,2,336,128]{3,2,1,0:T(8,128)(2,1)} %bitcast.17, bf16[1,2,336,128]{3,2,1,0:T(8,128)(2,1)} %bitcast.16, bf16[1,2,336,128]{3,2,1,0:T(8,128)(2,1)S(1)} %bitcast.26), kind=kLoop, calls=%fused_computation.2 | loop fusion | flops 1032192 | bytes 1376256 | tf_op jit(solution)/shard_map/stack | solution.py:514
  66.9 1.0 collective-permute-start.21
  67.9 6.0 %shard_map.114 = (bf16[1344,512]{1,0:T(8,128)(2,1)}, bf16[1344,512]{1,0:T(8,128)(2,1)}) custom-call(s32[9]{0:T(128)} %stack.75.where.order, bf16[512,5376]{1,0:T(8,128)(2,1)} %w_ref.3, bf16[4,2,336,128]{3,2,1,0:T(8,128)(2,1)} %pad_maximum_fusion.gate.p0), custom_call_target="tpu_custom_call" | custom-call | flops 1 | bytes 1 | tf_op jit(solution)/shard_map/pallas_call | solution.py:343
  73.9 1.7 %collective-permute-start.20 = (bf16[1344,512]{1,0:T(8,128)(2,1)}, bf16[1344,512]{1,0:T(8,128)(2,1)}, u32[]{:S(2)}, u32[]{:S(2)}) collective-permute-start(bf16[1344,512]{1,0:T(8,128)(2,1)} %get-tuple-element.53.refs_2_), channel_id=1, source_target_pairs={{0,1},{1,0},{2,3},{3,2},{4,5},{5,4},{6,7},{7,6},{8,9},{9,8},{10,11... | collective-permute-start | bytes 4128776 | tf_op jit(solution)/shard_map/ppermute | solution.py:42
  75.6 0.0 collective-permute-done.13.refs_1_
  75.6 0.0 collective-permute-done.12.two_back
  75.7 8.7 %collective-permute-done.11.one_back = bf16[512,512]{1,0:T(8,128)(2,1)} collective-permute-done((bf16[512,512]{1,0:T(8,128)(2,1)}, bf16[512,512]{1,0:T(8,128)(2,1)}, u32[]{:S(2)}, u32[]{:S(2)}) %collective-permute-start.11) | collective-permute-done | bytes 524320 | tf_op jit(solution)/shard_map/ppermute | solution.py:84
  84.4 9.3 %shard_map.115.c0 = bf16[512,512]{1,0:T(8,128)(2,1)} custom-call(s32[9]{0:T(128)} %stack.75.where.order, s32[4]{0:T(128)} %ids.3, s32[8]{0:T(128)} %lengths.3, s32[4]{0:T(128)} %reals.1, bf16[512,512]{1,0:T(8,128)(2,1)} %shard_map.113.q_ref, bf16[512,512]{1,0:T(8,128)(2,1)} %shard_map.112.refs_4_.own, bf16[512,512]{1,0:T(8,128)(2,1)} %collective-permute-done.11.one_back, ...), custom_call_target="tpu_custom_call" | custom-call | flops 1 | bytes 1 | tf_op jit(solution)/shard_map/pallas_call | solution.py:283
  93.6 2.1 %collective-permute-start.18 = (bf16[512,512]{1,0:T(8,128)(2,1)}, bf16[512,512]{1,0:T(8,128)(2,1)S(1)}, u32[]{:S(2)}, u32[]{:S(2)}) collective-permute-start(bf16[512,512]{1,0:T(8,128)(2,1)} %shard_map.115.c0), channel_id=1, source_target_pairs={{0,2},{1,3},{2,0},{3,1},{4,6},{5,7},{6,4},{7,5},{8,10},{9,11},{10,... | collective-permute-start | bytes 1572872 | tf_op jit(solution)/shard_map/ppermute | solution.py:42
  95.7 2.5 %collective-permute-start.23 = (bf16[4,2,336,128]{3,2,1,0:T(8,128)(2,1)}, bf16[4,2,336,128]{3,2,1,0:T(8,128)(2,1)S(1)}, u32[]{:S(2)}, u32[]{:S(2)}) collective-permute-start(bf16[4,2,336,128]{3,2,1,0:T(8,128)(2,1)} %pad_maximum_fusion.gate.p0), channel_id=1, source_target_pairs={{0,96},{4,100},{8,104},{12,108},{16,112},{20,116},{24,120},{28,124... | collective-permute-start | bytes 2064392 | tf_op jit(solution)/shard_map/ppermute | solution.py:56
  98.2 2.1 %collective-permute-start.17 = (bf16[512,512]{1,0:T(8,128)(2,1)}, bf16[512,512]{1,0:T(8,128)(2,1)S(1)}, u32[]{:S(2)}, u32[]{:S(2)}) collective-permute-start(bf16[512,512]{1,0:T(8,128)(2,1)} %shard_map.115.c0), channel_id=1, source_target_pairs={{0,1},{1,0},{2,3},{3,2},{4,5},{5,4},{6,7},{7,6},{8,9},{9,8},{10,11... | collective-permute-start | bytes 1572872 | tf_op jit(solution)/shard_map/ppermute | solution.py:42
  100.3 7.2 %collective-permute-done.18.c2 = bf16[512,512]{1,0:T(8,128)(2,1)S(1)} collective-permute-done((bf16[512,512]{1,0:T(8,128)(2,1)}, bf16[512,512]{1,0:T(8,128)(2,1)S(1)}, u32[]{:S(2)}, u32[]{:S(2)}) %collective-permute-start.18) | collective-permute-done | bytes 524320 | tf_op jit(solution)/shard_map/ppermute | solution.py:42
  107.5 2.3 %collective-permute-start.19 = (bf16[512,512]{1,0:T(8,128)(2,1)S(1)}, bf16[512,512]{1,0:T(8,128)(2,1)S(1)}, u32[]{:S(2)}, u32[]{:S(2)}) collective-permute-start(bf16[512,512]{1,0:T(8,128)(2,1)S(1)} %collective-permute-done.18.c2), channel_id=1, source_target_pairs={{0,1},{1,0},{2,3},{3,2},{4,5},{5,4},{6,7},{7,6},{8,9},{9,8},{10,11... | collective-permute-start | bytes 1572872 | tf_op jit(solution)/shard_map/ppermute | solution.py:42
  109.8 1.6 %collective-permute-done.23.p3 = bf16[4,2,336,128]{3,2,1,0:T(8,128)(2,1)S(1)} collective-permute-done((bf16[4,2,336,128]{3,2,1,0:T(8,128)(2,1)}, bf16[4,2,336,128]{3,2,1,0:T(8,128)(2,1)S(1)}, u32[]{:S(2)}, u32[]{:S(2)}) %collective-permute-start.23) | collective-permute-done | bytes 688160 | tf_op jit(solution)/shard_map/ppermute | solution.py:56
  111.3 0.0 collective-permute-done.17.c1
  111.3 3.0 %collective-permute-done.22.p2 = bf16[4,2,336,128]{3,2,1,0:T(8,128)(2,1)S(1)} collective-permute-done((bf16[4,2,336,128]{3,2,1,0:T(8,128)(2,1)}, bf16[4,2,336,128]{3,2,1,0:T(8,128)(2,1)S(1)}, u32[]{:S(2)}, u32[]{:S(2)}) %collective-permute-start.22) | collective-permute-done | bytes 688160 | tf_op jit(solution)/shard_map/ppermute | solution.py:56
  114.4 0.8 copy-done.5
  115.2 0.8 copy-done.8
  116.1 8.4 %shard_map.116 = (f32[1344,512]{1,0:T(8,128)}, f32[1,512]{1,0:T(1,128)}) custom-call(s32[9]{0:T(128)} %stack.75.where.order, bf16[512,512]{1,0:T(8,128)(2,1)} %shard_map.115.c0, bf16[512,512]{1,0:T(8,128)(2,1)} %copy-done.7, bf16[512,512]{1,0:T(8,128)(2,1)} %copy-done.6, bf16[512,512]{1,0:T(8,128)(2,1)} %copy-done.8, ...), custom_call_target="tpu_custom_call" | custom-call | flops 2818572288 | bytes 8000000 | tf_op jit(solution)/shard_map/pallas_call | solution.py:428
  124.5 3.4 %collective-permute-start.26 = (f32[1,512]{1,0:T(1,128)}, f32[1,512]{1,0:T(1,128)S(1)}, u32[]{:S(2)}, u32[]{:S(2)}) collective-permute-start(f32[1,512]{1,0:T(1,128)} %get-tuple-element.56), channel_id=1, source_target_pairs={{0,3},{1,2},{2,1},{3,0},{4,7},{5,6},{6,5},{7,4},{8,11},{9,10},{10,... | collective-permute-start | bytes 6152 | tf_op jit(solution)/shard_map/ppermute | solution.py:42
  127.8 2.6 %collective-permute-start.25 = (f32[1,512]{1,0:T(1,128)}, f32[1,512]{1,0:T(1,128)S(1)}, u32[]{:S(2)}, u32[]{:S(2)}) collective-permute-start(f32[1,512]{1,0:T(1,128)} %get-tuple-element.56), channel_id=1, source_target_pairs={{0,2},{1,3},{2,0},{3,1},{4,6},{5,7},{6,4},{7,5},{8,10},{9,11},{10,... | collective-permute-start | bytes 6152 | tf_op jit(solution)/shard_map/ppermute | solution.py:42
  130.4 0.0 collective-permute-start.24
  130.4 0.0 collective-permute-done.26
  130.4 1.4 %collective-permute-done.25 = f32[1,512]{1,0:T(1,128)S(1)} collective-permute-done((f32[1,512]{1,0:T(1,128)}, f32[1,512]{1,0:T(1,128)S(1)}, u32[]{:S(2)}, u32[]{:S(2)}) %collective-permute-start.25) | collective-permute-done | bytes 2080 | tf_op jit(solution)/shard_map/ppermute | solution.py:42
  131.8 0.0 collective-permute-done.24
  131.8 0.6 add_rsqrt_fusion
  132.5 3.7 %fusion = bf16[512,1344]{0,1:T(8,128)(2,1)} fusion(f32[1344,512]{1,0:T(8,128)} %get-tuple-element.55, f32[512]{0:T(512)S(1)} %bitcast.34, f32[1344]{0:T(1024)S(1)} %copy-done.3, bf16[512,1344]{0,1:T(8,128)(2,1)} %param.11), kind=kLoop, calls=%fused_computation.1 | loop fusion | flops 3440640 | bytes 5512448 | tf_op jit(solution)/shard_map/transpose | solution.py:531
  (29 shorter events, 0.1 us)
Async XLA Ops:
  0.0 5.1 %collective-permute-start.1 = (bf16[1344,512]{1,0:T(8,128)(2,1)}, bf16[1344,512]{1,0:T(8,128)(2,1)}, u32[]{:S(2)}, u32[]{:S(2)}) collective-permute-start(bf16[1344,512]{1,0:T(8,128)(2,1)} %bitcast.23), channel_id=1, source_target_pairs={{0,1},{1,0},{2,3},{3,2},{4,5},{5,4},{6,7},{7,6},{8,9},{9,8},{10,11... | collective-permute-start | bytes 4128776 | tf_op jit(solution)/shard_map/ppermute | solution.py:42
  1.4 33.8 %collective-permute-start = (bf16[1344,512]{1,0:T(8,128)(2,1)}, bf16[1344,512]{1,0:T(8,128)(2,1)}, u32[]{:S(2)}, u32[]{:S(2)}) collective-permute-start(bf16[1344,512]{1,0:T(8,128)(2,1)} %bitcast.24), channel_id=1, source_target_pairs={{0,2},{1,3},{2,0},{3,1},{4,6},{5,7},{6,4},{7,5},{8,10},{9,11},{10,... | collective-permute-start | bytes 4128776 | tf_op jit(solution)/shard_map/ppermute | solution.py:42
  9.2 20.2 %collective-permute-start.5 = (bf16[128,512]{1,0:T(8,128)(2,1)}, bf16[128,512]{1,0:T(8,128)(2,1)S(1)}, u32[]{:S(2)}, u32[]{:S(2)}) collective-permute-start(bf16[128,512]{1,0:T(8,128)(2,1)} %get-tuple-element.35), channel_id=1, source_target_pairs={{0,64},{4,68},{8,72},{12,76},{16,80},{20,84},{24,88},{28,92},{32,9... | collective-permute-start | bytes 393224 | tf_op jit(solution)/shard_map/ppermute | solution.py:56
  12.0 19.4 %collective-permute-start.6 = (bf16[128,512]{1,0:T(8,128)(2,1)}, bf16[128,512]{1,0:T(8,128)(2,1)S(1)}, u32[]{:S(2)}, u32[]{:S(2)}) collective-permute-start(bf16[128,512]{1,0:T(8,128)(2,1)} %get-tuple-element.36), channel_id=1, source_target_pairs={{0,96},{4,100},{8,104},{12,108},{16,112},{20,116},{24,120},{28,124... | collective-permute-start | bytes 393224 | tf_op jit(solution)/shard_map/ppermute | solution.py:56
  12.8 18.5 %collective-permute-start.4 = (bf16[128,512]{1,0:T(8,128)(2,1)}, bf16[128,512]{1,0:T(8,128)(2,1)S(1)}, u32[]{:S(2)}, u32[]{:S(2)}) collective-permute-start(bf16[128,512]{1,0:T(8,128)(2,1)} %get-tuple-element.31.gate), channel_id=1, source_target_pairs={{0,32},{4,36},{8,40},{12,44},{16,48},{20,52},{24,56},{28,60},{32,6... | collective-permute-start | bytes 393224 | tf_op jit(solution)/shard_map/ppermute | solution.py:56
  18.0 11.4 %copy-start.9 = (bf16[336,128]{1,0:T(8,128)(2,1)S(1)}, bf16[336,128]{1,0:T(8,128)(2,1)}, u32[]{:S(2)}) copy-start(bf16[336,128]{1,0:T(8,128)(2,1)} %get-tuple-element.33) | copy-start | bytes 258052
  18.0 13.4 %copy-start.2 = (bf16[128,512]{1,0:T(8,128)(2,1)S(1)}, bf16[128,512]{1,0:T(8,128)(2,1)}, u32[]{:S(2)}) copy-start(bf16[128,512]{1,0:T(8,128)(2,1)} %get-tuple-element.34) | copy-start | bytes 393220
  18.0 18.8 %copy-start.1 = (f32[512,128]{1,0:T(8,128)S(1)}, f32[512,128]{1,0:T(8,128)}, u32[]{:S(2)}) copy-start(f32[512,128]{1,0:T(8,128)} %get-tuple-element.41) | copy-start | bytes 786436
  18.0 20.8 %collective-permute-start.2 = (bf16[336,128]{1,0:T(8,128)(2,1)}, bf16[336,128]{1,0:T(8,128)(2,1)S(1)}, u32[]{:S(2)}, u32[]{:S(2)}) collective-permute-start(bf16[336,128]{1,0:T(8,128)(2,1)} %get-tuple-element.32.refs_6_), channel_id=1, source_target_pairs={{0,2},{1,3},{2,0},{3,1},{4,6},{5,7},{6,4},{7,5},{8,10},{9,11},{10,... | collective-permute-start | bytes 258056 | tf_op jit(solution)/shard_map/ppermute | solution.py:42
  29.4 9.4 %collective-permute-start.3 = (bf16[336,128]{1,0:T(8,128)(2,1)S(1)}, bf16[336,128]{1,0:T(8,128)(2,1)S(1)}, u32[]{:S(2)}, u32[]{:S(2)}) collective-permute-start(bf16[336,128]{1,0:T(8,128)(2,1)S(1)} %copy-done.9), channel_id=1, source_target_pairs={{0,3},{1,2},{2,1},{3,0},{4,7},{5,6},{6,5},{7,4},{8,11},{9,10},{10,... | collective-permute-start | bytes 258056 | tf_op jit(solution)/shard_map/ppermute | solution.py:42
  31.4 9.8 %collective-permute-start.9 = (bf16[128,512]{1,0:T(8,128)(2,1)S(1)}, bf16[128,512]{1,0:T(8,128)(2,1)S(1)}, u32[]{:S(2)}, u32[]{:S(2)}) collective-permute-start(bf16[128,512]{1,0:T(8,128)(2,1)S(1)} %add_add_fusion), channel_id=1, source_target_pairs={{0,12},{4,8},{8,4},{12,0},{16,28},{20,24},{24,20},{28,16},{32,44},... | collective-permute-start | bytes 393224 | tf_op jit(solution)/shard_map/ppermute | solution.py:75
  35.2 6.7 %collective-permute-start.8 = (bf16[128,512]{1,0:T(8,128)(2,1)S(1)}, bf16[128,512]{1,0:T(8,128)(2,1)S(1)}, u32[]{:S(2)}, u32[]{:S(2)}) collective-permute-start(bf16[128,512]{1,0:T(8,128)(2,1)S(1)} %add_add_fusion), channel_id=1, source_target_pairs={{0,8},{4,12},{8,0},{12,4},{16,24},{20,28},{24,16},{28,20},{32,40},... | collective-permute-start | bytes 393224 | tf_op jit(solution)/shard_map/ppermute | solution.py:75
  35.2 7.4 %collective-permute-start.7 = (bf16[128,512]{1,0:T(8,128)(2,1)S(1)}, bf16[128,512]{1,0:T(8,128)(2,1)S(1)}, u32[]{:S(2)}, u32[]{:S(2)}) collective-permute-start(bf16[128,512]{1,0:T(8,128)(2,1)S(1)} %add_add_fusion), channel_id=1, source_target_pairs={{0,4},{4,0},{8,12},{12,8},{16,20},{20,16},{24,28},{28,24},{32,36},... | collective-permute-start | bytes 393224 | tf_op jit(solution)/shard_map/ppermute | solution.py:75
  42.7 4.8 %collective-permute-start.10 = (bf16[1344,512]{1,0:T(8,128)(2,1)}, bf16[1344,512]{1,0:T(8,128)(2,1)}, u32[]{:S(2)}, u32[]{:S(2)}) collective-permute-start(bf16[1344,512]{1,0:T(8,128)(2,1)} %collective-permute-done.refs_0_), channel_id=1, source_target_pairs={{0,1},{1,0},{2,3},{3,2},{4,5},{5,4},{6,7},{7,6},{8,9},{9,8},{10,11... | collective-permute-start | bytes 4128776 | tf_op jit(solution)/shard_map/ppermute | solution.py:42
  43.2 14.0 %collective-permute-start.16 = (bf16[2,336,128]{2,1,0:T(8,128)(2,1)S(1)}, bf16[2,336,128]{2,1,0:T(8,128)(2,1)S(1)}, u32[]{:S(2)}, u32[]{:S(2)}) collective-permute-start(bf16[2,336,128]{2,1,0:T(8,128)(2,1)S(1)} %pad_maximum_fusion.2), channel_id=1, source_target_pairs={{0,12},{4,0},{8,4},{12,8},{16,28},{20,16},{24,20},{28,24},{32,44},... | collective-permute-start | bytes 516104 | tf_op jit(solution)/shard_map/ppermute | solution.py:66
  45.8 19.2 %collective-permute-start.15 = (bf16[2,336,128]{2,1,0:T(8,128)(2,1)S(1)}, bf16[2,336,128]{2,1,0:T(8,128)(2,1)}, u32[]{:S(2)}, u32[]{:S(2)}) collective-permute-start(bf16[2,336,128]{2,1,0:T(8,128)(2,1)S(1)} %pad_maximum_fusion.2), channel_id=1, source_target_pairs={{0,8},{4,12},{8,0},{12,4},{16,24},{20,28},{24,16},{28,20},{32,40},... | collective-permute-start | bytes 516104 | tf_op jit(solution)/shard_map/ppermute | solution.py:66
  45.9 19.1 %collective-permute-start.14 = (bf16[2,336,128]{2,1,0:T(8,128)(2,1)S(1)}, bf16[2,336,128]{2,1,0:T(8,128)(2,1)}, u32[]{:S(2)}, u32[]{:S(2)}) collective-permute-start(bf16[2,336,128]{2,1,0:T(8,128)(2,1)S(1)} %pad_maximum_fusion.2), channel_id=1, source_target_pairs={{0,4},{4,8},{8,12},{12,0},{16,20},{20,24},{24,28},{28,16},{32,36},... | collective-permute-start | bytes 516104 | tf_op jit(solution)/shard_map/ppermute | solution.py:66
  46.6 8.3 %copy-start = (bf16[4,128,512]{2,1,0:T(8,128)(2,1)}, bf16[4,128,512]{2,1,0:T(8,128)(2,1)S(1)}, u32[]{:S(2)}) copy-start(bf16[4,128,512]{2,1,0:T(8,128)(2,1)S(1)} %pad_maximum_fusion.1.refs_0_) | copy-start | bytes 1572868
  46.6 29.0 %collective-permute-start.13 = (bf16[4,128,512]{2,1,0:T(8,128)(2,1)S(1)}, bf16[4,128,512]{2,1,0:T(8,128)(2,1)}, u32[]{:S(2)}, u32[]{:S(2)}) collective-permute-start(bf16[4,128,512]{2,1,0:T(8,128)(2,1)S(1)} %pad_maximum_fusion.1.refs_0_), channel_id=1, source_target_pairs={{0,16},{4,20},{8,24},{12,28},{16,0},{20,4},{24,8},{28,12},{32,48},... | collective-permute-start | bytes 1572872 | tf_op jit(solution)/shard_map/ppermute | solution.py:71
  54.9 20.7 %collective-permute-start.12 = (bf16[512,512]{1,0:T(8,128)(2,1)}, bf16[512,512]{1,0:T(8,128)(2,1)}, u32[]{:S(2)}, u32[]{:S(2)}) collective-permute-start(bf16[512,512]{1,0:T(8,128)(2,1)} %shard_map.112.refs_4_.own), channel_id=1, source_target_pairs={{0,8},{4,12},{8,16},{12,20},{16,24},{20,28},{24,0},{28,4},{32,40},... | collective-permute-start | bytes 1572872 | tf_op jit(solution)/shard_map/ppermute | solution.py:84
  57.2 27.2 %collective-permute-start.11 = (bf16[512,512]{1,0:T(8,128)(2,1)}, bf16[512,512]{1,0:T(8,128)(2,1)}, u32[]{:S(2)}, u32[]{:S(2)}) collective-permute-start(bf16[512,512]{1,0:T(8,128)(2,1)} %shard_map.112.refs_4_.own), channel_id=1, source_target_pairs={{0,4},{4,8},{8,12},{12,16},{16,20},{20,24},{24,28},{28,0},{32,36},... | collective-permute-start | bytes 1572872 | tf_op jit(solution)/shard_map/ppermute | solution.py:84
  66.9 31.2 %collective-permute-start.21 = (bf16[4,2,336,128]{3,2,1,0:T(8,128)(2,1)}, bf16[4,2,336,128]{3,2,1,0:T(8,128)(2,1)}, u32[]{:S(2)}, u32[]{:S(2)}) collective-permute-start(bf16[4,2,336,128]{3,2,1,0:T(8,128)(2,1)} %pad_maximum_fusion.gate.p0), channel_id=1, source_target_pairs={{0,32},{4,36},{8,40},{12,44},{16,48},{20,52},{24,56},{28,60},{32,6... | collective-permute-start | bytes 2064392 | tf_op jit(solution)/shard_map/ppermute | solution.py:56
  73.9 40.4 %collective-permute-start.20 = (bf16[1344,512]{1,0:T(8,128)(2,1)}, bf16[1344,512]{1,0:T(8,128)(2,1)}, u32[]{:S(2)}, u32[]{:S(2)}) collective-permute-start(bf16[1344,512]{1,0:T(8,128)(2,1)} %get-tuple-element.53.refs_2_), channel_id=1, source_target_pairs={{0,1},{1,0},{2,3},{3,2},{4,5},{5,4},{6,7},{7,6},{8,9},{9,8},{10,11... | collective-permute-start | bytes 4128776 | tf_op jit(solution)/shard_map/ppermute | solution.py:42
  93.6 13.9 %collective-permute-start.18 = (bf16[512,512]{1,0:T(8,128)(2,1)}, bf16[512,512]{1,0:T(8,128)(2,1)S(1)}, u32[]{:S(2)}, u32[]{:S(2)}) collective-permute-start(bf16[512,512]{1,0:T(8,128)(2,1)} %shard_map.115.c0), channel_id=1, source_target_pairs={{0,2},{1,3},{2,0},{3,1},{4,6},{5,7},{6,4},{7,5},{8,10},{9,11},{10,... | collective-permute-start | bytes 1572872 | tf_op jit(solution)/shard_map/ppermute | solution.py:42
  95.7 15.6 %collective-permute-start.23 = (bf16[4,2,336,128]{3,2,1,0:T(8,128)(2,1)}, bf16[4,2,336,128]{3,2,1,0:T(8,128)(2,1)S(1)}, u32[]{:S(2)}, u32[]{:S(2)}) collective-permute-start(bf16[4,2,336,128]{3,2,1,0:T(8,128)(2,1)} %pad_maximum_fusion.gate.p0), channel_id=1, source_target_pairs={{0,96},{4,100},{8,104},{12,108},{16,112},{20,116},{24,120},{28,124... | collective-permute-start | bytes 2064392 | tf_op jit(solution)/shard_map/ppermute | solution.py:56
  98.2 16.2 %collective-permute-start.22 = (bf16[4,2,336,128]{3,2,1,0:T(8,128)(2,1)}, bf16[4,2,336,128]{3,2,1,0:T(8,128)(2,1)S(1)}, u32[]{:S(2)}, u32[]{:S(2)}) collective-permute-start(bf16[4,2,336,128]{3,2,1,0:T(8,128)(2,1)} %collective-permute-done.21.p1), channel_id=1, source_target_pairs={{0,32},{4,36},{8,40},{12,44},{16,48},{20,52},{24,56},{28,60},{32,6... | collective-permute-start | bytes 2064392 | tf_op jit(solution)/shard_map/ppermute | solution.py:56
  98.2 13.2 %collective-permute-start.17 = (bf16[512,512]{1,0:T(8,128)(2,1)}, bf16[512,512]{1,0:T(8,128)(2,1)S(1)}, u32[]{:S(2)}, u32[]{:S(2)}) collective-permute-start(bf16[512,512]{1,0:T(8,128)(2,1)} %shard_map.115.c0), channel_id=1, source_target_pairs={{0,1},{1,0},{2,3},{3,2},{4,5},{5,4},{6,7},{7,6},{8,9},{9,8},{10,11... | collective-permute-start | bytes 1572872 | tf_op jit(solution)/shard_map/ppermute | solution.py:42
  107.5 6.9 %copy-start.6 = (bf16[512,512]{1,0:T(8,128)(2,1)}, bf16[512,512]{1,0:T(8,128)(2,1)S(1)}, u32[]{:S(2)}) copy-start(bf16[512,512]{1,0:T(8,128)(2,1)S(1)} %collective-permute-done.18.c2) | copy-start | bytes 1572868
  107.5 6.9 %collective-permute-start.19 = (bf16[512,512]{1,0:T(8,128)(2,1)S(1)}, bf16[512,512]{1,0:T(8,128)(2,1)S(1)}, u32[]{:S(2)}, u32[]{:S(2)}) collective-permute-start(bf16[512,512]{1,0:T(8,128)(2,1)S(1)} %collective-permute-done.18.c2), channel_id=1, source_target_pairs={{0,1},{1,0},{2,3},{3,2},{4,5},{5,4},{6,7},{7,6},{8,9},{9,8},{10,11... | collective-permute-start | bytes 1572872 | tf_op jit(solution)/shard_map/ppermute | solution.py:42
  111.3 4.7 %copy-start.4 = (bf16[4,2,336,128]{3,2,1,0:T(8,128)(2,1)}, bf16[4,2,336,128]{3,2,1,0:T(8,128)(2,1)S(1)}, u32[]{:S(2)}) copy-start(bf16[4,2,336,128]{3,2,1,0:T(8,128)(2,1)S(1)} %collective-permute-done.23.p3) | copy-start | bytes 2064388
  111.3 3.0 %copy-start.7 = (bf16[512,512]{1,0:T(8,128)(2,1)}, bf16[512,512]{1,0:T(8,128)(2,1)S(1)}, u32[]{:S(2)}) copy-start(bf16[512,512]{1,0:T(8,128)(2,1)S(1)} %collective-permute-done.17.c1) | copy-start | bytes 1572868
  114.4 0.9 copy-start.5
  115.2 0.8 copy-start.8
  116.1 16.4 %copy-start.3 = (f32[1344]{0:T(1024)S(1)}, f32[1344]{0:T(1024)}, u32[]{:S(2)}) copy-start(f32[1344]{0:T(1024)} %param.17) | copy-start | bytes 16132
  124.5 6.0 %collective-permute-start.26 = (f32[1,512]{1,0:T(1,128)}, f32[1,512]{1,0:T(1,128)S(1)}, u32[]{:S(2)}, u32[]{:S(2)}) collective-permute-start(f32[1,512]{1,0:T(1,128)} %get-tuple-element.56), channel_id=1, source_target_pairs={{0,3},{1,2},{2,1},{3,0},{4,7},{5,6},{6,5},{7,4},{8,11},{9,10},{10,... | collective-permute-start | bytes 6152 | tf_op jit(solution)/shard_map/ppermute | solution.py:42
  127.8 4.0 %collective-permute-start.25 = (f32[1,512]{1,0:T(1,128)}, f32[1,512]{1,0:T(1,128)S(1)}, u32[]{:S(2)}, u32[]{:S(2)}) collective-permute-start(f32[1,512]{1,0:T(1,128)} %get-tuple-element.56), channel_id=1, source_target_pairs={{0,2},{1,3},{2,0},{3,1},{4,6},{5,7},{6,4},{7,5},{8,10},{9,11},{10,... | collective-permute-start | bytes 6152 | tf_op jit(solution)/shard_map/ppermute | solution.py:42
  130.4 1.4 %collective-permute-start.24 = (f32[1,512]{1,0:T(1,128)}, f32[1,512]{1,0:T(1,128)S(1)}, u32[]{:S(2)}, u32[]{:S(2)}) collective-permute-start(f32[1,512]{1,0:T(1,128)} %get-tuple-element.56), channel_id=1, source_target_pairs={{0,1},{1,0},{2,3},{3,2},{4,5},{5,4},{6,7},{7,6},{8,9},{9,8},{10,11... | collective-permute-start | bytes 6152 | tf_op jit(solution)/shard_map/ppermute | solution.py:42
